TPU v7x, 32 devices: a whole 2x2x4 slice. The times are simulated.
32 devices in a mesh: row: 4 (over y, core), col: 8 (over z, x).
Axes of the slice: x: 2, y: 2, z: 4, core: 2. Of those that a mesh axis runs over, the one named last changes fastest.
Arguments:
- features: bfloat16 [4096, 128], P('col', 'row'), may hold values from -6 to 6
- weight: bfloat16 [128, 128], replicated, may hold values from -0.5 to 0.5
- bias_vector: float32 [128], replicated, may hold values from -3 to 3
- tile_rows: int32 [4, 8, 128], P('row', 'col'), may hold values from 0 to 7
- tile_cols: int32 [4, 8, 128], P('row', 'col'), may hold values from 0 to 3
- neighbours: int32 [4, 8, 128, 2, 128], P('row', 'col'), may hold values from 0 to 127, as said below
- edge_weights: bfloat16 [4, 8, 128, 2, 128], P('row', 'col'), may hold values from 0.039794922 to 0.3984375
- tile_count: int32 [4, 8], P('row', 'col'), may hold values from 16 to 128, as said below
- cotangent: float32 [4096, 128], P(('row', 'col')), may hold values from -6 to 6
Outputs:
- activations: float32 [4096, 128], P(('row', 'col'))
- grad_features: bfloat16 [4096, 128], P('col', 'row')
- grad_weight: float32 [128, 128], replicated
- grad_bias: float32 [128], replicated
Inputs may be any that keep to these rules, and one draw needn't show every extreme that they name: `tile_count`: one device uses all 128 tile slots in every draw. The 2 neighbours of one galaxy within one tile are distinct.
All inputs are finite; a program needn't handle non-finite values.
Results may differ from a plain program's by a relative error of at most 0.006.
Values may be sent and summed in bfloat16 or wider, within the bound.
No kernel may reach another device: no remote copies, remote signals or barrier semaphores. Data moves between devices by JAX's collectives and lax.ppermute only.
A program may use at most 64 MiB of HBM per device.

v0:
```python
import jax
import jax.numpy as jnp
from jax import lax
from jax.sharding import PartitionSpec as P

tile_group = 16


def dense_tiles(neighbour_ids, edge_values, live_slot):
    width = neighbour_ids.shape[-1]
    columns = lax.broadcasted_iota(jnp.int32, (1, 1, width), 2)
    zero_value = jnp.zeros((), jnp.bfloat16)
    dense = jnp.zeros((neighbour_ids.shape[0], width, width), jnp.bfloat16)
    for lane in range(neighbour_ids.shape[1]):
        picked = neighbour_ids[:, lane, :, None] == columns
        scaled = jnp.where(live_slot[:, None], edge_values[:, lane, :], zero_value)
        dense = dense + jnp.where(picked, scaled[:, :, None], zero_value)
    return dense


def shards(
    features,
    weight,
    bias_vector,
    tile_rows,
    tile_cols,
    neighbours,
    edge_weights,
    tile_count,
    cotangent,
):
    tile_size = neighbours.shape[-1]
    hidden = weight.shape[1]
    blocks_own = cotangent.shape[0] // tile_size
    row_blocks = blocks_own * lax.axis_size("col")
    col_blocks = blocks_own * lax.axis_size("row")
    rows_here = tile_rows[0, 0]
    cols_here = tile_cols[0, 0]
    ids_here = neighbours[0, 0]
    values_here = edge_weights[0, 0]
    limit = tile_count[0, 0]
    groups_needed = (limit + tile_group - 1) // tile_group
    panel = lax.all_gather(features, "row", axis=1, tiled=True)
    projected = jnp.dot(panel, weight, preferred_element_type=jnp.float32).astype(jnp.bfloat16)
    proj_blocks = projected.reshape(col_blocks, tile_size, hidden)

    def slot_info(index):
        first = index * tile_group
        slot_ids = first + jnp.arange(tile_group, dtype=jnp.int32)
        live_slot = slot_ids < limit
        block_rows = lax.dynamic_slice_in_dim(rows_here, first, tile_group, 0)
        block_cols = lax.dynamic_slice_in_dim(cols_here, first, tile_group, 0)
        return (first, live_slot, block_rows, block_cols)

    def build_group(first, live_slot):
        group_ids = lax.dynamic_slice_in_dim(ids_here, first, tile_group, 0)
        group_values = lax.dynamic_slice_in_dim(values_here, first, tile_group, 0)
        return dense_tiles(group_ids, group_values, live_slot)

    stored_init = jnp.zeros((1, 1, 1), jnp.bfloat16)

    def forward_group(index, carry):
        sums, stored = carry
        first, live_slot, block_rows, block_cols = slot_info(index)
        dense = build_group(first, live_slot)
        gathered = jnp.take(proj_blocks, block_cols, axis=0)
        products = jnp.einsum("tij,tjh->tih", dense, gathered, preferred_element_type=jnp.float32)
        sums = sums.at[block_rows].add(products)
        return (sums, stored)

    forward_init = (jnp.zeros((row_blocks, tile_size, hidden), jnp.float32), stored_init)
    forward_sums, stored = lax.fori_loop(0, groups_needed, forward_group, forward_init)
    partial_value = forward_sums.reshape(row_blocks * tile_size, hidden)
    pre = lax.psum_scatter(partial_value, "col", scatter_dimension=0, tiled=True) + bias_vector
    squashed = jax.nn.sigmoid(pre)
    activations = pre * squashed
    pre_grad = (cotangent * squashed * (1.0 + pre * (1.0 - squashed))).astype(jnp.bfloat16)
    grad_band = lax.all_gather(pre_grad, "col", axis=0, tiled=True)
    bias_part = jnp.sum(pre_grad.astype(jnp.float32), axis=0)
    grad_blocks = grad_band.reshape(row_blocks, tile_size, hidden)

    def backward_group(index, sums):
        first, live_slot, block_rows, block_cols = slot_info(index)
        dense = build_group(first, live_slot)
        gathered = jnp.take(grad_blocks, block_rows, axis=0)
        products = jnp.einsum("tij,tih->tjh", dense, gathered, preferred_element_type=jnp.float32)
        return sums.at[block_cols].add(products)

    backward_init = jnp.zeros((col_blocks, tile_size, hidden), jnp.float32)
    proj_grad = lax.fori_loop(0, groups_needed, backward_group, backward_init).reshape(
        col_blocks * tile_size, hidden
    )
    weight_wide = weight.astype(jnp.float32)
    feature_term = jnp.einsum("nh,fh->nf", proj_grad, weight_wide, precision=lax.Precision.HIGHEST)
    grad_features = lax.psum_scatter(feature_term, "row", scatter_dimension=1, tiled=True).astype(
        jnp.bfloat16
    )
    weight_part = jnp.einsum(
        "nf,nh->fh",
        panel,
        proj_grad,
        precision=lax.Precision.HIGHEST,
        preferred_element_type=jnp.float32,
    )
    node_count = cotangent.shape[0] * lax.axis_size("row") * lax.axis_size("col")
    shrink = float(node_count) ** (-0.5)
    weight_sum, bias_sum = lax.psum((weight_part, bias_part), ("row", "col"))
    return (activations, grad_features, weight_sum * shrink, bias_sum * shrink)


def solution(mesh):
    in_specs = (
        P("col", "row"),
        P(),
        P(),
        P("row", "col", None),
        P("row", "col", None),
        P("row", "col", None, None, None),
        P("row", "col", None, None, None),
        P("row", "col"),
        P(("row", "col"), None),
    )
    out_specs = (P(("row", "col"), None), P("col", "row"), P(), P())
    return jax.shard_map(shards, mesh=mesh, in_specs=in_specs, out_specs=out_specs, check_vma=False)
```

profile of v0, /device:TPU:0, one launch (start us, length us, event | category | flops | bytes accessed | tf_op | source)
XLA Modules:
  0.0 330.6 jit_solution(12802950549451873855)
XLA Ops:
  7.2 0.0 reduce-scatter.3.cloned.1.call-start
  7.9 6.7 %all_gather.6 = bf16[512,128]{0,1:T(8,128)(2,1)S(1)} all-gather(bf16[512,32]{0,1:T(8,128)(2,1)} %param.13), channel_id=1, replica_groups=mesh['row'=4,'col'=8] {'row'}, dimensions={1}, use_global_device_ids=true | all-gather | bytes 163840 | tf_op jit(solution)/shard_map/all_gather | solution.py:43
  14.7 0.8 copy-done.4
  15.5 0.2 convolution_convert_fusion
  15.8 0.6 copy-done.5
  16.4 11.6 %while.20 = (s32[]{:T(128)}, f32[8,128,128]{2,1,0:T(8,128)S(1)}, s32[]{:T(128)}, s32[128]{0:T(128)S(1)}, s32[128,2,128]{2,0,1:T(8,128)S(1)}, /*index=5*/s32[]{:T...) while((s32[]{:T(128)}, f32[8,128,128]{2,1,0:T(8,128)S(1)}, ...), condition=%wide.region_2.3_spmd, body=%wide.region_0.2_spmd.sunk | while | flops 69735608 | bytes 5845727 | solution.py:72
  16.4 0.7 compare_and_fusion.4
  17.2 0.1 fusion.54
  17.2 0.6 gather_fusion
  17.9 2.6 fusion.55
  20.5 0.1 compare_select_fusion.8
  20.6 1.6 scatter_fusion
  22.2 0.7 compare_and_fusion.4
  23.0 0.1 fusion.54
  23.1 0.6 gather_fusion
  23.7 2.6 fusion.55
  26.4 0.1 compare_select_fusion.8
  26.4 1.6 scatter_fusion
  28.1 0.8 copy-done.1
  28.9 0.0 reduce-scatter.3.cloned.1.call-update
  28.9 0.0 all-reduce.2.cloned.1.call-start
  28.9 94.6 %reduce-scatter.3.cloned.1.call-done = f32[128,128]{1,0:T(8,128)} async-done(((f32[1024,128]{1,0:T(8,128)}), f32[128,128]{1,0:T(8,128)}) %reduce-scatter.3.cloned.1.call-update) | async-done | bytes 65552 | tf_op jit(solution)/shard_map/reduce_scatter | solution.py:74
  123.5 1.5 convert_reduce_fusion
  125.0 30.9 %all_gather.7 = bf16[1024,128]{1,0:T(8,128)(2,1)S(1)} all-gather(bf16[128,128]{1,0:T(8,128)(2,1)S(1)} %get-tuple-element.147), channel_id=1, replica_groups=mesh['row'=4,'col'=8] {'col'}, dimensions={0}, use_global_device_ids=true | all-gather | bytes 294912 | tf_op jit(solution)/shard_map/all_gather | solution.py:78
  155.9 7.3 %while.21 = (s32[]{:T(128)}, f32[4,128,128]{2,1,0:T(8,128)S(1)}, s32[]{:T(128)}, s32[128]{0:T(128)S(1)}, s32[128,2,128]{2,0,1:T(8,128)S(1)}, /*index=5*/s32[]{:T...) while((s32[]{:T(128)}, f32[4,128,128]{2,1,0:T(8,128)S(1)}, ...), condition=%wide.region_6.7_spmd, body=%wide.region_4.6_spmd.sunk | while | flops 69735608 | bytes 5845727 | solution.py:90
  155.9 0.7 compare_and_fusion.5
  156.7 0.1 fusion.58
  156.8 0.6 gather_fusion.1
  157.4 0.4 fusion.59
  157.9 0.1 compare_select_fusion.9
  157.9 1.6 scatter_fusion.1
  159.6 0.7 compare_and_fusion.5
  160.3 0.1 fusion.58
  160.4 0.6 gather_fusion.1
  161.1 0.4 fusion.59
  161.5 0.1 compare_select_fusion.9
  161.6 1.6 scatter_fusion.1
  163.2 1.0 convolution_bitcast_fusion
  164.2 0.0 all-reduce.2.cloned.1.call-update
  164.2 0.0 reduce-scatter.5.cloned.1.call-start
  164.3 1.0 fusion.37
  165.3 56.5 %psum.15 = f32[128]{0:T(128)S(1)} all-reduce(f32[128]{0:T(128)S(1)} %get-tuple-element.146), channel_id=1, replica_groups=mesh['row'=4,'col'=8] {'row','col'}, use_global_device_ids=true, to_apply=%region_10.11 | all-reduce | flops 128 | bytes 1024 | tf_op jit(solution)/shard_map/psum | solution.py:107
  221.8 0.5 broadcast_multiply_fusion.1
  222.3 76.8 %all-reduce.2.cloned.1.call-done = f32[128,128]{0,1:T(8,128)} async-done(((f32[128,128]{0,1:T(8,128)}), f32[128,128]{0,1:T(8,128)}) %all-reduce.2.cloned.1.call-update) | async-done | bytes 65552 | tf_op jit(solution)/shard_map/psum | solution.py:107
  299.2 0.8 broadcast_multiply_fusion
  300.0 0.7 copy.15
  300.7 21.9 %reduce-scatter.5.cloned.1.call-done = f32[512,32]{0,1:T(8,128)} async-done(((f32[512,128]{0,1:T(8,128)}), f32[512,32]{0,1:T(8,128)}) %reduce-scatter.5.cloned.1.call-update) | async-done | bytes 65552 | tf_op jit(solution)/shard_map/reduce_scatter | solution.py:95
  322.6 1.5 convert_element_type.15
  (26 shorter events, 0.2 us)
Async XLA Ops:
  7.2 8.4 %copy-start = (bf16[128,128]{1,0:T(8,128)(2,1)S(1)}, bf16[128,128]{1,0:T(8,128)(2,1)}, u32[]{:S(2)}) copy-start(bf16[128,128]{1,0:T(8,128)(2,1)} %param.14) | copy-start | bytes 98308
  7.2 7.5 %copy-start.2 = (s32[1,1,128,2,128]{4,3,2,1,0:T(2,128)S(1)}, s32[1,1,128,2,128]{4,3,2,1,0:T(2,128)}, u32[]{:S(2)}) copy-start(s32[1,1,128,2,128]{4,3,2,1,0:T(2,128)} %param.18) | copy-start | bytes 393220
  7.2 116.3 %reduce-scatter.3.cloned.1.call-start = ((), (), s32[]{:S(2)}) async-start(), calls=%async_computation.2 | async-start | bytes 589824 | tf_op jit(solution)/shard_map/reduce_scatter | solution.py:74
  14.7 0.8 copy-start.4
  15.8 0.7 copy-start.5
  15.8 0.7 copy-start.6
  28.1 0.8 copy-start.1
  28.1 95.4 %copy-start.3 = (f32[128,128]{1,0:T(8,128)S(1)}, f32[128,128]{1,0:T(8,128)}, u32[]{:S(2)}) copy-start(f32[128,128]{1,0:T(8,128)} %param.21) | copy-start | bytes 196612
  28.9 94.6 %copy-start.7 = (f32[128]{0:T(128)S(1)}, f32[128]{0:T(128)}, u32[]{:S(2)}) copy-start(f32[128]{0:T(128)} %param.15) | copy-start | bytes 1540
  28.9 270.3 %all-reduce.2.cloned.1.call-start = ((), (), s32[]{:S(2)}) async-start(), calls=%async_computation.4 | async-start | bytes 131072 | tf_op jit(solution)/shard_map/psum | solution.py:107
  164.2 158.4 %reduce-scatter.5.cloned.1.call-start = ((), (), s32[]{:S(2)}) async-start(), calls=%async_computation.3 | async-start | bytes 327680 | tf_op jit(solution)/shard_map/reduce_scatter | solution.py:95
Sparse Core Ops, SparseCore 0:
  29.0 94.4 reduce-scatter.2
  164.3 134.7 all-reduce.1
  301.8 20.8 reduce-scatter.4
where the time goes:
time: 330 us; the launch traced here: 331 us
  waiting for transfers between devices  193 us (58%)
  blocking collectives  94.1 us (29%)
  between operations  14.6 us (4%)
  other arithmetic  14.3 us (4%)
  matrix products  8.33 us (3%)
  local copies, waits for them, and re-layouts  5.68 us (2%)
    reduce_scatter x1, waiting for transfers between devices, shards(): lax.psum_scatter(partial_value, 'col', scatter_dimension=0, tiled=True)  94.6 us
    psum x1, waiting for transfers between devices, shards(): weight_sum, bias_sum = lax.psum((weight_part, bias_part), ('row', 'col'))  76.8 us
    psum x1, blocking collectives, shards(): weight_sum, bias_sum = lax.psum((weight_part, bias_part), ('row', 'col'))  56.5 us
    all_gather x1, blocking collectives, shards(): grad_band = lax.all_gather(pre_grad, 'col', axis=0, tiled=True)  30.9 us
    reduce_scatter x1, waiting for transfers between devices, shards(): lax.psum_scatter(feature_term, 'row', scatter_dimension=1, tiled=True)  21.9 us
    all_gather x1, blocking collectives, shards(): panel = lax.all_gather(features, 'row', axis=1, tiled=True)  6.72 us
  transfers between devices with their start and end apart: 3, of which 3 were waited for; matrix products, arithmetic and copies ran while one was open for 1% of the time, Pallas kernels for 0%

commit v1 on v0

v1 whole, which is shorter than its diff:
```python
import functools

import jax
import jax.numpy as jnp
from jax import lax
from jax.experimental import pallas as pl
from jax.experimental.pallas import tpu as pltpu
from jax.sharding import PartitionSpec as P

f32 = jnp.float32
bf16 = jnp.bfloat16
tail = 16
wide = 1024
grant = 8 * 2**20


def room(*arrays):
    size = sum(a.size * a.dtype.itemsize for a in arrays)
    return pltpu.CompilerParams(vmem_limit_bytes=grant + 2 * size)


def vmem():
    return pl.BlockSpec(memory_space=pltpu.VMEM)


def smem():
    return pl.BlockSpec(memory_space=pltpu.SMEM)


def struct(shape, dtype):
    return jax.ShapeDtypeStruct(shape, dtype)


def dims(left, right):
    return (((left,), (right,)), ((), ()))


def dot(a, b, left=1, right=0):
    return lax.dot_general(a, b, dims(left, right), preferred_element_type=f32)


def each(count, body):
    if count <= 64:
        for index in range(count):
            body(index)
    else:
        lax.fori_loop(0, count, lambda index, none: (body(index), none)[1], 0)


def start_of(index, size):
    return index * size if isinstance(index, int) else pl.multiple_of(index * size, size)


def partner(me, step, size):
    if size & (size - 1) == 0:
        return me ^ step
    return (me + step) % size


def source(me, step, size):
    if size & (size - 1) == 0:
        return me ^ step
    return (me + size - step) % size


def exchange(value, axis, step):
    size = lax.axis_size(axis)
    return lax.ppermute(value, axis, [(i, partner(i, step, size)) for i in range(size)])


def band_kernel(limit, rows, cols, ids, values, band, sums, scaled):
    blocks, tile, _ = sums.shape
    row_blocks = band.shape[1] // tile
    slots = rows.shape[-1]
    lanes = ids.shape[0] // slots

    def clear(index):
        sums[index] = jnp.zeros((tile, tile), f32)

    each(blocks, clear)
    scaled[...] = values[...].astype(f32)
    which = lax.broadcasted_iota(jnp.int32, (tile, tile), 0)

    def add(slot, none):
        block = cols[0, 0, slot] * row_blocks + rows[0, 0, slot]
        dense = sums[block]
        for lane in range(lanes):
            line = pl.ds(slot * lanes + lane, 1)
            dense = dense + jnp.where(which == ids[line, :], scaled[line, :], 0.0)
        sums[block] = dense
        return none

    lax.fori_loop(0, limit[0, 0], add, 0)

    def put(index):
        col, row = index // row_blocks, index % row_blocks
        band[pl.ds(start_of(col, tile), tile), pl.ds(start_of(row, tile), tile)] = sums[index].astype(bf16)

    each(blocks, put)


def make_band(limit, rows, cols, ids, values, row_blocks, col_blocks):
    tile = ids.shape[-1]
    lines = ids.shape[-3] * ids.shape[-2]
    ids = ids.reshape(lines, tile)
    values = values.reshape(lines, tile)
    out = struct((col_blocks * tile, row_blocks * tile), bf16)
    sums = struct((col_blocks * row_blocks, tile, tile), f32)
    return pl.pallas_call(
        band_kernel,
        out_shape=out,
        in_specs=[smem(), smem(), smem(), vmem(), vmem()],
        out_specs=vmem(),
        scratch_shapes=[pltpu.VMEM(sums.shape, f32), pltpu.VMEM((lines, tile), f32)],
        compiler_params=pltpu.CompilerParams(vmem_limit_bytes=grant + sums.size * 4 + out.size * 2),
        cost_estimate=pl.CostEstimate(flops=8 * sums.size * 8, bytes_accessed=8 * 2**20, transcendentals=0),
        name="band",
    )(limit, rows, cols, ids, values)


def forward_kernel(size, owners, *refs):
    parts, (band, out, panel) = refs[:size], refs[size:]
    me = lax.axis_index("row")
    width = parts[0].shape[0]
    for step, part in enumerate(parts):
        slot = pl.multiple_of(source(me, step, size) * width, width)
        panel[pl.ds(slot, width), :] = part[...].astype(f32)
    left = panel[...].astype(bf16)
    own = out.shape[2]
    many = min(wide, band.shape[1])

    def piece(index):
        got = dot(left, band[:, pl.ds(start_of(index, many), many)]).astype(bf16)
        for part in range(many // own):
            out[index * (many // own) + part] = got[:, part * own : (part + 1) * own]

    each(band.shape[1] // many, piece)


def forward(parts, band, owners):
    hidden = parts[0].shape[0] * len(parts)
    nodes, total = band.shape
    return pl.pallas_call(
        functools.partial(forward_kernel, len(parts), owners),
        out_shape=struct((owners, hidden, total // owners), bf16),
        in_specs=[vmem()] * (len(parts) + 1),
        out_specs=vmem(),
        scratch_shapes=[pltpu.VMEM((hidden, nodes), f32)],
        compiler_params=room(band),
        name="forward",
    )(*parts, band)


def pair_rows(line):
    high = line.astype(bf16).astype(f32)
    row = lax.broadcasted_iota(jnp.int32, (tail, line.shape[1]), 0)
    return jnp.where(row == 0, high, jnp.where(row == 1, line - high, 0.0))


def own_kernel(got, weight, bias, cotangent, act, message):
    owners, hidden, own = got.shape
    total = got[0].astype(f32)
    for index in range(1, owners):
        total = total + got[index].astype(f32)
    high = total.astype(bf16)
    low = (total - high.astype(f32)).astype(bf16)
    pre = dot(high, weight[...], 0, 0) + dot(low, weight[...], 0, 0) + bias[...]
    squashed = jax.nn.sigmoid(pre)
    act[...] = pre * squashed
    grad = cotangent[...] * squashed * (1.0 + pre * (1.0 - squashed))
    grad = grad.astype(bf16)
    back = dot(weight[...], grad, 1, 1).astype(bf16)
    weight_part = dot(high, grad).astype(bf16)
    bias_part = pair_rows(jnp.sum(grad.astype(f32), axis=0, keepdims=True)).astype(bf16)
    for index in range(owners):
        message[index, :hidden, :] = back
        message[index, hidden : 2 * hidden, :] = weight_part
        message[index, 2 * hidden :, :] = bias_part


def own_rows(got, weight, bias, cotangent):
    owners, hidden, own = got.shape
    return pl.pallas_call(
        own_kernel,
        out_shape=(struct(cotangent.shape, f32), struct((owners, 2 * hidden + tail, own), bf16)),
        in_specs=[vmem()] * 4,
        out_specs=(vmem(), vmem()),
        compiler_params=room(got),
        name="own_rows",
    )(got, weight, bias.reshape(1, hidden), cotangent)


def backward_kernel(size, got, band, *refs):
    messages, (kept, wide_rows, grads, packed) = refs[:size], refs[size:]
    owners, _, own = got.shape
    hidden = kept.shape[0] * size
    width, nodes = kept.shape
    me = lax.axis_index("row")
    weight_part = jnp.zeros((hidden, own), f32)
    bias_part = jnp.zeros((1, own), f32)
    for index in range(owners):
        wide_rows[:, index * own : (index + 1) * own] = got[index, :hidden, :]
        weight_part = weight_part + got[index, hidden : 2 * hidden, :].astype(f32)
        bias_part = bias_part + jnp.sum(got[index, 2 * hidden :, :].astype(f32), axis=0, keepdims=True)
    many = min(wide, nodes)

    def piece(index):
        place = pl.ds(start_of(index, many), many)
        grads[:, place] = dot(wide_rows[...], band[place, :], 1, 1)

    each(nodes // many, piece)
    per_row = nodes // own
    for part in range(hidden // width):
        packed[width : 2 * width, part * own : (part + 1) * own] = weight_part[part * width : (part + 1) * width]
    packed[2 * width :, :] = jnp.zeros((tail, nodes), f32)
    packed[2 * width :, :own] = pair_rows(bias_part)
    for step in range(size):
        slot = pl.multiple_of(partner(me, step, size) * width, width)
        block = grads[pl.ds(slot, width), :]
        if step == 0:
            kept[...] = block
        packed[:width, :] = block
        messages[step][...] = packed[...].astype(bf16)


def backward(got, band, size):
    owners, _, own = got.shape
    nodes, total = band.shape
    hidden = (got.shape[1] - tail) // 2
    width = hidden // size
    message = struct((2 * width + tail, nodes), bf16)
    return pl.pallas_call(
        functools.partial(backward_kernel, size),
        out_shape=(message,) * size + (struct((width, nodes), f32),),
        in_specs=[vmem()] * 2,
        out_specs=(vmem(),) * (size + 1),
        scratch_shapes=[
            pltpu.VMEM((hidden, total), bf16),
            pltpu.VMEM((hidden, nodes), f32),
            pltpu.VMEM((2 * width + tail, nodes), f32),
        ],
        compiler_params=room(band, got),
        name="backward",
    )(got, band)


def final_kernel(size, shrink, *refs):
    messages, (kept, features, weight, bias, slots) = refs[:size], refs[size:]
    width, nodes = kept.shape
    hidden = weight.shape[0]
    me = lax.axis_index("row")
    total = kept[...]
    for step, message in enumerate(messages):
        whole = message[...].astype(f32)
        if step > 0:
            total = total + whole[:width]
        slots[source(me, step, size)] = whole[width:]
    features[...] = total.T.astype(bf16)
    summed = slots[0]
    for index in range(1, size):
        summed = summed + slots[index]
    summed = summed * shrink
    for part in range(hidden // width):
        weight[part * width : (part + 1) * width, :] = summed[:width, part * hidden : (part + 1) * hidden]
    bias[...] = summed[width : width + 1, :hidden] + summed[width + 1 : width + 2, :hidden]


def final(messages, kept, hidden, shrink):
    width, nodes = kept.shape
    size = len(messages)
    return pl.pallas_call(
        functools.partial(final_kernel, size, shrink),
        out_shape=(struct((nodes, width), bf16), struct((hidden, hidden), f32), struct((1, hidden), f32)),
        in_specs=[vmem()] * (size + 1),
        out_specs=(vmem(),) * 3,
        scratch_shapes=[pltpu.VMEM((size, width + tail, nodes), f32)],
        compiler_params=room(*messages),
        name="final",
    )(*messages, kept)


def shards(
    features,
    weight,
    bias_vector,
    tile_rows,
    tile_cols,
    neighbours,
    edge_weights,
    tile_count,
    cotangent,
):
    tile_size = neighbours.shape[-1]
    hidden = weight.shape[1]
    size, owners = lax.axis_size("row"), lax.axis_size("col")
    blocks_own = cotangent.shape[0] // tile_size
    row_blocks = blocks_own * owners
    col_blocks = blocks_own * size
    turned = features.T
    parts = [turned] + [exchange(turned, "row", step) for step in range(1, size)]
    band = make_band(tile_count, tile_rows, tile_cols, neighbours, edge_weights, row_blocks, col_blocks)
    sums = forward(parts, band, owners)
    sums = lax.all_to_all(sums, "col", 0, 0, tiled=True)
    activations, message = own_rows(sums, weight, bias_vector, cotangent)
    message = lax.all_to_all(message, "col", 0, 0, tiled=True)
    *messages, kept = backward(message, band, size)
    messages = [messages[0]] + [exchange(messages[step], "row", step) for step in range(1, size)]
    node_count = cotangent.shape[0] * size * owners
    grad_features, grad_weight, grad_bias = final(messages, kept, hidden, float(node_count) ** (-0.5))
    return (activations, grad_features, grad_weight, grad_bias.reshape(hidden))


def solution(mesh):
    in_specs = (
        P("col", "row"),
        P(),
        P(),
        P("row", "col", None),
        P("row", "col", None),
        P("row", "col", None, None, None),
        P("row", "col", None, None, None),
        P("row", "col"),
        P(("row", "col"), None),
    )
    out_specs = (P(("row", "col"), None), P("col", "row"), P(), P())
    return jax.shard_map(shards, mesh=mesh, in_specs=in_specs, out_specs=out_specs, check_vma=False)
```

time: 330 us -> 53.7 us (0.16)
  waiting for transfers between devices: 193 us -> 4.3 us
  blocking collectives: 94.1 us -> 34.8 us
  other arithmetic: 14.3 us -> 0 us
  between operations: 14.6 us -> 1.39 us
  matrix products: 8.33 us -> 0 us
  starting transfers between devices: 0.12 us -> 5.08 us
  Pallas kernels: 0 us -> 3.92 us
    reduce_scatter x2 -> x0, waiting for transfers between devices: 116 us -> none  [the longest x1 94.6 us: shards(): lax.psum_scatter(partial_value, 'col', scatter_dimension=0, tiled=True)]
    psum x1 -> x0, waiting for transfers between devices: 76.8 us -> none  [shards(): weight_sum, bias_sum = lax.psum((weight_part, bias_part), ('row', 'col'))]
    psum x1 -> x0, blocking collectives: 56.5 us -> none  [shards(): weight_sum, bias_sum = lax.psum((weight_part, bias_part), ('row', 'col'))]
    all_gather x2 -> x0, blocking collectives: 37.6 us -> none  [the longest x1 30.9 us: shards(): grad_band = lax.all_gather(pre_grad, 'col', axis=0, tiled=True)]
    all_to_all x0 -> x2, blocking collectives: none -> 34.8 us  [the longest x1 19.4 us: shards(): message = lax.all_to_all(message, 'col', 0, 0, tiled=True)]
    dot_general x7 -> x0, matrix products: 8.33 us -> none  [the longest x2 5.25 us: forward_group(): jnp.einsum('tij,tjh->tih', dense, gathered, preferred_element_type=jnp.fl...]
    scatter-add x4 -> x0, other arithmetic: 6.39 us -> none  [the longest x2 3.2 us: forward_group(): sums = sums.at[block_rows].add(products)]
    ppermute x0 -> x6, starting transfers between devices: none -> 5.08 us  [exchange(): lax.ppermute(value, axis, [(i, partner(i, step, size)) for i in range(siz...]
  transfers between devices with their start and end apart: 3 -> 6, of which waited for: 3 -> 2; matrix products, arithmetic and copies ran while one was open for 1% -> 0% of each run, Pallas kernels for 0% -> 3%
where the time goes in v1:
time: 53.7 us; the launch traced here: 53.3 us
  blocking collectives  34.8 us (65%)
  starting transfers between devices  5.08 us (9%)
  waiting for transfers between devices  4.3 us (8%)
  Pallas kernels  3.92 us (7%)
  local copies, waits for them, and re-layouts  3.77 us (7%)
  between operations  1.39 us (3%)
    all_to_all x1, blocking collectives, shards(): message = lax.all_to_all(message, 'col', 0, 0, tiled=True)  19.4 us
    all_to_all x1, blocking collectives, shards(): sums = lax.all_to_all(sums, 'col', 0, 0, tiled=True)  15.4 us
    ppermute x6, starting transfers between devices, exchange(): lax.ppermute(value, axis, [(i, partner(i, step, size)) for i in range(siz...  5.08 us
    ppermute x6, waiting for transfers between devices, exchange(): lax.ppermute(value, axis, [(i, partner(i, step, size)) for i in range(siz...  4.3 us
    unnamed x17, local copies, waits for them, and re-layouts  3.77 us
    pallas_call x1, Pallas kernels, make_band(): pl.pallas_call(band_kernel, out_shape=out, in_specs=[smem(), smem(), smem...  1.49 us
  transfers between devices with their start and end apart: 6, of which 2 were waited for; matrix products, arithmetic and copies ran while one was open for 0% of the time, Pallas kernels for 3%

profile of v1, /device:TPU:0, one launch (start us, length us, event | category | flops | bytes accessed | tf_op | source)
XLA Modules:
  0.0 53.3 jit_solution(5674644117144428373)
XLA Ops:
  0.6 2.5 %collective-permute-start.2 = (bf16[32,512]{1,0:T(8,128)(2,1)}, bf16[32,512]{1,0:T(8,128)(2,1)S(1)}, u32[]{:S(2)}, u32[]{:S(2)}) collective-permute-start(bf16[32,512]{1,0:T(8,128)(2,1)} %bitcast.7), channel_id=1, source_target_pairs={{0,24},{8,16},{16,8},{24,0},{1,25},{9,17},{17,9},{25,1},{2,26},{10... | collective-permute-start | bytes 98312 | tf_op jit(solution)/shard_map/ppermute | solution.py:68
  3.1 0.6 %collective-permute-start.1 = (bf16[32,512]{1,0:T(8,128)(2,1)}, bf16[32,512]{1,0:T(8,128)(2,1)S(1)}, u32[]{:S(2)}, u32[]{:S(2)}) collective-permute-start(bf16[32,512]{1,0:T(8,128)(2,1)} %bitcast.8), channel_id=1, source_target_pairs={{0,16},{8,24},{16,0},{24,8},{1,17},{9,25},{17,1},{25,9},{2,18},{10... | collective-permute-start | bytes 98312 | tf_op jit(solution)/shard_map/ppermute | solution.py:68
  3.7 0.0 collective-permute-start
  4.4 0.0 copy-start.5
  4.4 0.0 copy-start.6
  4.5 0.6 %copy-done.5 = s32[1,1,128]{2,1,0:T(1,128)S(1)} copy-done((s32[1,1,128]{2,1,0:T(1,128)S(1)}, s32[1,1,128]{2,1,0:T(1,128)}, u32[]{:S(2)}) %copy-start.5) | copy-done | bytes 536
  5.1 0.0 copy-done.6
  5.1 0.0 copy-start
  5.1 0.9 %copy-done = s32[1,1,128,2,128]{4,3,2,1,0:T(2,128)S(1)} copy-done((s32[1,1,128,2,128]{4,3,2,1,0:T(2,128)S(1)}, s32[1,1,128,2,128]{4,3,2,1,0:T(2,128)}, u32[]{:S(2)}) %copy-start) | copy-done | bytes 131096
  6.0 0.0 copy-start.2
  6.0 0.8 %copy-done.2 = bf16[1,1,128,2,128]{4,3,2,1,0:T(2,128)(2,1)S(1)} copy-done((bf16[1,1,128,2,128]{4,3,2,1,0:T(2,128)(2,1)S(1)}, bf16[1,1,128,2,128]{4,3,2,1,0:T(2,128)(2,1)}, u32[]{:S(2)}) %copy-start.2) | copy-done | bytes 65560
  6.9 0.0 copy-start.3
  6.9 1.5 %band.1.refs_4_ = bf16[512,1024]{1,0:T(8,128)(2,1)S(1)} custom-call(s32[1,1]{1,0:T(1,128)S(6)} %copy.14.limit, s32[1,1,128]{2,1,0:T(1,128)S(1)} %copy-done.5, s32[1,1,128]{2,1,0:T(1,128)S(1)} %copy-done.6, s32[256,128]{1,0:T(8,128)S(1)} %bitcast.5, bf16[256,128]{1,0:T(8,128)(2,1)S(1)} %bitcast.6), custom_call_target="tpu_custom_call" | custom-call | flops 33554432 | bytes 8388608 | tf_op jit(solution)/shard_map/band/pallas_call | solution.py:109
  8.4 0.0 collective-permute-done.2.refs_3_
  8.4 0.0 collective-permute-done.1.refs_2_
  8.4 0.0 collective-permute-done.refs_1_
  8.4 0.0 copy-done.3
  8.4 0.3 forward.1
  8.7 0.0 copy-start.1
  8.7 0.0 copy-start.4
  8.7 15.4 %all_to_all.10.got = bf16[8,128,128]{2,1,0:T(8,128)(2,1)S(1)} all-to-all(bf16[8,128,128]{2,1,0:T(8,128)(2,1)S(1)} %forward.1), channel_id=1, replica_groups=mesh['row'=4,'col'=8] {'col'}, dimensions={0} | all-to-all | bytes 524288 | tf_op jit(solution)/shard_map/all_to_all | solution.py:303
  24.2 0.0 copy-start.7
  24.2 0.0 copy-done.1
  24.2 0.0 copy-done.4
  24.2 0.6 %copy-done.7 = f32[128]{0:T(128)S(1)} copy-done((f32[128]{0:T(128)S(1)}, f32[128]{0:T(128)}, u32[]{:S(2)}) %copy-start.7) | copy-done | bytes 536
  24.8 0.9 %own_rows.1 = (f32[128,128]{1,0:T(8,128)}, bf16[8,272,128]{2,1,0:T(8,128)(2,1)S(1)}) custom-call(bf16[8,128,128]{2,1,0:T(8,128)(2,1)S(1)} %all_to_all.10.got, bf16[128,128]{1,0:T(8,128)(2,1)S(1)} %copy-done.4, f32[1,128]{1,0:T(1,128)S(1)} %bitcast.11, f32[128,128]{1,0:T(8,128)S(1)} %copy-done.1), custom_call_target="tpu_custom_call" | custom-call | tf_op jit(solution)/shard_map/own_rows/pallas_call | solution.py:183
  25.7 19.4 %all_to_all.11.got = bf16[8,272,128]{2,1,0:T(8,128)(2,1)S(1)} all-to-all(bf16[8,272,128]{2,1,0:T(8,128)(2,1)S(1)} %get-tuple-element.15), channel_id=1, replica_groups=mesh['row'=4,'col'=8] {'col'}, dimensions={0} | all-to-all | bytes 1114112 | tf_op jit(solution)/shard_map/all_to_all | solution.py:305
  45.1 0.5 backward.1
  45.6 0.1 collective-permute-start.3
  45.7 1.4 %collective-permute-start.4 = (bf16[80,512]{1,0:T(8,128)(2,1)S(1)}, bf16[80,512]{1,0:T(8,128)(2,1)S(1)}, u32[]{:S(2)}, u32[]{:S(2)}) collective-permute-start(bf16[80,512]{1,0:T(8,128)(2,1)S(1)} %get-tuple-element.18), channel_id=1, source_target_pairs={{0,16},{8,24},{16,0},{24,8},{1,17},{9,25},{17,1},{25,9},{2,18},{10... | collective-permute-start | bytes 245768 | tf_op jit(solution)/shard_map/ppermute | solution.py:68
  47.1 0.4 collective-permute-start.5
  47.6 0.0 collective-permute-done.3.refs_1_
  47.6 3.4 %collective-permute-done.4.refs_2_ = bf16[80,512]{1,0:T(8,128)(2,1)S(1)} collective-permute-done((bf16[80,512]{1,0:T(8,128)(2,1)S(1)}, bf16[80,512]{1,0:T(8,128)(2,1)S(1)}, u32[]{:S(2)}, u32[]{:S(2)}) %collective-permute-start.4) | collective-permute-done | bytes 81952 | tf_op jit(solution)/shard_map/ppermute | solution.py:68
  51.0 0.8 %collective-permute-done.5.refs_3_ = bf16[80,512]{1,0:T(8,128)(2,1)S(1)} collective-permute-done((bf16[80,512]{1,0:T(8,128)(2,1)S(1)}, bf16[80,512]{1,0:T(8,128)(2,1)S(1)}, u32[]{:S(2)}, u32[]{:S(2)}) %collective-permute-start.5) | collective-permute-done | bytes 81952 | tf_op jit(solution)/shard_map/ppermute | solution.py:68
  51.9 0.7 %final.1 = (bf16[512,32]{1,0:T(8,128)(2,1)S(1)}, f32[128,128]{1,0:T(8,128)}, f32[1,128]{1,0:T(1,128)}) custom-call(bf16[80,512]{1,0:T(8,128)(2,1)S(1)} %get-tuple-element.16.refs_0_, bf16[80,512]{1,0:T(8,128)(2,1)S(1)} %collective-permute-done.3.refs_1_, bf16[80,512]{1,0:T(8,128)(2,1)S(1)} %collective-permute-done.4.refs_2_, ...), custom_call_target="tpu_custom_call" | custom-call | tf_op jit(solution)/shard_map/final/pallas_call | solution.py:271
  52.6 0.7 %copy.13 = bf16[512,32]{0,1:T(8,128)(2,1)} copy(bf16[512,32]{1,0:T(8,128)(2,1)S(1)} %get-tuple-element.25) | data formatting | bytes 65536
Async XLA Ops:
  0.6 7.7 %collective-permute-start.2 = (bf16[32,512]{1,0:T(8,128)(2,1)}, bf16[32,512]{1,0:T(8,128)(2,1)S(1)}, u32[]{:S(2)}, u32[]{:S(2)}) collective-permute-start(bf16[32,512]{1,0:T(8,128)(2,1)} %bitcast.7), channel_id=1, source_target_pairs={{0,24},{8,16},{16,8},{24,0},{1,25},{9,17},{17,9},{25,1},{2,26},{10... | collective-permute-start | bytes 98312 | tf_op jit(solution)/shard_map/ppermute | solution.py:68
  3.1 5.3 %collective-permute-start.1 = (bf16[32,512]{1,0:T(8,128)(2,1)}, bf16[32,512]{1,0:T(8,128)(2,1)S(1)}, u32[]{:S(2)}, u32[]{:S(2)}) collective-permute-start(bf16[32,512]{1,0:T(8,128)(2,1)} %bitcast.8), channel_id=1, source_target_pairs={{0,16},{8,24},{16,0},{24,8},{1,17},{9,25},{17,1},{25,9},{2,18},{10... | collective-permute-start | bytes 98312 | tf_op jit(solution)/shard_map/ppermute | solution.py:68
  3.7 4.6 %collective-permute-start = (bf16[32,512]{1,0:T(8,128)(2,1)}, bf16[32,512]{1,0:T(8,128)(2,1)S(1)}, u32[]{:S(2)}, u32[]{:S(2)}) collective-permute-start(bf16[32,512]{1,0:T(8,128)(2,1)} %bitcast.9), channel_id=1, source_target_pairs={{0,8},{8,0},{16,24},{24,16},{1,9},{9,1},{17,25},{25,17},{2,10},{10... | collective-permute-start | bytes 98312 | tf_op jit(solution)/shard_map/ppermute | solution.py:68
  4.4 0.7 %copy-start.5 = (s32[1,1,128]{2,1,0:T(1,128)S(1)}, s32[1,1,128]{2,1,0:T(1,128)}, u32[]{:S(2)}) copy-start(s32[1,1,128]{2,1,0:T(1,128)} %rows.1) | copy-start | bytes 1540
  4.4 0.7 %copy-start.6 = (s32[1,1,128]{2,1,0:T(1,128)S(1)}, s32[1,1,128]{2,1,0:T(1,128)}, u32[]{:S(2)}) copy-start(s32[1,1,128]{2,1,0:T(1,128)} %cols.1) | copy-start | bytes 1540
  5.1 0.9 %copy-start = (s32[1,1,128,2,128]{4,3,2,1,0:T(2,128)S(1)}, s32[1,1,128,2,128]{4,3,2,1,0:T(2,128)}, u32[]{:S(2)}) copy-start(s32[1,1,128,2,128]{4,3,2,1,0:T(2,128)} %param.14) | copy-start | bytes 393220
  6.0 0.8 %copy-start.2 = (bf16[1,1,128,2,128]{4,3,2,1,0:T(2,128)(2,1)S(1)}, bf16[1,1,128,2,128]{4,3,2,1,0:T(2,128)(2,1)}, u32[]{:S(2)}) copy-start(bf16[1,1,128,2,128]{4,3,2,1,0:T(2,128)(2,1)} %param.15) | copy-start | bytes 196612
  6.9 1.5 %copy-start.3 = (bf16[512,32]{0,1:T(8,128)(2,1)S(1)}, bf16[512,32]{0,1:T(8,128)(2,1)}, u32[]{:S(2)}) copy-start(bf16[512,32]{0,1:T(8,128)(2,1)} %param.9) | copy-start | bytes 98308
  8.7 15.5 %copy-start.1 = (f32[128,128]{1,0:T(8,128)S(1)}, f32[128,128]{1,0:T(8,128)}, u32[]{:S(2)}) copy-start(f32[128,128]{1,0:T(8,128)} %cotangent.1) | copy-start | bytes 196612
  8.7 15.5 %copy-start.4 = (bf16[128,128]{1,0:T(8,128)(2,1)S(1)}, bf16[128,128]{1,0:T(8,128)(2,1)}, u32[]{:S(2)}) copy-start(bf16[128,128]{1,0:T(8,128)(2,1)} %weight.1) | copy-start | bytes 98308
  24.2 0.7 %copy-start.7 = (f32[128]{0:T(128)S(1)}, f32[128]{0:T(128)}, u32[]{:S(2)}) copy-start(f32[128]{0:T(128)} %param.11) | copy-start | bytes 1540
  45.6 1.9 %collective-permute-start.3 = (bf16[80,512]{1,0:T(8,128)(2,1)S(1)}, bf16[80,512]{1,0:T(8,128)(2,1)S(1)}, u32[]{:S(2)}, u32[]{:S(2)}) collective-permute-start(bf16[80,512]{1,0:T(8,128)(2,1)S(1)} %get-tuple-element.17), channel_id=1, source_target_pairs={{0,8},{8,0},{16,24},{24,16},{1,9},{9,1},{17,25},{25,17},{2,10},{10... | collective-permute-start | bytes 245768 | tf_op jit(solution)/shard_map/ppermute | solution.py:68
  45.7 5.3 %collective-permute-start.4 = (bf16[80,512]{1,0:T(8,128)(2,1)S(1)}, bf16[80,512]{1,0:T(8,128)(2,1)S(1)}, u32[]{:S(2)}, u32[]{:S(2)}) collective-permute-start(bf16[80,512]{1,0:T(8,128)(2,1)S(1)} %get-tuple-element.18), channel_id=1, source_target_pairs={{0,16},{8,24},{16,0},{24,8},{1,17},{9,25},{17,1},{25,9},{2,18},{10... | collective-permute-start | bytes 245768 | tf_op jit(solution)/shard_map/ppermute | solution.py:68
  47.1 4.7 %collective-permute-start.5 = (bf16[80,512]{1,0:T(8,128)(2,1)S(1)}, bf16[80,512]{1,0:T(8,128)(2,1)S(1)}, u32[]{:S(2)}, u32[]{:S(2)}) collective-permute-start(bf16[80,512]{1,0:T(8,128)(2,1)S(1)} %get-tuple-element.19), channel_id=1, source_target_pairs={{0,24},{8,16},{16,8},{24,0},{1,25},{9,17},{17,9},{25,1},{2,26},{10... | collective-permute-start | bytes 245768 | tf_op jit(solution)/shard_map/ppermute | solution.py:68

commit v2 on v1

--- a/solution.py
+++ b/solution.py
@@ -68,54 +68,69 @@
     return lax.ppermute(value, axis, [(i, partner(i, step, size)) for i in range(size)])
 
 
-def band_kernel(limit, rows, cols, ids, values, band, sums, scaled):
+def band_kernel(limit, rows, cols, ids, values, bias, band, bias_out, sums, scaled, here, row, col, sems):
     blocks, tile, _ = sums.shape
     row_blocks = band.shape[1] // tile
     slots = rows.shape[-1]
-    lanes = ids.shape[0] // slots
+    ids_here, values_here = here
+    lanes = ids_here.shape[0] // slots
+    pairs = ((ids, ids_here), (values, values_here), (rows, row), (cols, col), (bias, bias_out))
+    copies = [pltpu.make_async_copy(a, b, sems.at[i]) for i, (a, b) in enumerate(pairs)]
+    for copy in copies:
+        copy.start()
 
     def clear(index):
         sums[index] = jnp.zeros((tile, tile), f32)
 
     each(blocks, clear)
-    scaled[...] = values[...].astype(f32)
+    for copy in copies:
+        copy.wait()
+    scaled[...] = values_here[...].astype(f32)
     which = lax.broadcasted_iota(jnp.int32, (tile, tile), 0)
 
     def add(slot, none):
-        block = cols[0, 0, slot] * row_blocks + rows[0, 0, slot]
+        block = col[0, 0, slot] * row_blocks + row[0, 0, slot]
         dense = sums[block]
         for lane in range(lanes):
             line = pl.ds(slot * lanes + lane, 1)
-            dense = dense + jnp.where(which == ids[line, :], scaled[line, :], 0.0)
+            dense = dense + jnp.where(which == ids_here[line, :], scaled[line, :], 0.0)
         sums[block] = dense
         return none
 
     lax.fori_loop(0, limit[0, 0], add, 0)
 
     def put(index):
-        col, row = index // row_blocks, index % row_blocks
-        band[pl.ds(start_of(col, tile), tile), pl.ds(start_of(row, tile), tile)] = sums[index].astype(bf16)
+        c, r = index // row_blocks, index % row_blocks
+        band[pl.ds(start_of(c, tile), tile), pl.ds(start_of(r, tile), tile)] = sums[index].astype(bf16)
 
     each(blocks, put)
 
 
-def make_band(limit, rows, cols, ids, values, row_blocks, col_blocks):
+def make_band(limit, rows, cols, ids, values, bias, row_blocks, col_blocks):
     tile = ids.shape[-1]
     lines = ids.shape[-3] * ids.shape[-2]
     ids = ids.reshape(lines, tile)
     values = values.reshape(lines, tile)
+    bias = bias.reshape(1, -1)
     out = struct((col_blocks * tile, row_blocks * tile), bf16)
     sums = struct((col_blocks * row_blocks, tile, tile), f32)
     return pl.pallas_call(
         band_kernel,
-        out_shape=out,
-        in_specs=[smem(), smem(), smem(), vmem(), vmem()],
-        out_specs=vmem(),
-        scratch_shapes=[pltpu.VMEM(sums.shape, f32), pltpu.VMEM((lines, tile), f32)],
+        out_shape=(out, struct(bias.shape, f32)),
+        in_specs=[smem()] + [pl.BlockSpec(memory_space=pltpu.HBM)] * 5,
+        out_specs=(vmem(), vmem()),
+        scratch_shapes=[
+            pltpu.VMEM(sums.shape, f32),
+            pltpu.VMEM((lines, tile), f32),
+            (pltpu.VMEM((lines, tile), jnp.int32), pltpu.VMEM((lines, tile), bf16)),
+            pltpu.SMEM(rows.shape, jnp.int32),
+            pltpu.SMEM(cols.shape, jnp.int32),
+            pltpu.SemaphoreType.DMA((5,)),
+        ],
         compiler_params=pltpu.CompilerParams(vmem_limit_bytes=grant + sums.size * 4 + out.size * 2),
         cost_estimate=pl.CostEstimate(flops=8 * sums.size * 8, bytes_accessed=8 * 2**20, transcendentals=0),
         name="band",
-    )(limit, rows, cols, ids, values)
+    )(limit, *[pltpu.with_memory_space_constraint(a, pltpu.HBM) for a in (rows, cols, ids, values, bias)])
 
 
 def forward_kernel(size, owners, *refs):
@@ -170,7 +185,7 @@
     grad = cotangent[...] * squashed * (1.0 + pre * (1.0 - squashed))
     grad = grad.astype(bf16)
     back = dot(weight[...], grad, 1, 1).astype(bf16)
-    weight_part = dot(high, grad).astype(bf16)
+    weight_part = (dot(high, grad) + dot(low, grad)).astype(bf16)
     bias_part = pair_rows(jnp.sum(grad.astype(f32), axis=0, keepdims=True)).astype(bf16)
     for index in range(owners):
         message[index, :hidden, :] = back
@@ -187,7 +202,7 @@
         out_specs=(vmem(), vmem()),
         compiler_params=room(got),
         name="own_rows",
-    )(got, weight, bias.reshape(1, hidden), cotangent)
+    )(got, weight, bias, cotangent)
 
 
 def backward_kernel(size, got, band, *refs):
@@ -255,7 +270,7 @@
         if step > 0:
             total = total + whole[:width]
         slots[source(me, step, size)] = whole[width:]
-    features[...] = total.T.astype(bf16)
+    features[...] = total.astype(bf16)
     summed = slots[0]
     for index in range(1, size):
         summed = summed + slots[index]
@@ -270,7 +285,7 @@
     size = len(messages)
     return pl.pallas_call(
         functools.partial(final_kernel, size, shrink),
-        out_shape=(struct((nodes, width), bf16), struct((hidden, hidden), f32), struct((1, hidden), f32)),
+        out_shape=(struct((width, nodes), bf16), struct((hidden, hidden), f32), struct((1, hidden), f32)),
         in_specs=[vmem()] * (size + 1),
         out_specs=(vmem(),) * 3,
         scratch_shapes=[pltpu.VMEM((size, width + tail, nodes), f32)],
@@ -298,16 +313,18 @@
     col_blocks = blocks_own * size
     turned = features.T
     parts = [turned] + [exchange(turned, "row", step) for step in range(1, size)]
-    band = make_band(tile_count, tile_rows, tile_cols, neighbours, edge_weights, row_blocks, col_blocks)
+    band, bias = make_band(
+        tile_count, tile_rows, tile_cols, neighbours, edge_weights, bias_vector, row_blocks, col_blocks
+    )
     sums = forward(parts, band, owners)
     sums = lax.all_to_all(sums, "col", 0, 0, tiled=True)
-    activations, message = own_rows(sums, weight, bias_vector, cotangent)
+    activations, message = own_rows(sums, weight, bias, cotangent)
     message = lax.all_to_all(message, "col", 0, 0, tiled=True)
     *messages, kept = backward(message, band, size)
     messages = [messages[0]] + [exchange(messages[step], "row", step) for step in range(1, size)]
     node_count = cotangent.shape[0] * size * owners
     grad_features, grad_weight, grad_bias = final(messages, kept, hidden, float(node_count) ** (-0.5))
-    return (activations, grad_features, grad_weight, grad_bias.reshape(hidden))
+    return (activations, grad_features.T, grad_weight, grad_bias.reshape(hidden))
 
 
 def solution(mesh):

time: 53.7 us -> 49.9 us (0.929)
  local copies, waits for them, and re-layouts: 3.77 us -> 0.02 us
  waiting for transfers between devices: 4.3 us -> 5.42 us
  blocking collectives: 34.8 us -> 33.7 us
    unnamed x17 -> x6, local copies, waits for them, and re-layouts: 3.77 us -> 0.02 us
    ppermute x6, waiting for transfers between devices: 4.3 us -> 5.42 us  [exchange(): lax.ppermute(value, axis, [(i, partner(i, step, size)) for i in range(siz...]
    all_to_all x1, blocking collectives: 15.4 us -> 14.6 us  [shards(): sums = lax.all_to_all(sums, 'col', 0, 0, tiled=True)]
  transfers between devices with their start and end apart: 6 -> 6, of which waited for: 2 -> 3; matrix products, arithmetic and copies ran while one was open for 0% -> 0% of each run, Pallas kernels for 3% -> 3%
where the time goes in v2:
time: 49.9 us; the launch traced here: 49.6 us
  blocking collectives  33.7 us (68%)
  waiting for transfers between devices  5.42 us (11%)
  starting transfers between devices  5.08 us (10%)
  Pallas kernels  4.08 us (8%)
  between operations  1.36 us (3%)
    all_to_all x1, blocking collectives, shards(): message = lax.all_to_all(message, 'col', 0, 0, tiled=True)  19 us
    all_to_all x1, blocking collectives, shards(): sums = lax.all_to_all(sums, 'col', 0, 0, tiled=True)  14.6 us
    ppermute x6, waiting for transfers between devices, exchange(): lax.ppermute(value, axis, [(i, partner(i, step, size)) for i in range(siz...  5.42 us
    ppermute x6, starting transfers between devices, exchange(): lax.ppermute(value, axis, [(i, partner(i, step, size)) for i in range(siz...  5.08 us
    pallas_call x1, Pallas kernels, make_band(): pl.pallas_call(band_kernel, out_shape=(out, struct(bias.shape, f32)), in_...  1.7 us
  transfers between devices with their start and end apart: 6, of which 3 were waited for; matrix products, arithmetic and copies ran while one was open for 0% of the time, Pallas kernels for 3%

profile of v2, /device:TPU:0, one launch (start us, length us, event | category | flops | bytes accessed | tf_op | source)
XLA Modules:
  0.0 49.6 jit_solution(11619639276323144043)
XLA Ops:
  0.6 2.5 %collective-permute-start.2 = (bf16[32,512]{1,0:T(8,128)(2,1)}, bf16[32,512]{1,0:T(8,128)(2,1)S(1)}, u32[]{:S(2)}, u32[]{:S(2)}) collective-permute-start(bf16[32,512]{1,0:T(8,128)(2,1)} %bitcast.6), channel_id=1, source_target_pairs={{0,24},{8,16},{16,8},{24,0},{1,25},{9,17},{17,9},{25,1},{2,26},{10... | collective-permute-start | bytes 98312 | tf_op jit(solution)/shard_map/ppermute | solution.py:68
  3.1 0.6 %collective-permute-start.1 = (bf16[32,512]{1,0:T(8,128)(2,1)}, bf16[32,512]{1,0:T(8,128)(2,1)S(1)}, u32[]{:S(2)}, u32[]{:S(2)}) collective-permute-start(bf16[32,512]{1,0:T(8,128)(2,1)} %bitcast.7), channel_id=1, source_target_pairs={{0,16},{8,24},{16,0},{24,8},{1,17},{9,25},{17,1},{25,9},{2,18},{10... | collective-permute-start | bytes 98312 | tf_op jit(solution)/shard_map/ppermute | solution.py:68
  3.7 0.0 collective-permute-start
  4.4 0.0 copy-start.1
  4.4 1.7 %band.1 = (bf16[512,1024]{1,0:T(8,128)(2,1)S(1)}, f32[1,128]{1,0:T(1,128)S(1)}) custom-call(s32[1,1]{1,0:T(1,128)S(6)} %copy.13.limit, s32[1,1,128]{2,1,0:T(1,128)} %rows.1, s32[1,1,128]{2,1,0:T(1,128)} %cols.1, s32[256,128]{1,0:T(8,128)} %bitcast.10, bf16[256,128]{1,0:T(8,128)(2,1)} %bitcast.11, f32[1,128]{1,0:T(1,128)} %bitcast.12), custom_call_target="tpu_custom_call" | custom-call | flops 33554432 | bytes 8388608 | tf_op jit(solution)/shard_map/band/pallas_call | solution.py:117
  6.2 0.0 collective-permute-done.2.refs_3_
  6.2 1.1 %collective-permute-done.1.refs_2_ = bf16[32,512]{1,0:T(8,128)(2,1)S(1)} collective-permute-done((bf16[32,512]{1,0:T(8,128)(2,1)}, bf16[32,512]{1,0:T(8,128)(2,1)S(1)}, u32[]{:S(2)}, u32[]{:S(2)}) %collective-permute-start.1) | collective-permute-done | bytes 32800 | tf_op jit(solution)/shard_map/ppermute | solution.py:68
  7.3 0.0 collective-permute-done.refs_1_
  7.3 0.0 copy-done.1
  7.3 0.3 forward.1
  7.6 0.0 copy-start
  7.6 0.0 copy-start.2
  7.6 14.6 %all_to_all.10.got = bf16[8,128,128]{2,1,0:T(8,128)(2,1)S(1)} all-to-all(bf16[8,128,128]{2,1,0:T(8,128)(2,1)S(1)} %forward.1), channel_id=1, replica_groups=mesh['row'=4,'col'=8] {'col'}, dimensions={0} | all-to-all | bytes 524288 | tf_op jit(solution)/shard_map/all_to_all | solution.py:320
  22.3 0.0 copy-done
  22.3 0.0 copy-done.2
  22.3 0.9 %own_rows.1 = (f32[128,128]{1,0:T(8,128)}, bf16[8,272,128]{2,1,0:T(8,128)(2,1)S(1)}) custom-call(bf16[8,128,128]{2,1,0:T(8,128)(2,1)S(1)} %all_to_all.10.got, bf16[128,128]{1,0:T(8,128)(2,1)S(1)} %copy-done.2, f32[1,128]{1,0:T(1,128)S(1)} %get-tuple-element.17.bias, f32[128,128]{1,0:T(8,128)S(1)} %copy-done), custom_call_target="tpu_custom_call" | custom-call | tf_op jit(solution)/shard_map/own_rows/pallas_call | solution.py:198
  23.2 19.0 %all_to_all.11.got = bf16[8,272,128]{2,1,0:T(8,128)(2,1)S(1)} all-to-all(bf16[8,272,128]{2,1,0:T(8,128)(2,1)S(1)} %get-tuple-element.19), channel_id=1, replica_groups=mesh['row'=4,'col'=8] {'col'}, dimensions={0} | all-to-all | bytes 1114112 | tf_op jit(solution)/shard_map/all_to_all | solution.py:322
  42.2 0.5 %backward.1 = (bf16[80,512]{1,0:T(8,128)(2,1)S(1)}, bf16[80,512]{1,0:T(8,128)(2,1)S(1)}, bf16[80,512]{1,0:T(8,128)(2,1)S(1)}, bf16[80,512]{1,0:T(8,128)(2,1)S(1)}, f32[32,512]{1,0:T(8,128)S(1)}) custom-call(bf16[8,272,128]{2,1,0:T(8,128)(2,1)S(1)} %all_to_all.11.got, bf16[512,1024]{1,0:T(8,128)(2,1)S(1)} %get-tuple-element.16.refs_4_.band), custom_call_target="tpu_custom_call" | custom-call | tf_op jit(solution)/shard_map/backward/pallas_call | solution.py:247
  42.7 0.1 collective-permute-start.3
  42.8 1.3 %collective-permute-start.4 = (bf16[80,512]{1,0:T(8,128)(2,1)S(1)}, bf16[80,512]{1,0:T(8,128)(2,1)S(1)}, u32[]{:S(2)}, u32[]{:S(2)}) collective-permute-start(bf16[80,512]{1,0:T(8,128)(2,1)S(1)} %get-tuple-element.22), channel_id=1, source_target_pairs={{0,16},{8,24},{16,0},{24,8},{1,17},{9,25},{17,1},{25,9},{2,18},{10... | collective-permute-start | bytes 245768 | tf_op jit(solution)/shard_map/ppermute | solution.py:68
  44.1 0.5 %collective-permute-start.5 = (bf16[80,512]{1,0:T(8,128)(2,1)S(1)}, bf16[80,512]{1,0:T(8,128)(2,1)S(1)}, u32[]{:S(2)}, u32[]{:S(2)}) collective-permute-start(bf16[80,512]{1,0:T(8,128)(2,1)S(1)} %get-tuple-element.23), channel_id=1, source_target_pairs={{0,24},{8,16},{16,8},{24,0},{1,25},{9,17},{17,9},{25,1},{2,26},{10... | collective-permute-start | bytes 245768 | tf_op jit(solution)/shard_map/ppermute | solution.py:68
  44.6 0.0 collective-permute-done.3.refs_1_
  44.6 3.4 %collective-permute-done.4.refs_2_ = bf16[80,512]{1,0:T(8,128)(2,1)S(1)} collective-permute-done((bf16[80,512]{1,0:T(8,128)(2,1)S(1)}, bf16[80,512]{1,0:T(8,128)(2,1)S(1)}, u32[]{:S(2)}, u32[]{:S(2)}) %collective-permute-start.4) | collective-permute-done | bytes 81952 | tf_op jit(solution)/shard_map/ppermute | solution.py:68
  48.1 0.8 %collective-permute-done.5.refs_3_ = bf16[80,512]{1,0:T(8,128)(2,1)S(1)} collective-permute-done((bf16[80,512]{1,0:T(8,128)(2,1)S(1)}, bf16[80,512]{1,0:T(8,128)(2,1)S(1)}, u32[]{:S(2)}, u32[]{:S(2)}) %collective-permute-start.5) | collective-permute-done | bytes 81952 | tf_op jit(solution)/shard_map/ppermute | solution.py:68
  48.9 0.7 %final.1 = (bf16[32,512]{1,0:T(8,128)(2,1)}, f32[128,128]{1,0:T(8,128)}, f32[1,128]{1,0:T(1,128)}) custom-call(bf16[80,512]{1,0:T(8,128)(2,1)S(1)} %get-tuple-element.20.refs_0_, bf16[80,512]{1,0:T(8,128)(2,1)S(1)} %collective-permute-done.3.refs_1_, bf16[80,512]{1,0:T(8,128)(2,1)S(1)} %collective-permute-done.4.refs_2_, ...), custom_call_target="tpu_custom_call" | custom-call | tf_op jit(solution)/shard_map/final/pallas_call | solution.py:286
Async XLA Ops:
  0.6 5.5 %collective-permute-start.2 = (bf16[32,512]{1,0:T(8,128)(2,1)}, bf16[32,512]{1,0:T(8,128)(2,1)S(1)}, u32[]{:S(2)}, u32[]{:S(2)}) collective-permute-start(bf16[32,512]{1,0:T(8,128)(2,1)} %bitcast.6), channel_id=1, source_target_pairs={{0,24},{8,16},{16,8},{24,0},{1,25},{9,17},{17,9},{25,1},{2,26},{10... | collective-permute-start | bytes 98312 | tf_op jit(solution)/shard_map/ppermute | solution.py:68
  3.1 4.2 %collective-permute-start.1 = (bf16[32,512]{1,0:T(8,128)(2,1)}, bf16[32,512]{1,0:T(8,128)(2,1)S(1)}, u32[]{:S(2)}, u32[]{:S(2)}) collective-permute-start(bf16[32,512]{1,0:T(8,128)(2,1)} %bitcast.7), channel_id=1, source_target_pairs={{0,16},{8,24},{16,0},{24,8},{1,17},{9,25},{17,1},{25,9},{2,18},{10... | collective-permute-start | bytes 98312 | tf_op jit(solution)/shard_map/ppermute | solution.py:68
  3.7 3.5 %collective-permute-start = (bf16[32,512]{1,0:T(8,128)(2,1)}, bf16[32,512]{1,0:T(8,128)(2,1)S(1)}, u32[]{:S(2)}, u32[]{:S(2)}) collective-permute-start(bf16[32,512]{1,0:T(8,128)(2,1)} %bitcast.8), channel_id=1, source_target_pairs={{0,8},{8,0},{16,24},{24,16},{1,9},{9,1},{17,25},{25,17},{2,10},{10... | collective-permute-start | bytes 98312 | tf_op jit(solution)/shard_map/ppermute | solution.py:68
  4.4 2.9 %copy-start.1 = (bf16[512,32]{0,1:T(8,128)(2,1)S(1)}, bf16[512,32]{0,1:T(8,128)(2,1)}, u32[]{:S(2)}) copy-start(bf16[512,32]{0,1:T(8,128)(2,1)} %param.9) | copy-start | bytes 98308
  7.6 14.7 %copy-start = (f32[128,128]{1,0:T(8,128)S(1)}, f32[128,128]{1,0:T(8,128)}, u32[]{:S(2)}) copy-start(f32[128,128]{1,0:T(8,128)} %cotangent.1) | copy-start | bytes 196612
  7.6 14.7 %copy-start.2 = (bf16[128,128]{1,0:T(8,128)(2,1)S(1)}, bf16[128,128]{1,0:T(8,128)(2,1)}, u32[]{:S(2)}) copy-start(bf16[128,128]{1,0:T(8,128)(2,1)} %weight.1) | copy-start | bytes 98308
  42.7 1.9 %collective-permute-start.3 = (bf16[80,512]{1,0:T(8,128)(2,1)S(1)}, bf16[80,512]{1,0:T(8,128)(2,1)S(1)}, u32[]{:S(2)}, u32[]{:S(2)}) collective-permute-start(bf16[80,512]{1,0:T(8,128)(2,1)S(1)} %get-tuple-element.21), channel_id=1, source_target_pairs={{0,8},{8,0},{16,24},{24,16},{1,9},{9,1},{17,25},{25,17},{2,10},{10... | collective-permute-start | bytes 245768 | tf_op jit(solution)/shard_map/ppermute | solution.py:68
  42.8 5.3 %collective-permute-start.4 = (bf16[80,512]{1,0:T(8,128)(2,1)S(1)}, bf16[80,512]{1,0:T(8,128)(2,1)S(1)}, u32[]{:S(2)}, u32[]{:S(2)}) collective-permute-start(bf16[80,512]{1,0:T(8,128)(2,1)S(1)} %get-tuple-element.22), channel_id=1, source_target_pairs={{0,16},{8,24},{16,0},{24,8},{1,17},{9,25},{17,1},{25,9},{2,18},{10... | collective-permute-start | bytes 245768 | tf_op jit(solution)/shard_map/ppermute | solution.py:68
  44.1 4.8 %collective-permute-start.5 = (bf16[80,512]{1,0:T(8,128)(2,1)S(1)}, bf16[80,512]{1,0:T(8,128)(2,1)S(1)}, u32[]{:S(2)}, u32[]{:S(2)}) collective-permute-start(bf16[80,512]{1,0:T(8,128)(2,1)S(1)} %get-tuple-element.23), channel_id=1, source_target_pairs={{0,24},{8,16},{16,8},{24,0},{1,25},{9,17},{17,9},{25,1},{2,26},{10... | collective-permute-start | bytes 245768 | tf_op jit(solution)/shard_map/ppermute | solution.py:68

commit v3 on v2

--- a/solution.py
+++ b/solution.py
@@ -85,19 +85,26 @@
     each(blocks, clear)
     for copy in copies:
         copy.wait()
-    scaled[...] = values_here[...].astype(f32)
+    line = lax.broadcasted_iota(jnp.int32, scaled.shape, 0)
+    scaled[...] = jnp.where(line < limit[0, 0] * lanes, values_here[...].astype(f32), 0.0)
     which = lax.broadcasted_iota(jnp.int32, (tile, tile), 0)
 
-    def add(slot, none):
+    def add(slot):
         block = col[0, 0, slot] * row_blocks + row[0, 0, slot]
-        dense = sums[block]
+        dense = jnp.zeros((tile, tile), f32)
         for lane in range(lanes):
-            line = pl.ds(slot * lanes + lane, 1)
-            dense = dense + jnp.where(which == ids_here[line, :], scaled[line, :], 0.0)
-        sums[block] = dense
+            place = pl.ds(slot * lanes + lane, 1)
+            dense = jnp.where(which == ids_here[place, :], scaled[place, :], dense)
+        sums[block] = sums[block] + dense
+
+    several = next(count for count in (4, 2, 1) if slots % count == 0)
+
+    def group(index, none):
+        for other in range(several):
+            add(index * several + other)
         return none
 
-    lax.fori_loop(0, limit[0, 0], add, 0)
+    lax.fori_loop(0, (limit[0, 0] + several - 1) // several, group, 0)
 
     def put(index):
         c, r = index // row_blocks, index % row_blocks
@@ -172,8 +179,13 @@
     return jnp.where(row == 0, high, jnp.where(row == 1, line - high, 0.0))
 
 
-def own_kernel(got, weight, bias, cotangent, act, message):
+def shares_of(size):
+    return 2 if size % 2 == 0 else 1
+
+
+def own_kernel(shares, got, weight, bias, cotangent, act, grad_out, kept, sent, bias_out, part):
     owners, hidden, own = got.shape
+    share = hidden // shares
     total = got[0].astype(f32)
     for index in range(1, owners):
         total = total + got[index].astype(f32)
@@ -184,39 +196,89 @@
     act[...] = pre * squashed
     grad = cotangent[...] * squashed * (1.0 + pre * (1.0 - squashed))
     grad = grad.astype(bf16)
-    back = dot(weight[...], grad, 1, 1).astype(bf16)
-    weight_part = (dot(high, grad) + dot(low, grad)).astype(bf16)
-    bias_part = pair_rows(jnp.sum(grad.astype(f32), axis=0, keepdims=True)).astype(bf16)
-    for index in range(owners):
-        message[index, :hidden, :] = back
-        message[index, hidden : 2 * hidden, :] = weight_part
-        message[index, 2 * hidden :, :] = bias_part
-
-
-def own_rows(got, weight, bias, cotangent):
+    grad_out[...] = grad
+    part[...] = dot(high, grad) + dot(low, grad)
+    bias_out[...] = pair_rows(jnp.sum(grad.astype(f32), axis=0, keepdims=True)).astype(bf16)
+    mine = lax.rem(lax.axis_index("row"), shares)
+    kept[...] = part[pl.ds(pl.multiple_of(mine * share, share), share), :]
+    sent[...] = part[pl.ds(pl.multiple_of((shares - 1 - mine) * share, share), share), :].astype(bf16)
+
+
+def own_rows(got, weight, bias, cotangent, shares):
     owners, hidden, own = got.shape
-    return pl.pallas_call(
-        own_kernel,
-        out_shape=(struct(cotangent.shape, f32), struct((owners, 2 * hidden + tail, own), bf16)),
+    share = hidden // shares
+    return pl.pallas_call(
+        functools.partial(own_kernel, shares),
+        out_shape=(
+            struct(cotangent.shape, f32),
+            struct(cotangent.shape, bf16),
+            struct((share, hidden), f32),
+            struct((share, hidden), bf16),
+            struct((tail, hidden), bf16),
+        ),
         in_specs=[vmem()] * 4,
-        out_specs=(vmem(), vmem()),
+        out_specs=(vmem(),) * 5,
+        scratch_shapes=[pltpu.VMEM((hidden, hidden), f32)],
         compiler_params=room(got),
         name="own_rows",
     )(got, weight, bias, cotangent)
 
 
-def backward_kernel(size, got, band, *refs):
+def turn_kernel(grad, weight, back):
+    back[...] = dot(weight[...], grad[...], 1, 1).astype(bf16)
+
+
+def turn(grad, weight):
+    own, hidden = grad.shape
+    return pl.pallas_call(
+        turn_kernel,
+        out_shape=struct((hidden, own), bf16),
+        in_specs=[vmem()] * 2,
+        out_specs=vmem(),
+        compiler_params=room(grad, weight),
+        name="turn",
+    )(grad, weight)
+
+
+def gather_kernel(shares, back, kept, got, bias, message):
+    owners, _, own = message.shape
+    hidden = back.shape[0]
+    share = kept.shape[0]
+    total = kept[...]
+    if shares > 1:
+        total = total + got[...].astype(f32)
+    total = total.astype(bf16)
+    for index in range(owners):
+        message[index, :hidden, :] = back[...]
+        message[index, hidden : hidden + share, :] = total
+        message[index, hidden + share :, :] = bias[...]
+
+
+def gather(back, kept, got, bias, shares, owners):
+    hidden, own = back.shape
+    rows = hidden + kept.shape[0] + bias.shape[0]
+    return pl.pallas_call(
+        functools.partial(gather_kernel, shares),
+        out_shape=struct((owners, rows, own), bf16),
+        in_specs=[vmem()] * 4,
+        out_specs=vmem(),
+        compiler_params=room(back),
+        name="gather",
+    )(back, kept, got, bias)
+
+
+def backward_kernel(size, share, got, band, *refs):
     messages, (kept, wide_rows, grads, packed) = refs[:size], refs[size:]
     owners, _, own = got.shape
-    hidden = kept.shape[0] * size
     width, nodes = kept.shape
+    hidden = width * size
     me = lax.axis_index("row")
-    weight_part = jnp.zeros((hidden, own), f32)
+    weight_part = jnp.zeros((share, own), f32)
     bias_part = jnp.zeros((1, own), f32)
     for index in range(owners):
         wide_rows[:, index * own : (index + 1) * own] = got[index, :hidden, :]
-        weight_part = weight_part + got[index, hidden : 2 * hidden, :].astype(f32)
-        bias_part = bias_part + jnp.sum(got[index, 2 * hidden :, :].astype(f32), axis=0, keepdims=True)
+        weight_part = weight_part + got[index, hidden : hidden + share, :].astype(f32)
+        bias_part = bias_part + jnp.sum(got[index, hidden + share :, :].astype(f32), axis=0, keepdims=True)
     many = min(wide, nodes)
 
     def piece(index):
@@ -224,71 +286,75 @@
         grads[:, place] = dot(wide_rows[...], band[place, :], 1, 1)
 
     each(nodes // many, piece)
-    per_row = nodes // own
-    for part in range(hidden // width):
-        packed[width : 2 * width, part * own : (part + 1) * own] = weight_part[part * width : (part + 1) * width]
-    packed[2 * width :, :] = jnp.zeros((tail, nodes), f32)
-    packed[2 * width :, :own] = pair_rows(bias_part)
+    split = nodes // own
+    packed[split * width : split * width + share, :] = weight_part
+    packed[split * width + share :, :] = pair_rows(bias_part)
     for step in range(size):
         slot = pl.multiple_of(partner(me, step, size) * width, width)
         block = grads[pl.ds(slot, width), :]
         if step == 0:
             kept[...] = block
-        packed[:width, :] = block
+        for index in range(split):
+            packed[index * width : (index + 1) * width, :] = block[:, index * own : (index + 1) * own]
         messages[step][...] = packed[...].astype(bf16)
 
 
-def backward(got, band, size):
-    owners, _, own = got.shape
+def backward(got, band, size, hidden):
+    owners, rows, own = got.shape
     nodes, total = band.shape
-    hidden = (got.shape[1] - tail) // 2
     width = hidden // size
-    message = struct((2 * width + tail, nodes), bf16)
-    return pl.pallas_call(
-        functools.partial(backward_kernel, size),
+    share = rows - hidden - tail
+    message = struct((width * (nodes // own) + share + tail, own), bf16)
+    return pl.pallas_call(
+        functools.partial(backward_kernel, size, share),
         out_shape=(message,) * size + (struct((width, nodes), f32),),
         in_specs=[vmem()] * 2,
         out_specs=(vmem(),) * (size + 1),
         scratch_shapes=[
             pltpu.VMEM((hidden, total), bf16),
             pltpu.VMEM((hidden, nodes), f32),
-            pltpu.VMEM((2 * width + tail, nodes), f32),
+            pltpu.VMEM(message.shape, f32),
         ],
         compiler_params=room(band, got),
         name="backward",
     )(got, band)
 
 
-def final_kernel(size, shrink, *refs):
+def final_kernel(size, shares, shrink, *refs):
     messages, (kept, features, weight, bias, slots) = refs[:size], refs[size:]
     width, nodes = kept.shape
-    hidden = weight.shape[0]
+    share = weight.shape[0] // shares
+    own = messages[0].shape[1]
+    split = nodes // own
     me = lax.axis_index("row")
-    total = kept[...]
     for step, message in enumerate(messages):
-        whole = message[...].astype(f32)
-        if step > 0:
-            total = total + whole[:width]
-        slots[source(me, step, size)] = whole[width:]
-    features[...] = total.astype(bf16)
-    summed = slots[0]
-    for index in range(1, size):
-        summed = summed + slots[index]
-    summed = summed * shrink
-    for part in range(hidden // width):
-        weight[part * width : (part + 1) * width, :] = summed[:width, part * hidden : (part + 1) * hidden]
-    bias[...] = summed[width : width + 1, :hidden] + summed[width + 1 : width + 2, :hidden]
-
-
-def final(messages, kept, hidden, shrink):
+        slots[source(me, step, size)] = message[split * width :, :].astype(f32)
+    for index in range(split):
+        place = slice(index * own, (index + 1) * own)
+        total = kept[:, place]
+        for message in messages[1:]:
+            total = total + message[index * width : (index + 1) * width, :].astype(f32)
+        features[:, place] = total.astype(bf16)
+    bias_part = jnp.zeros((tail, own), f32)
+    for half in range(shares):
+        total = jnp.zeros((share, own), f32)
+        for index in range(half, size, shares):
+            total = total + slots[index, :share, :]
+            bias_part = bias_part + slots[index, share:, :]
+        weight[half * share : (half + 1) * share, :] = total * shrink
+    bias[...] = jnp.sum(bias_part, axis=0, keepdims=True) * shrink
+
+
+def final(messages, kept, hidden, shares, shrink):
     width, nodes = kept.shape
     size = len(messages)
-    return pl.pallas_call(
-        functools.partial(final_kernel, size, shrink),
+    rows, own = messages[0].shape
+    return pl.pallas_call(
+        functools.partial(final_kernel, size, shares, shrink),
         out_shape=(struct((width, nodes), bf16), struct((hidden, hidden), f32), struct((1, hidden), f32)),
         in_specs=[vmem()] * (size + 1),
         out_specs=(vmem(),) * 3,
-        scratch_shapes=[pltpu.VMEM((size, width + tail, nodes), f32)],
+        scratch_shapes=[pltpu.VMEM((size, hidden // shares + tail, own), f32)],
         compiler_params=room(*messages),
         name="final",
     )(*messages, kept)
@@ -318,12 +384,17 @@
     )
     sums = forward(parts, band, owners)
     sums = lax.all_to_all(sums, "col", 0, 0, tiled=True)
-    activations, message = own_rows(sums, weight, bias, cotangent)
+    shares = shares_of(size)
+    activations, grad, kept, sent, bias_part = own_rows(sums, weight, bias, cotangent, shares)
+    got = exchange(sent, "row", 1) if shares > 1 else sent
+    message = gather(turn(grad, weight), kept, got, bias_part, shares, owners)
     message = lax.all_to_all(message, "col", 0, 0, tiled=True)
-    *messages, kept = backward(message, band, size)
+    *messages, kept = backward(message, band, size, hidden)
     messages = [messages[0]] + [exchange(messages[step], "row", step) for step in range(1, size)]
     node_count = cotangent.shape[0] * size * owners
-    grad_features, grad_weight, grad_bias = final(messages, kept, hidden, float(node_count) ** (-0.5))
+    grad_features, grad_weight, grad_bias = final(
+        messages, kept, hidden, shares, float(node_count) ** (-0.5)
+    )
     return (activations, grad_features.T, grad_weight, grad_bias.reshape(hidden))
 
 

time: 49.9 us -> 47.4 us (0.950)
  blocking collectives: 33.7 us -> 31 us
    all_to_all x1, blocking collectives: 19 us -> 16.3 us  [shards(): message = lax.all_to_all(message, 'col', 0, 0, tiled=True)]
    ppermute x6 -> x7, waiting for transfers between devices: 5.42 us -> 5.68 us  [exchange(): lax.ppermute(value, axis, [(i, partner(i, step, size)) for i in range(siz...]
    pallas_call x3 -> x5, Pallas kernels: 2.07 us -> 2.25 us  [the longest x1 0.9 us: own_rows(): pl.pallas_call(functools.partial(own_kernel, shares), out_shape=(struct(c...]
    ppermute x6 -> x7, starting transfers between devices: 5.08 us -> 5.09 us  [exchange(): lax.ppermute(value, axis, [(i, partner(i, step, size)) for i in range(siz...]
  transfers between devices with their start and end apart: 6 -> 7, of which waited for: 3 -> 4; matrix products, arithmetic and copies ran while one was open for 0% -> 0% of each run, Pallas kernels for 3% -> 3%
where the time goes in v3:
time: 47.4 us; the launch traced here: 47.1 us
  blocking collectives  31 us (65%)
  waiting for transfers between devices  5.68 us (12%)
  starting transfers between devices  5.09 us (11%)
  Pallas kernels  4.02 us (8%)
  between operations  1.36 us (3%)
    all_to_all x1, blocking collectives, shards(): message = lax.all_to_all(message, 'col', 0, 0, tiled=True)  16.3 us
    all_to_all x1, blocking collectives, shards(): sums = lax.all_to_all(sums, 'col', 0, 0, tiled=True)  14.6 us
    ppermute x7, waiting for transfers between devices, exchange(): lax.ppermute(value, axis, [(i, partner(i, step, size)) for i in range(siz...  5.68 us
    ppermute x7, starting transfers between devices, exchange(): lax.ppermute(value, axis, [(i, partner(i, step, size)) for i in range(siz...  5.09 us
    pallas_call x1, Pallas kernels, make_band(): pl.pallas_call(band_kernel, out_shape=(out, struct(bias.shape, f32)), in_...  1.45 us
  transfers between devices with their start and end apart: 7, of which 4 were waited for; matrix products, arithmetic and copies ran while one was open for 0% of the time, Pallas kernels for 3%

profile of v3, /device:TPU:0, one launch (start us, length us, event | category | flops | bytes accessed | tf_op | source)
XLA Modules:
  0.0 47.1 jit_solution(585621568586646527)
XLA Ops:
  0.6 2.5 %collective-permute-start.2 = (bf16[32,512]{1,0:T(8,128)(2,1)}, bf16[32,512]{1,0:T(8,128)(2,1)S(1)}, u32[]{:S(2)}, u32[]{:S(2)}) collective-permute-start(bf16[32,512]{1,0:T(8,128)(2,1)} %bitcast.6), channel_id=1, source_target_pairs={{0,24},{8,16},{16,8},{24,0},{1,25},{9,17},{17,9},{25,1},{2,26},{10... | collective-permute-start | bytes 98312 | tf_op jit(solution)/shard_map/ppermute | solution.py:68
  3.1 0.6 %collective-permute-start.1 = (bf16[32,512]{1,0:T(8,128)(2,1)}, bf16[32,512]{1,0:T(8,128)(2,1)S(1)}, u32[]{:S(2)}, u32[]{:S(2)}) collective-permute-start(bf16[32,512]{1,0:T(8,128)(2,1)} %bitcast.7), channel_id=1, source_target_pairs={{0,16},{8,24},{16,0},{24,8},{1,17},{9,25},{17,1},{25,9},{2,18},{10... | collective-permute-start | bytes 98312 | tf_op jit(solution)/shard_map/ppermute | solution.py:68
  3.7 0.0 collective-permute-start
  4.4 0.0 copy-start.2
  4.4 1.5 %band.1 = (bf16[512,1024]{1,0:T(8,128)(2,1)S(1)}, f32[1,128]{1,0:T(1,128)S(1)}) custom-call(s32[1,1]{1,0:T(1,128)S(6)} %copy.13.limit, s32[1,1,128]{2,1,0:T(1,128)} %rows.1, s32[1,1,128]{2,1,0:T(1,128)} %cols.1, s32[256,128]{1,0:T(8,128)} %bitcast.10, bf16[256,128]{1,0:T(8,128)(2,1)} %bitcast.11, f32[1,128]{1,0:T(1,128)} %bitcast.12), custom_call_target="tpu_custom_call" | custom-call | flops 33554432 | bytes 8388608 | tf_op jit(solution)/shard_map/band/pallas_call | solution.py:124
  5.9 0.0 collective-permute-done.2.refs_3_
  5.9 1.4 %collective-permute-done.1.refs_2_ = bf16[32,512]{1,0:T(8,128)(2,1)S(1)} collective-permute-done((bf16[32,512]{1,0:T(8,128)(2,1)}, bf16[32,512]{1,0:T(8,128)(2,1)S(1)}, u32[]{:S(2)}, u32[]{:S(2)}) %collective-permute-start.1) | collective-permute-done | bytes 32800 | tf_op jit(solution)/shard_map/ppermute | solution.py:68
  7.3 0.0 collective-permute-done.refs_1_
  7.3 0.0 copy-done.2
  7.3 0.3 forward.1
  7.6 0.0 copy-start
  7.6 0.0 copy-start.1
  7.6 14.6 %all_to_all.10.got = bf16[8,128,128]{2,1,0:T(8,128)(2,1)S(1)} all-to-all(bf16[8,128,128]{2,1,0:T(8,128)(2,1)S(1)} %forward.1), channel_id=1, replica_groups=mesh['row'=4,'col'=8] {'col'}, dimensions={0} | all-to-all | bytes 524288 | tf_op jit(solution)/shard_map/all_to_all | solution.py:386
  22.3 0.0 copy-done
  22.3 0.0 copy-done.1
  22.3 0.9 %own_rows.1 = (f32[128,128]{1,0:T(8,128)}, bf16[128,128]{1,0:T(8,128)(2,1)S(1)}, f32[64,128]{1,0:T(8,128)S(1)}, bf16[64,128]{1,0:T(8,128)(2,1)S(1)}, bf16[16,128]{1,0:T(8,128)(2,1)S(1)}) custom-call(bf16[8,128,128]{2,1,0:T(8,128)(2,1)S(1)} %all_to_all.10.got, bf16[128,128]{1,0:T(8,128)(2,1)S(1)} %copy-done, f32[1,128]{1,0:T(1,128)S(1)} %get-tuple-element.20.bias, ...), custom_call_target="tpu_custom_call" | custom-call | tf_op jit(solution)/shard_map/own_rows/pallas_call | solution.py:210
  23.2 0.0 collective-permute-start.3
  23.2 0.1 turn.1.back
  23.3 1.1 %collective-permute-done.3.got = bf16[64,128]{1,0:T(8,128)(2,1)S(1)} collective-permute-done((bf16[64,128]{1,0:T(8,128)(2,1)S(1)}, bf16[64,128]{1,0:T(8,128)(2,1)S(1)}, u32[]{:S(2)}, u32[]{:S(2)}) %collective-permute-start.3) | collective-permute-done | bytes 16416 | tf_op jit(solution)/shard_map/ppermute | solution.py:68
  24.4 16.3 %all_to_all.11.got = bf16[8,208,128]{2,1,0:T(8,128)(2,1)S(1)} all-to-all(bf16[8,208,128]{2,1,0:T(8,128)(2,1)S(1)} %gather.1), channel_id=1, replica_groups=mesh['row'=4,'col'=8] {'col'}, dimensions={0} | all-to-all | bytes 851968 | tf_op jit(solution)/shard_map/all_to_all | solution.py:391
  40.8 0.5 %backward.1 = (bf16[208,128]{1,0:T(8,128)(2,1)S(1)}, bf16[208,128]{1,0:T(8,128)(2,1)S(1)}, bf16[208,128]{1,0:T(8,128)(2,1)S(1)}, bf16[208,128]{1,0:T(8,128)(2,1)S(1)}, f32[32,512]{1,0:T(8,128)S(1)}) custom-call(bf16[8,208,128]{2,1,0:T(8,128)(2,1)S(1)} %all_to_all.11.got, bf16[512,1024]{1,0:T(8,128)(2,1)S(1)} %get-tuple-element.19.refs_4_.band), custom_call_target="tpu_custom_call" | custom-call | tf_op jit(solution)/shard_map/backward/pallas_call | solution.py:308
  41.3 0.1 collective-permute-start.4
  41.3 1.3 %collective-permute-start.5 = (bf16[208,128]{1,0:T(8,128)(2,1)S(1)}, bf16[208,128]{1,0:T(8,128)(2,1)S(1)}, u32[]{:S(2)}, u32[]{:S(2)}) collective-permute-start(bf16[208,128]{1,0:T(8,128)(2,1)S(1)} %get-tuple-element.28), channel_id=1, source_target_pairs={{0,16},{8,24},{16,0},{24,8},{1,17},{9,25},{17,1},{25,9},{2,18},{10... | collective-permute-start | bytes 159752 | tf_op jit(solution)/shard_map/ppermute | solution.py:68
  42.7 0.5 %collective-permute-start.6 = (bf16[208,128]{1,0:T(8,128)(2,1)S(1)}, bf16[208,128]{1,0:T(8,128)(2,1)S(1)}, u32[]{:S(2)}, u32[]{:S(2)}) collective-permute-start(bf16[208,128]{1,0:T(8,128)(2,1)S(1)} %get-tuple-element.29), channel_id=1, source_target_pairs={{0,24},{8,16},{16,8},{24,0},{1,25},{9,17},{17,9},{25,1},{2,26},{10... | collective-permute-start | bytes 159752 | tf_op jit(solution)/shard_map/ppermute | solution.py:68
  43.2 0.0 collective-permute-done.4.refs_1_
  43.2 2.4 %collective-permute-done.5.refs_2_ = bf16[208,128]{1,0:T(8,128)(2,1)S(1)} collective-permute-done((bf16[208,128]{1,0:T(8,128)(2,1)S(1)}, bf16[208,128]{1,0:T(8,128)(2,1)S(1)}, u32[]{:S(2)}, u32[]{:S(2)}) %collective-permute-start.5) | collective-permute-done | bytes 53280 | tf_op jit(solution)/shard_map/ppermute | solution.py:68
  45.6 0.9 %collective-permute-done.6.refs_3_ = bf16[208,128]{1,0:T(8,128)(2,1)S(1)} collective-permute-done((bf16[208,128]{1,0:T(8,128)(2,1)S(1)}, bf16[208,128]{1,0:T(8,128)(2,1)S(1)}, u32[]{:S(2)}, u32[]{:S(2)}) %collective-permute-start.6) | collective-permute-done | bytes 53280 | tf_op jit(solution)/shard_map/ppermute | solution.py:68
  46.5 0.7 %final.1 = (bf16[32,512]{1,0:T(8,128)(2,1)}, f32[128,128]{1,0:T(8,128)}, f32[1,128]{1,0:T(1,128)}) custom-call(bf16[208,128]{1,0:T(8,128)(2,1)S(1)} %get-tuple-element.26.refs_0_, bf16[208,128]{1,0:T(8,128)(2,1)S(1)} %collective-permute-done.4.refs_1_, bf16[208,128]{1,0:T(8,128)(2,1)S(1)} %collective-permute-done.5.refs_2_, ...), custom_call_target="tpu_custom_call" | custom-call | tf_op jit(solution)/shard_map/final/pallas_call | solution.py:352
  (1 shorter events, 0.0 us)
Async XLA Ops:
  0.6 5.3 %collective-permute-start.2 = (bf16[32,512]{1,0:T(8,128)(2,1)}, bf16[32,512]{1,0:T(8,128)(2,1)S(1)}, u32[]{:S(2)}, u32[]{:S(2)}) collective-permute-start(bf16[32,512]{1,0:T(8,128)(2,1)} %bitcast.6), channel_id=1, source_target_pairs={{0,24},{8,16},{16,8},{24,0},{1,25},{9,17},{17,9},{25,1},{2,26},{10... | collective-permute-start | bytes 98312 | tf_op jit(solution)/shard_map/ppermute | solution.py:68
  3.1 4.2 %collective-permute-start.1 = (bf16[32,512]{1,0:T(8,128)(2,1)}, bf16[32,512]{1,0:T(8,128)(2,1)S(1)}, u32[]{:S(2)}, u32[]{:S(2)}) collective-permute-start(bf16[32,512]{1,0:T(8,128)(2,1)} %bitcast.7), channel_id=1, source_target_pairs={{0,16},{8,24},{16,0},{24,8},{1,17},{9,25},{17,1},{25,9},{2,18},{10... | collective-permute-start | bytes 98312 | tf_op jit(solution)/shard_map/ppermute | solution.py:68
  3.7 3.5 %collective-permute-start = (bf16[32,512]{1,0:T(8,128)(2,1)}, bf16[32,512]{1,0:T(8,128)(2,1)S(1)}, u32[]{:S(2)}, u32[]{:S(2)}) collective-permute-start(bf16[32,512]{1,0:T(8,128)(2,1)} %bitcast.8), channel_id=1, source_target_pairs={{0,8},{8,0},{16,24},{24,16},{1,9},{9,1},{17,25},{25,17},{2,10},{10... | collective-permute-start | bytes 98312 | tf_op jit(solution)/shard_map/ppermute | solution.py:68
  4.4 2.9 %copy-start.2 = (bf16[512,32]{0,1:T(8,128)(2,1)S(1)}, bf16[512,32]{0,1:T(8,128)(2,1)}, u32[]{:S(2)}) copy-start(bf16[512,32]{0,1:T(8,128)(2,1)} %param.9) | copy-start | bytes 98308
  7.6 14.7 %copy-start = (bf16[128,128]{1,0:T(8,128)(2,1)S(1)}, bf16[128,128]{1,0:T(8,128)(2,1)}, u32[]{:S(2)}) copy-start(bf16[128,128]{1,0:T(8,128)(2,1)} %weight.3) | copy-start | bytes 98308
  7.6 14.7 %copy-start.1 = (f32[128,128]{1,0:T(8,128)S(1)}, f32[128,128]{1,0:T(8,128)}, u32[]{:S(2)}) copy-start(f32[128,128]{1,0:T(8,128)} %cotangent.1) | copy-start | bytes 196612
  23.2 1.2 %collective-permute-start.3 = (bf16[64,128]{1,0:T(8,128)(2,1)S(1)}, bf16[64,128]{1,0:T(8,128)(2,1)S(1)}, u32[]{:S(2)}, u32[]{:S(2)}) collective-permute-start(bf16[64,128]{1,0:T(8,128)(2,1)S(1)} %get-tuple-element.24), channel_id=1, source_target_pairs={{0,8},{8,0},{16,24},{24,16},{1,9},{9,1},{17,25},{25,17},{2,10},{10... | collective-permute-start | bytes 49160 | tf_op jit(solution)/shard_map/ppermute | solution.py:68
  41.3 1.9 %collective-permute-start.4 = (bf16[208,128]{1,0:T(8,128)(2,1)S(1)}, bf16[208,128]{1,0:T(8,128)(2,1)S(1)}, u32[]{:S(2)}, u32[]{:S(2)}) collective-permute-start(bf16[208,128]{1,0:T(8,128)(2,1)S(1)} %get-tuple-element.27), channel_id=1, source_target_pairs={{0,8},{8,0},{16,24},{24,16},{1,9},{9,1},{17,25},{25,17},{2,10},{10... | collective-permute-start | bytes 159752 | tf_op jit(solution)/shard_map/ppermute | solution.py:68
  41.3 4.2 %collective-permute-start.5 = (bf16[208,128]{1,0:T(8,128)(2,1)S(1)}, bf16[208,128]{1,0:T(8,128)(2,1)S(1)}, u32[]{:S(2)}, u32[]{:S(2)}) collective-permute-start(bf16[208,128]{1,0:T(8,128)(2,1)S(1)} %get-tuple-element.28), channel_id=1, source_target_pairs={{0,16},{8,24},{16,0},{24,8},{1,17},{9,25},{17,1},{25,9},{2,18},{10... | collective-permute-start | bytes 159752 | tf_op jit(solution)/shard_map/ppermute | solution.py:68
  42.7 3.8 %collective-permute-start.6 = (bf16[208,128]{1,0:T(8,128)(2,1)S(1)}, bf16[208,128]{1,0:T(8,128)(2,1)S(1)}, u32[]{:S(2)}, u32[]{:S(2)}) collective-permute-start(bf16[208,128]{1,0:T(8,128)(2,1)S(1)} %get-tuple-element.29), channel_id=1, source_target_pairs={{0,24},{8,16},{16,8},{24,0},{1,25},{9,17},{17,9},{25,1},{2,26},{10... | collective-permute-start | bytes 159752 | tf_op jit(solution)/shard_map/ppermute | solution.py:68

commit v4 on v3

--- a/solution.py
+++ b/solution.py
@@ -183,7 +183,7 @@
     return 2 if size % 2 == 0 else 1
 
 
-def own_kernel(shares, got, weight, bias, cotangent, act, grad_out, kept, sent, bias_out, part):
+def own_kernel(shares, got, weight, bias, cotangent, pre_out, grad_out, kept, sent, part):
     owners, hidden, own = got.shape
     share = hidden // shares
     total = got[0].astype(f32)
@@ -192,13 +192,12 @@
     high = total.astype(bf16)
     low = (total - high.astype(f32)).astype(bf16)
     pre = dot(high, weight[...], 0, 0) + dot(low, weight[...], 0, 0) + bias[...]
+    pre_out[...] = pre
     squashed = jax.nn.sigmoid(pre)
-    act[...] = pre * squashed
     grad = cotangent[...] * squashed * (1.0 + pre * (1.0 - squashed))
     grad = grad.astype(bf16)
     grad_out[...] = grad
     part[...] = dot(high, grad) + dot(low, grad)
-    bias_out[...] = pair_rows(jnp.sum(grad.astype(f32), axis=0, keepdims=True)).astype(bf16)
     mine = lax.rem(lax.axis_index("row"), shares)
     kept[...] = part[pl.ds(pl.multiple_of(mine * share, share), share), :]
     sent[...] = part[pl.ds(pl.multiple_of((shares - 1 - mine) * share, share), share), :].astype(bf16)
@@ -214,110 +213,104 @@
             struct(cotangent.shape, bf16),
             struct((share, hidden), f32),
             struct((share, hidden), bf16),
-            struct((tail, hidden), bf16),
         ),
         in_specs=[vmem()] * 4,
-        out_specs=(vmem(),) * 5,
+        out_specs=(vmem(),) * 4,
         scratch_shapes=[pltpu.VMEM((hidden, hidden), f32)],
         compiler_params=room(got),
         name="own_rows",
     )(got, weight, bias, cotangent)
 
 
-def turn_kernel(grad, weight, back):
-    back[...] = dot(weight[...], grad[...], 1, 1).astype(bf16)
-
-
-def turn(grad, weight):
-    own, hidden = grad.shape
-    return pl.pallas_call(
-        turn_kernel,
-        out_shape=struct((hidden, own), bf16),
-        in_specs=[vmem()] * 2,
+def activate_kernel(pre, act):
+    act[...] = pre[...] * jax.nn.sigmoid(pre[...])
+
+
+def activate(pre):
+    return pl.pallas_call(
+        activate_kernel,
+        out_shape=struct(pre.shape, f32),
+        in_specs=[vmem()],
         out_specs=vmem(),
-        compiler_params=room(grad, weight),
-        name="turn",
-    )(grad, weight)
-
-
-def gather_kernel(shares, back, kept, got, bias, message):
-    owners, _, own = message.shape
-    hidden = back.shape[0]
-    share = kept.shape[0]
+        compiler_params=room(pre),
+        name="activate",
+    )(pre)
+
+
+def gather_kernel(shares, grad, kept, got, message):
+    owners = message.shape[0]
+    own = grad.shape[0]
     total = kept[...]
     if shares > 1:
         total = total + got[...].astype(f32)
     total = total.astype(bf16)
     for index in range(owners):
-        message[index, :hidden, :] = back[...]
-        message[index, hidden : hidden + share, :] = total
-        message[index, hidden + share :, :] = bias[...]
-
-
-def gather(back, kept, got, bias, shares, owners):
-    hidden, own = back.shape
-    rows = hidden + kept.shape[0] + bias.shape[0]
+        message[index, :own, :] = grad[...]
+        message[index, own:, :] = total
+
+
+def gather(grad, kept, got, shares, owners):
+    own, hidden = grad.shape
     return pl.pallas_call(
         functools.partial(gather_kernel, shares),
-        out_shape=struct((owners, rows, own), bf16),
-        in_specs=[vmem()] * 4,
+        out_shape=struct((owners, own + kept.shape[0], hidden), bf16),
+        in_specs=[vmem()] * 3,
         out_specs=vmem(),
-        compiler_params=room(back),
+        compiler_params=room(grad),
         name="gather",
-    )(back, kept, got, bias)
-
-
-def backward_kernel(size, share, got, band, *refs):
-    messages, (kept, wide_rows, grads, packed) = refs[:size], refs[size:]
-    owners, _, own = got.shape
+    )(grad, kept, got)
+
+
+def backward_kernel(size, own, got, weight, band, *refs):
+    messages, (kept, rows, back, grads, packed) = refs[:size], refs[size:]
+    owners, lines, hidden = got.shape
+    share = lines - own
     width, nodes = kept.shape
-    hidden = width * size
     me = lax.axis_index("row")
-    weight_part = jnp.zeros((share, own), f32)
-    bias_part = jnp.zeros((1, own), f32)
+    weight_part = jnp.zeros((share, hidden), f32)
     for index in range(owners):
-        wide_rows[:, index * own : (index + 1) * own] = got[index, :hidden, :]
-        weight_part = weight_part + got[index, hidden : hidden + share, :].astype(f32)
-        bias_part = bias_part + jnp.sum(got[index, hidden + share :, :].astype(f32), axis=0, keepdims=True)
+        rows[index * own : (index + 1) * own, :] = got[index, :own, :]
+        weight_part = weight_part + got[index, own:, :].astype(f32)
+    back[...] = dot(weight[...], rows[...], 1, 1).astype(bf16)
     many = min(wide, nodes)
 
     def piece(index):
         place = pl.ds(start_of(index, many), many)
-        grads[:, place] = dot(wide_rows[...], band[place, :], 1, 1)
+        grads[:, place] = dot(back[...], band[place, :], 1, 1)
 
     each(nodes // many, piece)
-    split = nodes // own
+    split = nodes // hidden
     packed[split * width : split * width + share, :] = weight_part
-    packed[split * width + share :, :] = pair_rows(bias_part)
+    packed[split * width + share :, :] = pair_rows(jnp.sum(rows[...].astype(f32), axis=0, keepdims=True))
     for step in range(size):
         slot = pl.multiple_of(partner(me, step, size) * width, width)
         block = grads[pl.ds(slot, width), :]
         if step == 0:
             kept[...] = block
         for index in range(split):
-            packed[index * width : (index + 1) * width, :] = block[:, index * own : (index + 1) * own]
+            packed[index * width : (index + 1) * width, :] = block[:, index * hidden : (index + 1) * hidden]
         messages[step][...] = packed[...].astype(bf16)
 
 
-def backward(got, band, size, hidden):
-    owners, rows, own = got.shape
+def backward(got, weight, band, size, own):
+    owners, lines, hidden = got.shape
     nodes, total = band.shape
     width = hidden // size
-    share = rows - hidden - tail
-    message = struct((width * (nodes // own) + share + tail, own), bf16)
-    return pl.pallas_call(
-        functools.partial(backward_kernel, size, share),
+    message = struct((width * (nodes // hidden) + lines - own + tail, hidden), bf16)
+    return pl.pallas_call(
+        functools.partial(backward_kernel, size, own),
         out_shape=(message,) * size + (struct((width, nodes), f32),),
-        in_specs=[vmem()] * 2,
+        in_specs=[vmem()] * 3,
         out_specs=(vmem(),) * (size + 1),
         scratch_shapes=[
+            pltpu.VMEM((total, hidden), bf16),
             pltpu.VMEM((hidden, total), bf16),
             pltpu.VMEM((hidden, nodes), f32),
             pltpu.VMEM(message.shape, f32),
         ],
         compiler_params=room(band, got),
         name="backward",
-    )(got, band)
+    )(got, weight, band)
 
 
 def final_kernel(size, shares, shrink, *refs):
@@ -385,11 +378,12 @@
     sums = forward(parts, band, owners)
     sums = lax.all_to_all(sums, "col", 0, 0, tiled=True)
     shares = shares_of(size)
-    activations, grad, kept, sent, bias_part = own_rows(sums, weight, bias, cotangent, shares)
+    pre, grad, kept, sent = own_rows(sums, weight, bias, cotangent, shares)
     got = exchange(sent, "row", 1) if shares > 1 else sent
-    message = gather(turn(grad, weight), kept, got, bias_part, shares, owners)
+    activations = activate(pre)
+    message = gather(grad, kept, got, shares, owners)
     message = lax.all_to_all(message, "col", 0, 0, tiled=True)
-    *messages, kept = backward(message, band, size, hidden)
+    *messages, kept = backward(message, weight, band, size, cotangent.shape[0])
     messages = [messages[0]] + [exchange(messages[step], "row", step) for step in range(1, size)]
     node_count = cotangent.shape[0] * size * owners
     grad_features, grad_weight, grad_bias = final(

time: 47.4 us -> 46.5 us (0.981)
  blocking collectives: 31 us -> 30.4 us
  waiting for transfers between devices: 5.68 us -> 5.11 us
    pallas_call x2, Pallas kernels: 0.64 us -> 1.25 us  [the longest x1 0.65 us: activate(): pl.pallas_call(activate_kernel, out_shape=struct(pre.shape, f32), in_spec...]
    ppermute x7, waiting for transfers between devices: 5.68 us -> 5.11 us  [exchange(): lax.ppermute(value, axis, [(i, partner(i, step, size)) for i in range(siz...]
    all_to_all x1, blocking collectives: 16.3 us -> 15.8 us  [shards(): message = lax.all_to_all(message, 'col', 0, 0, tiled=True)]
    pallas_call x1, Pallas kernels: 0.9 us -> 0.41 us  [own_rows(): pl.pallas_call(functools.partial(own_kernel, shares), out_shape=(struct(c...]
  transfers between devices with their start and end apart: 7 -> 7, of which waited for: 4 -> 4; matrix products, arithmetic and copies ran while one was open for 0% -> 0% of each run, Pallas kernels for 3% -> 5%
where the time goes in v4:
time: 46.5 us; the launch traced here: 46.2 us
  blocking collectives  30.4 us (65%)
  starting transfers between devices  5.15 us (11%)
  waiting for transfers between devices  5.11 us (11%)
  Pallas kernels  4.19 us (9%)
  between operations  1.37 us (3%)
    all_to_all x1, blocking collectives, shards(): message = lax.all_to_all(message, 'col', 0, 0, tiled=True)  15.8 us
    all_to_all x1, blocking collectives, shards(): sums = lax.all_to_all(sums, 'col', 0, 0, tiled=True)  14.6 us
    ppermute x7, starting transfers between devices, exchange(): lax.ppermute(value, axis, [(i, partner(i, step, size)) for i in range(siz...  5.15 us
    ppermute x7, waiting for transfers between devices, exchange(): lax.ppermute(value, axis, [(i, partner(i, step, size)) for i in range(siz...  5.11 us
    pallas_call x1, Pallas kernels, make_band(): pl.pallas_call(band_kernel, out_shape=(out, struct(bias.shape, f32)), in_...  1.5 us
  transfers between devices with their start and end apart: 7, of which 4 were waited for; matrix products, arithmetic and copies ran while one was open for 0% of the time, Pallas kernels for 5%

profile of v4, /device:TPU:0, one launch (start us, length us, event | category | flops | bytes accessed | tf_op | source)
XLA Modules:
  0.0 46.2 jit_solution(15688771700545547364)
XLA Ops:
  0.6 2.5 %collective-permute-start.2 = (bf16[32,512]{1,0:T(8,128)(2,1)}, bf16[32,512]{1,0:T(8,128)(2,1)S(1)}, u32[]{:S(2)}, u32[]{:S(2)}) collective-permute-start(bf16[32,512]{1,0:T(8,128)(2,1)} %bitcast.6), channel_id=1, source_target_pairs={{0,24},{8,16},{16,8},{24,0},{1,25},{9,17},{17,9},{25,1},{2,26},{10... | collective-permute-start | bytes 98312 | tf_op jit(solution)/shard_map/ppermute | solution.py:68
  3.1 0.6 %collective-permute-start.1 = (bf16[32,512]{1,0:T(8,128)(2,1)}, bf16[32,512]{1,0:T(8,128)(2,1)S(1)}, u32[]{:S(2)}, u32[]{:S(2)}) collective-permute-start(bf16[32,512]{1,0:T(8,128)(2,1)} %bitcast.7), channel_id=1, source_target_pairs={{0,16},{8,24},{16,0},{24,8},{1,17},{9,25},{17,1},{25,9},{2,18},{10... | collective-permute-start | bytes 98312 | tf_op jit(solution)/shard_map/ppermute | solution.py:68
  3.7 0.0 collective-permute-start
  4.4 0.0 copy-start.2
  4.4 1.5 %band.1 = (bf16[512,1024]{1,0:T(8,128)(2,1)S(1)}, f32[1,128]{1,0:T(1,128)S(1)}) custom-call(s32[1,1]{1,0:T(1,128)S(6)} %copy.13.limit, s32[1,1,128]{2,1,0:T(1,128)} %rows.1, s32[1,1,128]{2,1,0:T(1,128)} %cols.1, s32[256,128]{1,0:T(8,128)} %bitcast.10, bf16[256,128]{1,0:T(8,128)(2,1)} %bitcast.11, f32[1,128]{1,0:T(1,128)} %bitcast.12), custom_call_target="tpu_custom_call" | custom-call | flops 33554432 | bytes 8388608 | tf_op jit(solution)/shard_map/band/pallas_call | solution.py:124
  6.0 0.0 collective-permute-done.2.refs_3_
  6.0 1.3 %collective-permute-done.1.refs_2_ = bf16[32,512]{1,0:T(8,128)(2,1)S(1)} collective-permute-done((bf16[32,512]{1,0:T(8,128)(2,1)}, bf16[32,512]{1,0:T(8,128)(2,1)S(1)}, u32[]{:S(2)}, u32[]{:S(2)}) %collective-permute-start.1) | collective-permute-done | bytes 32800 | tf_op jit(solution)/shard_map/ppermute | solution.py:68
  7.3 0.0 collective-permute-done.refs_1_
  7.3 0.0 copy-done.2
  7.3 0.3 forward.1
  7.6 0.0 copy-start
  7.6 0.0 copy-start.1
  7.6 14.6 %all_to_all.10.got = bf16[8,128,128]{2,1,0:T(8,128)(2,1)S(1)} all-to-all(bf16[8,128,128]{2,1,0:T(8,128)(2,1)S(1)} %forward.1), channel_id=1, replica_groups=mesh['row'=4,'col'=8] {'col'}, dimensions={0} | all-to-all | bytes 524288 | tf_op jit(solution)/shard_map/all_to_all | solution.py:379
  22.3 0.0 copy-done
  22.3 0.0 copy-done.1
  22.3 0.4 own_rows.1
  22.7 0.1 collective-permute-start.3
  22.8 1.2 %collective-permute-done.3.got = bf16[64,128]{1,0:T(8,128)(2,1)S(1)} collective-permute-done((bf16[64,128]{1,0:T(8,128)(2,1)S(1)}, bf16[64,128]{1,0:T(8,128)(2,1)S(1)}, u32[]{:S(2)}, u32[]{:S(2)}) %collective-permute-start.3) | collective-permute-done | bytes 16416 | tf_op jit(solution)/shard_map/ppermute | solution.py:68
  24.0 15.8 %all_to_all.11.got = bf16[8,192,128]{2,1,0:T(8,128)(2,1)S(1)} all-to-all(bf16[8,192,128]{2,1,0:T(8,128)(2,1)S(1)} %gather.1), channel_id=1, replica_groups=mesh['row'=4,'col'=8] {'col'}, dimensions={0} | all-to-all | bytes 786432 | tf_op jit(solution)/shard_map/all_to_all | solution.py:385
  39.8 0.6 %backward.1 = (bf16[208,128]{1,0:T(8,128)(2,1)S(1)}, bf16[208,128]{1,0:T(8,128)(2,1)S(1)}, bf16[208,128]{1,0:T(8,128)(2,1)S(1)}, bf16[208,128]{1,0:T(8,128)(2,1)S(1)}, f32[32,512]{1,0:T(8,128)S(1)}) custom-call(bf16[8,192,128]{2,1,0:T(8,128)(2,1)S(1)} %all_to_all.11.got, bf16[128,128]{1,0:T(8,128)(2,1)S(1)} %copy-done, ...), custom_call_target="tpu_custom_call" | custom-call | tf_op jit(solution)/shard_map/backward/pallas_call | solution.py:300
  40.4 0.1 collective-permute-start.4
  40.5 1.3 %collective-permute-start.5 = (bf16[208,128]{1,0:T(8,128)(2,1)S(1)}, bf16[208,128]{1,0:T(8,128)(2,1)S(1)}, u32[]{:S(2)}, u32[]{:S(2)}) collective-permute-start(bf16[208,128]{1,0:T(8,128)(2,1)S(1)} %get-tuple-element.26), channel_id=1, source_target_pairs={{0,16},{8,24},{16,0},{24,8},{1,17},{9,25},{17,1},{25,9},{2,18},{10... | collective-permute-start | bytes 159752 | tf_op jit(solution)/shard_map/ppermute | solution.py:68
  41.8 0.5 %collective-permute-start.6 = (bf16[208,128]{1,0:T(8,128)(2,1)S(1)}, bf16[208,128]{1,0:T(8,128)(2,1)S(1)}, u32[]{:S(2)}, u32[]{:S(2)}) collective-permute-start(bf16[208,128]{1,0:T(8,128)(2,1)S(1)} %get-tuple-element.27), channel_id=1, source_target_pairs={{0,24},{8,16},{16,8},{24,0},{1,25},{9,17},{17,9},{25,1},{2,26},{10... | collective-permute-start | bytes 159752 | tf_op jit(solution)/shard_map/ppermute | solution.py:68
  42.3 0.6 %activate.1 = f32[128,128]{1,0:T(8,128)} custom-call(f32[128,128]{1,0:T(8,128)S(1)} %get-tuple-element.20.pre), custom_call_target="tpu_custom_call" | custom-call | tf_op jit(solution)/shard_map/activate/pallas_call | solution.py:230
  43.0 0.0 collective-permute-done.4.refs_1_
  43.0 1.7 %collective-permute-done.5.refs_2_ = bf16[208,128]{1,0:T(8,128)(2,1)S(1)} collective-permute-done((bf16[208,128]{1,0:T(8,128)(2,1)S(1)}, bf16[208,128]{1,0:T(8,128)(2,1)S(1)}, u32[]{:S(2)}, u32[]{:S(2)}) %collective-permute-start.5) | collective-permute-done | bytes 53280 | tf_op jit(solution)/shard_map/ppermute | solution.py:68
  44.7 0.9 %collective-permute-done.6.refs_3_ = bf16[208,128]{1,0:T(8,128)(2,1)S(1)} collective-permute-done((bf16[208,128]{1,0:T(8,128)(2,1)S(1)}, bf16[208,128]{1,0:T(8,128)(2,1)S(1)}, u32[]{:S(2)}, u32[]{:S(2)}) %collective-permute-start.6) | collective-permute-done | bytes 53280 | tf_op jit(solution)/shard_map/ppermute | solution.py:68
  45.6 0.7 %final.1 = (bf16[32,512]{1,0:T(8,128)(2,1)}, f32[128,128]{1,0:T(8,128)}, f32[1,128]{1,0:T(1,128)}) custom-call(bf16[208,128]{1,0:T(8,128)(2,1)S(1)} %get-tuple-element.24.refs_0_, bf16[208,128]{1,0:T(8,128)(2,1)S(1)} %collective-permute-done.4.refs_1_, bf16[208,128]{1,0:T(8,128)(2,1)S(1)} %collective-permute-done.5.refs_2_, ...), custom_call_target="tpu_custom_call" | custom-call | tf_op jit(solution)/shard_map/final/pallas_call | solution.py:345
  (1 shorter events, 0.0 us)
Async XLA Ops:
  0.6 5.3 %collective-permute-start.2 = (bf16[32,512]{1,0:T(8,128)(2,1)}, bf16[32,512]{1,0:T(8,128)(2,1)S(1)}, u32[]{:S(2)}, u32[]{:S(2)}) collective-permute-start(bf16[32,512]{1,0:T(8,128)(2,1)} %bitcast.6), channel_id=1, source_target_pairs={{0,24},{8,16},{16,8},{24,0},{1,25},{9,17},{17,9},{25,1},{2,26},{10... | collective-permute-start | bytes 98312 | tf_op jit(solution)/shard_map/ppermute | solution.py:68
  3.1 4.2 %collective-permute-start.1 = (bf16[32,512]{1,0:T(8,128)(2,1)}, bf16[32,512]{1,0:T(8,128)(2,1)S(1)}, u32[]{:S(2)}, u32[]{:S(2)}) collective-permute-start(bf16[32,512]{1,0:T(8,128)(2,1)} %bitcast.7), channel_id=1, source_target_pairs={{0,16},{8,24},{16,0},{24,8},{1,17},{9,25},{17,1},{25,9},{2,18},{10... | collective-permute-start | bytes 98312 | tf_op jit(solution)/shard_map/ppermute | solution.py:68
  3.7 3.5 %collective-permute-start = (bf16[32,512]{1,0:T(8,128)(2,1)}, bf16[32,512]{1,0:T(8,128)(2,1)S(1)}, u32[]{:S(2)}, u32[]{:S(2)}) collective-permute-start(bf16[32,512]{1,0:T(8,128)(2,1)} %bitcast.8), channel_id=1, source_target_pairs={{0,8},{8,0},{16,24},{24,16},{1,9},{9,1},{17,25},{25,17},{2,10},{10... | collective-permute-start | bytes 98312 | tf_op jit(solution)/shard_map/ppermute | solution.py:68
  4.4 2.9 %copy-start.2 = (bf16[512,32]{0,1:T(8,128)(2,1)S(1)}, bf16[512,32]{0,1:T(8,128)(2,1)}, u32[]{:S(2)}) copy-start(bf16[512,32]{0,1:T(8,128)(2,1)} %param.9) | copy-start | bytes 98308
  7.6 14.7 %copy-start = (bf16[128,128]{1,0:T(8,128)(2,1)S(1)}, bf16[128,128]{1,0:T(8,128)(2,1)}, u32[]{:S(2)}) copy-start(bf16[128,128]{1,0:T(8,128)(2,1)} %weight.3) | copy-start | bytes 98308
  7.6 14.7 %copy-start.1 = (f32[128,128]{1,0:T(8,128)S(1)}, f32[128,128]{1,0:T(8,128)}, u32[]{:S(2)}) copy-start(f32[128,128]{1,0:T(8,128)} %cotangent.1) | copy-start | bytes 196612
  22.7 1.2 %collective-permute-start.3 = (bf16[64,128]{1,0:T(8,128)(2,1)S(1)}, bf16[64,128]{1,0:T(8,128)(2,1)S(1)}, u32[]{:S(2)}, u32[]{:S(2)}) collective-permute-start(bf16[64,128]{1,0:T(8,128)(2,1)S(1)} %get-tuple-element.23), channel_id=1, source_target_pairs={{0,8},{8,0},{16,24},{24,16},{1,9},{9,1},{17,25},{25,17},{2,10},{10... | collective-permute-start | bytes 49160 | tf_op jit(solution)/shard_map/ppermute | solution.py:68
  40.4 2.6 %collective-permute-start.4 = (bf16[208,128]{1,0:T(8,128)(2,1)S(1)}, bf16[208,128]{1,0:T(8,128)(2,1)S(1)}, u32[]{:S(2)}, u32[]{:S(2)}) collective-permute-start(bf16[208,128]{1,0:T(8,128)(2,1)S(1)} %get-tuple-element.25), channel_id=1, source_target_pairs={{0,8},{8,0},{16,24},{24,16},{1,9},{9,1},{17,25},{25,17},{2,10},{10... | collective-permute-start | bytes 159752 | tf_op jit(solution)/shard_map/ppermute | solution.py:68
  40.5 4.2 %collective-permute-start.5 = (bf16[208,128]{1,0:T(8,128)(2,1)S(1)}, bf16[208,128]{1,0:T(8,128)(2,1)S(1)}, u32[]{:S(2)}, u32[]{:S(2)}) collective-permute-start(bf16[208,128]{1,0:T(8,128)(2,1)S(1)} %get-tuple-element.26), channel_id=1, source_target_pairs={{0,16},{8,24},{16,0},{24,8},{1,17},{9,25},{17,1},{25,9},{2,18},{10... | collective-permute-start | bytes 159752 | tf_op jit(solution)/shard_map/ppermute | solution.py:68
  41.8 3.8 %collective-permute-start.6 = (bf16[208,128]{1,0:T(8,128)(2,1)S(1)}, bf16[208,128]{1,0:T(8,128)(2,1)S(1)}, u32[]{:S(2)}, u32[]{:S(2)}) collective-permute-start(bf16[208,128]{1,0:T(8,128)(2,1)S(1)} %get-tuple-element.27), channel_id=1, source_target_pairs={{0,24},{8,16},{16,8},{24,0},{1,25},{9,17},{17,9},{25,1},{2,26},{10... | collective-permute-start | bytes 159752 | tf_op jit(solution)/shard_map/ppermute | solution.py:68

commit v5 on v4

v5 whole, which is shorter than its diff:
```python
import functools

import jax
import jax.numpy as jnp
from jax import lax
from jax.experimental import pallas as pl
from jax.experimental.pallas import tpu as pltpu
from jax.sharding import PartitionSpec as P

f32 = jnp.float32
bf16 = jnp.bfloat16
tail = 16
wide = 1024
grant = 8 * 2**20


def room(*arrays):
    size = sum(a.size * a.dtype.itemsize for a in arrays)
    return pltpu.CompilerParams(vmem_limit_bytes=grant + 2 * size)


def vmem():
    return pl.BlockSpec(memory_space=pltpu.VMEM)


def smem():
    return pl.BlockSpec(memory_space=pltpu.SMEM)


def struct(shape, dtype):
    return jax.ShapeDtypeStruct(shape, dtype)


def dims(left, right):
    return (((left,), (right,)), ((), ()))


def dot(a, b, left=1, right=0):
    return lax.dot_general(a, b, dims(left, right), preferred_element_type=f32)


def each(count, body):
    if count <= 64:
        for index in range(count):
            body(index)
    else:
        lax.fori_loop(0, count, lambda index, none: (body(index), none)[1], 0)


def start_of(index, size):
    return index * size if isinstance(index, int) else pl.multiple_of(index * size, size)


def partner(me, step, size):
    if size & (size - 1) == 0:
        return me ^ step
    return (me + step) % size


def source(me, step, size):
    if size & (size - 1) == 0:
        return me ^ step
    return (me + size - step) % size


def exchange(value, axis, step, near=1):
    far = lax.axis_size(axis) // near
    pairs = [(i * near + j, partner(i, step, far) * near + j) for i in range(far) for j in range(near)]
    return lax.ppermute(value, axis, pairs)


def exchange_near(value, axis, near):
    size = lax.axis_size(axis)
    return lax.ppermute(value, axis, [(i, i // near * near + (near - 1 - i % near)) for i in range(size)])


def band_kernel(limit, rows, cols, ids, values, bias, band, bias_out, sums, scaled, here, row, col, sems):
    blocks, tile, _ = sums.shape
    row_blocks = band.shape[1] // tile
    slots = rows.shape[-1]
    ids_here, values_here = here
    lanes = ids_here.shape[0] // slots
    pairs = ((ids, ids_here), (values, values_here), (rows, row), (cols, col), (bias, bias_out))
    copies = [pltpu.make_async_copy(a, b, sems.at[i]) for i, (a, b) in enumerate(pairs)]
    for copy in copies:
        copy.start()

    def clear(index):
        sums[index] = jnp.zeros((tile, tile), f32)

    each(blocks, clear)
    for copy in copies:
        copy.wait()
    line = lax.broadcasted_iota(jnp.int32, scaled.shape, 0)
    scaled[...] = jnp.where(line < limit[0, 0] * lanes, values_here[...].astype(f32), 0.0)
    which = lax.broadcasted_iota(jnp.int32, (tile, tile), 0)

    def add(slot):
        block = col[0, 0, slot] * row_blocks + row[0, 0, slot]
        dense = jnp.zeros((tile, tile), f32)
        for lane in range(lanes):
            place = pl.ds(slot * lanes + lane, 1)
            dense = jnp.where(which == ids_here[place, :], scaled[place, :], dense)
        sums[block] = sums[block] + dense

    several = next(count for count in (4, 2, 1) if slots % count == 0)

    def group(index, none):
        for other in range(several):
            add(index * several + other)
        return none

    lax.fori_loop(0, (limit[0, 0] + several - 1) // several, group, 0)

    def put(index):
        c, r = index // row_blocks, index % row_blocks
        band[pl.ds(start_of(c, tile), tile), pl.ds(start_of(r, tile), tile)] = sums[index].astype(bf16)

    each(blocks, put)


def make_band(limit, rows, cols, ids, values, bias, row_blocks, col_blocks):
    tile = ids.shape[-1]
    lines = ids.shape[-3] * ids.shape[-2]
    ids = ids.reshape(lines, tile)
    values = values.reshape(lines, tile)
    bias = bias.reshape(1, -1)
    out = struct((col_blocks * tile, row_blocks * tile), bf16)
    sums = struct((col_blocks * row_blocks, tile, tile), f32)
    return pl.pallas_call(
        band_kernel,
        out_shape=(out, struct(bias.shape, f32)),
        in_specs=[smem()] + [pl.BlockSpec(memory_space=pltpu.HBM)] * 5,
        out_specs=(vmem(), vmem()),
        scratch_shapes=[
            pltpu.VMEM(sums.shape, f32),
            pltpu.VMEM((lines, tile), f32),
            (pltpu.VMEM((lines, tile), jnp.int32), pltpu.VMEM((lines, tile), bf16)),
            pltpu.SMEM(rows.shape, jnp.int32),
            pltpu.SMEM(cols.shape, jnp.int32),
            pltpu.SemaphoreType.DMA((5,)),
        ],
        compiler_params=pltpu.CompilerParams(vmem_limit_bytes=grant + sums.size * 4 + out.size * 2),
        cost_estimate=pl.CostEstimate(flops=8 * sums.size * 8, bytes_accessed=8 * 2**20, transcendentals=0),
        name="band",
    )(limit, *[pltpu.with_memory_space_constraint(a, pltpu.HBM) for a in (rows, cols, ids, values, bias)])


def forward_kernel(size, near, *refs):
    parts, (band, kept), messages, (panel, sums) = refs[:size], refs[size : size + 2], refs[size + 2 : -2], refs[-2:]
    me = lax.axis_index("row")
    mine = lax.axis_index("col") // near
    far, _, own = sums.shape
    width = parts[0].shape[0]
    for step, part in enumerate(parts):
        slot = pl.multiple_of(source(me, step, size) * width, width)
        panel[pl.ds(slot, width), :] = part[...].astype(f32)
    left = panel[...].astype(bf16)
    many = max(own, min(wide, band.shape[1]))

    def piece(index):
        got = dot(left, band[:, pl.ds(start_of(index, many), many)])
        for part in range(many // own):
            sums[index * (many // own) + part] = got[:, part * own : (part + 1) * own]

    each(band.shape[1] // many, piece)
    kept[...] = sums[mine]
    for step, message in enumerate(messages):
        message[...] = sums[partner(mine, step + 1, far)].astype(bf16)


def forward(parts, band, far, near):
    hidden = parts[0].shape[0] * len(parts)
    nodes, total = band.shape
    block = (hidden, total // far)
    return pl.pallas_call(
        functools.partial(forward_kernel, len(parts), near),
        out_shape=(struct(block, f32),) + (struct(block, bf16),) * (far - 1),
        in_specs=[vmem()] * (len(parts) + 1),
        out_specs=(vmem(),) * far,
        scratch_shapes=[pltpu.VMEM((hidden, nodes), f32), pltpu.VMEM((far,) + block, f32)],
        compiler_params=room(band, struct((far,) + block, f32)),
        name="forward",
    )(*parts, band)


def add_kernel(kept, *refs):
    parts, out = refs[:-1], refs[-1]
    total = kept[...]
    for part in parts:
        total = total + part[...].astype(f32)
    out[...] = total.astype(bf16)


def add(kept, parts):
    return pl.pallas_call(
        add_kernel,
        out_shape=struct(kept.shape, bf16),
        in_specs=[vmem()] * (len(parts) + 1),
        out_specs=vmem(),
        compiler_params=room(kept),
        name="add",
    )(kept, *parts)


def pair_rows(line):
    high = line.astype(bf16).astype(f32)
    row = lax.broadcasted_iota(jnp.int32, (tail, line.shape[1]), 0)
    return jnp.where(row == 0, high, jnp.where(row == 1, line - high, 0.0))


def own_kernel(near, *refs):
    sums, (weight, bias), cotangents = refs[:near], refs[near : near + 2], refs[near + 2 : 2 * near + 2]
    pre_out, message, wide_pre, given = refs[2 * near + 2 :]
    mine = lax.rem(lax.axis_index("col"), near)
    own = cotangents[0].shape[0]
    total = sums[0][...].astype(f32)
    for part in sums[1:]:
        total = total + part[...].astype(f32)
    for index, part in enumerate(cotangents):
        place = mine if index == 0 else near - 1 - mine
        given[pl.ds(pl.multiple_of(place * own, own), own), :] = part[...]
    high = total.astype(bf16)
    low = (total - high.astype(f32)).astype(bf16)
    pre = dot(high, weight[...], 0, 0) + dot(low, weight[...], 0, 0) + bias[...]
    wide_pre[...] = pre
    squashed = jax.nn.sigmoid(pre)
    grad = given[...] * squashed * (1.0 + pre * (1.0 - squashed))
    grad = grad.astype(bf16)
    rows = grad.shape[0]
    message[:rows, :] = grad
    message[rows:, :] = (dot(high, grad) + dot(low, grad)).astype(bf16)
    pre_out[...] = wide_pre[pl.ds(pl.multiple_of(mine * own, own), own), :]


def own_rows(sums, weight, bias, cotangents):
    near = len(sums)
    hidden, rows = sums[0].shape
    own = cotangents[0].shape[0]
    return pl.pallas_call(
        functools.partial(own_kernel, near),
        out_shape=(struct((own, hidden), f32), struct((rows + hidden, hidden), bf16)),
        in_specs=[vmem()] * (2 * near + 2),
        out_specs=(vmem(),) * 2,
        scratch_shapes=[pltpu.VMEM((rows, hidden), f32), pltpu.VMEM((rows, hidden), f32)],
        compiler_params=room(*sums),
        name="own_rows",
    )(*sums, weight, bias, *cotangents)


def activate_kernel(pre, act):
    act[...] = pre[...] * jax.nn.sigmoid(pre[...])


def activate(pre):
    return pl.pallas_call(
        activate_kernel,
        out_shape=struct(pre.shape, f32),
        in_specs=[vmem()],
        out_specs=vmem(),
        compiler_params=room(pre),
        name="activate",
    )(pre)


def backward_kernel(size, far, near, *refs):
    got, (weight, band), messages = refs[:far], refs[far : far + 2], refs[far + 2 : far + 2 + size]
    kept, rows, slots, back, grads, packed = refs[far + 2 + size :]
    hidden = weight.shape[0]
    own = got[0].shape[0] - hidden
    width, nodes = kept.shape
    me = lax.axis_index("row")
    mine = lax.axis_index("col") // near
    for step, part in enumerate(got):
        place = source(mine, step, far)
        rows[pl.ds(pl.multiple_of(place * own, own), own), :] = part[:own, :]
        slots[place] = part[own:, :].astype(f32)
    weight_part = slots[0]
    for index in range(1, far):
        weight_part = weight_part + slots[index]
    back[...] = dot(weight[...], rows[...], 1, 1).astype(bf16)
    many = min(wide, nodes)

    def piece(index):
        place = pl.ds(start_of(index, many), many)
        grads[:, place] = dot(back[...], band[place, :], 1, 1)

    each(nodes // many, piece)
    split = nodes // hidden
    packed[split * width : split * width + hidden, :] = weight_part
    packed[split * width + hidden :, :] = pair_rows(jnp.sum(rows[...].astype(f32), axis=0, keepdims=True))
    for step in range(size):
        slot = pl.multiple_of(partner(me, step, size) * width, width)
        block = grads[pl.ds(slot, width), :]
        if step == 0:
            kept[...] = block
        for index in range(split):
            packed[index * width : (index + 1) * width, :] = block[:, index * hidden : (index + 1) * hidden]
        messages[step][...] = packed[...].astype(bf16)


def backward(got, weight, band, size, near):
    far = len(got)
    hidden = weight.shape[0]
    nodes, total = band.shape
    width = hidden // size
    message = struct((width * (nodes // hidden) + hidden + tail, hidden), bf16)
    return pl.pallas_call(
        functools.partial(backward_kernel, size, far, near),
        out_shape=(message,) * size + (struct((width, nodes), f32),),
        in_specs=[vmem()] * (far + 2),
        out_specs=(vmem(),) * (size + 1),
        scratch_shapes=[
            pltpu.VMEM((total, hidden), bf16),
            pltpu.VMEM((far, hidden, hidden), f32),
            pltpu.VMEM((hidden, total), bf16),
            pltpu.VMEM((hidden, nodes), f32),
            pltpu.VMEM(message.shape, f32),
        ],
        compiler_params=room(band, *got),
        name="backward",
    )(*got, weight, band)


def final_kernel(size, shrink, *refs):
    messages, (kept, features, weight, bias, slots) = refs[:size], refs[size:]
    width, nodes = kept.shape
    hidden = weight.shape[0]
    split = nodes // hidden
    me = lax.axis_index("row")
    for step, message in enumerate(messages):
        slots[source(me, step, size)] = message[split * width :, :].astype(f32)
    for index in range(split):
        place = slice(index * hidden, (index + 1) * hidden)
        total = kept[:, place]
        for message in messages[1:]:
            total = total + message[index * width : (index + 1) * width, :].astype(f32)
        features[:, place] = total.astype(bf16)
    total = slots[0]
    for index in range(1, size):
        total = total + slots[index]
    weight[...] = total[:hidden] * shrink
    bias[...] = jnp.sum(total[hidden:], axis=0, keepdims=True) * shrink


def final(messages, kept, hidden, shrink):
    width, nodes = kept.shape
    size = len(messages)
    return pl.pallas_call(
        functools.partial(final_kernel, size, shrink),
        out_shape=(struct((width, nodes), bf16), struct((hidden, hidden), f32), struct((1, hidden), f32)),
        in_specs=[vmem()] * (size + 1),
        out_specs=(vmem(),) * 3,
        scratch_shapes=[pltpu.VMEM((size, hidden + tail, hidden), f32)],
        compiler_params=room(*messages),
        name="final",
    )(*messages, kept)


def shards(
    features,
    weight,
    bias_vector,
    tile_rows,
    tile_cols,
    neighbours,
    edge_weights,
    tile_count,
    cotangent,
):
    tile_size = neighbours.shape[-1]
    hidden = weight.shape[1]
    size, owners = lax.axis_size("row"), lax.axis_size("col")
    near = 2 if owners % 2 == 0 else 1
    far = owners // near
    blocks_own = cotangent.shape[0] // tile_size
    row_blocks = blocks_own * owners
    col_blocks = blocks_own * size
    turned = features.T
    parts = [turned] + [exchange(turned, "row", step) for step in range(1, size)]
    band, bias = make_band(
        tile_count, tile_rows, tile_cols, neighbours, edge_weights, bias_vector, row_blocks, col_blocks
    )
    kept, *messages = forward(parts, band, far, near)
    got = [exchange(message, "col", step + 1, near) for step, message in enumerate(messages)]
    cotangents = [cotangent]
    if near > 1:
        other, messages[0] = lax.optimization_barrier((cotangent, messages[0]))
        cotangents.append(exchange_near(other, "col", near))
    sums = [add(kept, got)]
    if near > 1:
        sums.append(exchange_near(sums[0], "col", near))
    pre, message = own_rows(sums, weight, bias, cotangents)
    activations = activate(pre)
    got = [message] + [exchange(message, "col", step, near) for step in range(1, far)]
    *messages, kept = backward(got, weight, band, size, near)
    messages = [messages[0]] + [exchange(messages[step], "row", step) for step in range(1, size)]
    node_count = cotangent.shape[0] * size * owners
    grad_features, grad_weight, grad_bias = final(messages, kept, hidden, float(node_count) ** (-0.5))
    return (activations, grad_features.T, grad_weight, grad_bias.reshape(hidden))


def solution(mesh):
    in_specs = (
        P("col", "row"),
        P(),
        P(),
        P("row", "col", None),
        P("row", "col", None),
        P("row", "col", None, None, None),
        P("row", "col", None, None, None),
        P("row", "col"),
        P(("row", "col"), None),
    )
    out_specs = (P(("row", "col"), None), P("col", "row"), P(), P())
    return jax.shard_map(shards, mesh=mesh, in_specs=in_specs, out_specs=out_specs, check_vma=False)
```

time: 46.5 us -> 39.5 us (0.85)
  blocking collectives: 30.4 us -> 0 us
  waiting for transfers between devices: 5.11 us -> 16.9 us
  starting transfers between devices: 5.15 us -> 16.9 us
    all_to_all x2 -> x0, blocking collectives: 30.4 us -> none  [the longest x1 15.8 us: shards(): message = lax.all_to_all(message, 'col', 0, 0, tiled=True)]
    ppermute x7 -> x14, starting transfers between devices: 5.15 us -> 16.9 us  [the longest x12 13.9 us: exchange(): return lax.ppermute(value, axis, pairs)]
    ppermute x7 -> x14, waiting for transfers between devices: 5.11 us -> 16.9 us  [the longest x12 14.1 us: exchange(): return lax.ppermute(value, axis, pairs)]
  transfers between devices with their start and end apart: 7 -> 14, of which waited for: 4 -> 9; matrix products, arithmetic and copies ran while one was open for 0% -> 0% of each run, Pallas kernels for 5% -> 6%
where the time goes in v5:
time: 39.5 us; the launch traced here: 39.4 us
  starting transfers between devices  16.9 us (43%)
  waiting for transfers between devices  16.9 us (43%)
  Pallas kernels  4.3 us (11%)
  between operations  1.36 us (3%)
    ppermute x12, waiting for transfers between devices, exchange(): return lax.ppermute(value, axis, pairs)  14.1 us
    ppermute x12, starting transfers between devices, exchange(): return lax.ppermute(value, axis, pairs)  13.9 us
    ppermute x2, starting transfers between devices, exchange_near(): lax.ppermute(value, axis, [(i, i // near * near + (near - 1 - i % near))...  3.04 us
    ppermute x2, waiting for transfers between devices, exchange_near(): lax.ppermute(value, axis, [(i, i // near * near + (near - 1 - i % near))...  2.78 us
    pallas_call x1, Pallas kernels, make_band(): pl.pallas_call(band_kernel, out_shape=(out, struct(bias.shape, f32)), in_...  1.5 us
  transfers between devices with their start and end apart: 14, of which 9 were waited for; matrix products, arithmetic and copies ran while one was open for 0% of the time, Pallas kernels for 6%

profile of v5, /device:TPU:0, one launch (start us, length us, event | category | flops | bytes accessed | tf_op | source)
XLA Modules:
  0.0 39.4 jit_solution(8947730816872570336)
XLA Ops:
  0.6 2.5 %collective-permute-start.2 = (bf16[32,512]{1,0:T(8,128)(2,1)}, bf16[32,512]{1,0:T(8,128)(2,1)S(1)}, u32[]{:S(2)}, u32[]{:S(2)}) collective-permute-start(bf16[32,512]{1,0:T(8,128)(2,1)} %bitcast.6), channel_id=1, source_target_pairs={{0,24},{8,16},{16,8},{24,0},{1,25},{9,17},{17,9},{25,1},{2,26},{10... | collective-permute-start | bytes 98312 | tf_op jit(solution)/shard_map/ppermute | solution.py:69
  3.1 0.6 %collective-permute-start.1 = (bf16[32,512]{1,0:T(8,128)(2,1)}, bf16[32,512]{1,0:T(8,128)(2,1)S(1)}, u32[]{:S(2)}, u32[]{:S(2)}) collective-permute-start(bf16[32,512]{1,0:T(8,128)(2,1)} %bitcast.7), channel_id=1, source_target_pairs={{0,16},{8,24},{16,0},{24,8},{1,17},{9,25},{17,1},{25,9},{2,18},{10... | collective-permute-start | bytes 98312 | tf_op jit(solution)/shard_map/ppermute | solution.py:69
  3.7 0.0 collective-permute-start
  4.4 0.0 copy-start.2
  4.4 1.5 %band.1 = (bf16[512,1024]{1,0:T(8,128)(2,1)S(1)}, f32[1,128]{1,0:T(1,128)S(1)}) custom-call(s32[1,1]{1,0:T(1,128)S(6)} %copy.13.limit, s32[1,1,128]{2,1,0:T(1,128)} %rows.1, s32[1,1,128]{2,1,0:T(1,128)} %cols.1, s32[256,128]{1,0:T(8,128)} %bitcast.10, bf16[256,128]{1,0:T(8,128)(2,1)} %bitcast.11, f32[1,128]{1,0:T(1,128)} %bitcast.12), custom_call_target="tpu_custom_call" | custom-call | flops 33554432 | bytes 8388608 | tf_op jit(solution)/shard_map/band/pallas_call | solution.py:130
  6.0 0.0 collective-permute-done.2.refs_3_
  6.0 1.3 %collective-permute-done.1.refs_2_ = bf16[32,512]{1,0:T(8,128)(2,1)S(1)} collective-permute-done((bf16[32,512]{1,0:T(8,128)(2,1)}, bf16[32,512]{1,0:T(8,128)(2,1)S(1)}, u32[]{:S(2)}, u32[]{:S(2)}) %collective-permute-start.1) | collective-permute-done | bytes 32800 | tf_op jit(solution)/shard_map/ppermute | solution.py:69
  7.3 0.0 collective-permute-done.refs_1_
  7.3 0.0 copy-done.2
  7.3 0.0 copy-start.1
  7.3 0.3 forward.1
  7.6 2.7 %collective-permute-start.4 = (bf16[128,256]{1,0:T(8,128)(2,1)S(1)}, bf16[128,256]{1,0:T(8,128)(2,1)S(1)}, u32[]{:S(2)}, u32[]{:S(2)}) collective-permute-start(bf16[128,256]{1,0:T(8,128)(2,1)S(1)} %get-tuple-element.24), channel_id=1, source_target_pairs={{0,4},{1,5},{2,6},{3,7},{4,0},{5,1},{6,2},{7,3},{8,12},{9,13},{10,... | collective-permute-start | bytes 196616 | tf_op jit(solution)/shard_map/ppermute | solution.py:69
  10.3 1.3 %collective-permute-start.5 = (bf16[128,256]{1,0:T(8,128)(2,1)S(1)}, bf16[128,256]{1,0:T(8,128)(2,1)S(1)}, u32[]{:S(2)}, u32[]{:S(2)}) collective-permute-start(bf16[128,256]{1,0:T(8,128)(2,1)S(1)} %get-tuple-element.25), channel_id=1, source_target_pairs={{0,6},{1,7},{2,4},{3,5},{4,2},{5,3},{6,0},{7,1},{8,14},{9,15},{10,... | collective-permute-start | bytes 196616 | tf_op jit(solution)/shard_map/ppermute | solution.py:69
  11.7 0.2 collective-permute-start.3
  11.9 0.0 copy-done.1
  11.9 1.5 %collective-permute-start.7 = (f32[128,128]{1,0:T(8,128)S(1)}, f32[128,128]{1,0:T(8,128)S(1)}, u32[]{:S(2)}, u32[]{:S(2)}) collective-permute-start(f32[128,128]{1,0:T(8,128)S(1)} %copy-done.1), channel_id=1, source_target_pairs={{0,1},{1,0},{2,3},{3,2},{4,5},{5,4},{6,7},{7,6},{8,9},{9,8},{10,11... | collective-permute-start | bytes 196616 | tf_op jit(solution)/shard_map/ppermute | solution.py:74
  13.4 1.7 %collective-permute-done.4.refs_1_ = bf16[128,256]{1,0:T(8,128)(2,1)S(1)} collective-permute-done((bf16[128,256]{1,0:T(8,128)(2,1)S(1)}, bf16[128,256]{1,0:T(8,128)(2,1)S(1)}, u32[]{:S(2)}, u32[]{:S(2)}) %collective-permute-start.4) | collective-permute-done | bytes 65568 | tf_op jit(solution)/shard_map/ppermute | solution.py:69
  15.1 1.5 %collective-permute-done.5.refs_2_ = bf16[128,256]{1,0:T(8,128)(2,1)S(1)} collective-permute-done((bf16[128,256]{1,0:T(8,128)(2,1)S(1)}, bf16[128,256]{1,0:T(8,128)(2,1)S(1)}, u32[]{:S(2)}, u32[]{:S(2)}) %collective-permute-start.5) | collective-permute-done | bytes 65568 | tf_op jit(solution)/shard_map/ppermute | solution.py:69
  16.5 0.1 collective-permute-done.3.refs_0_
  16.6 0.0 copy-start
  16.7 1.6 %collective-permute-start.6 = (bf16[128,256]{1,0:T(8,128)(2,1)S(1)}, bf16[128,256]{1,0:T(8,128)(2,1)S(1)}, u32[]{:S(2)}, u32[]{:S(2)}) collective-permute-start(bf16[128,256]{1,0:T(8,128)(2,1)S(1)} %add.1.refs_0_), channel_id=1, source_target_pairs={{0,1},{1,0},{2,3},{3,2},{4,5},{5,4},{6,7},{7,6},{8,9},{9,8},{10,11... | collective-permute-start | bytes 196616 | tf_op jit(solution)/shard_map/ppermute | solution.py:74
  18.2 0.0 collective-permute-done.7.refs_5_
  18.2 2.8 %collective-permute-done.6.refs_1_ = bf16[128,256]{1,0:T(8,128)(2,1)S(1)} collective-permute-done((bf16[128,256]{1,0:T(8,128)(2,1)S(1)}, bf16[128,256]{1,0:T(8,128)(2,1)S(1)}, u32[]{:S(2)}, u32[]{:S(2)}) %collective-permute-start.6) | collective-permute-done | bytes 65568 | tf_op jit(solution)/shard_map/ppermute | solution.py:74
  21.0 0.0 copy-done
  21.0 0.5 %own_rows.1 = (f32[128,128]{1,0:T(8,128)S(1)}, bf16[384,128]{1,0:T(8,128)(2,1)S(1)}) custom-call(bf16[128,256]{1,0:T(8,128)(2,1)S(1)} %add.1.refs_0_, bf16[128,256]{1,0:T(8,128)(2,1)S(1)} %collective-permute-done.6.refs_1_, bf16[128,128]{1,0:T(8,128)(2,1)S(1)} %copy-done, f32[1,128]{1,0:T(1,128)S(1)} %get-tuple-element.26.refs_3_, f32[128,128]{1,0:T(8,128)S(1)} %copy-done.1, ...), custom_call_target="tpu_custom_call" | custom-call | tf_op jit(solution)/shard_map/own_rows/pallas_call | solution.py:240
  21.5 3.0 %collective-permute-start.10 = (bf16[384,128]{1,0:T(8,128)(2,1)S(1)}, bf16[384,128]{1,0:T(8,128)(2,1)S(1)}, u32[]{:S(2)}, u32[]{:S(2)}) collective-permute-start(bf16[384,128]{1,0:T(8,128)(2,1)S(1)} %get-tuple-element.29.refs_0_), channel_id=1, source_target_pairs={{0,6},{1,7},{2,4},{3,5},{4,2},{5,3},{6,0},{7,1},{8,14},{9,15},{10,... | collective-permute-start | bytes 294920 | tf_op jit(solution)/shard_map/ppermute | solution.py:69
  24.5 0.0 collective-permute-start.9
  24.5 1.4 %collective-permute-start.8 = (bf16[384,128]{1,0:T(8,128)(2,1)S(1)}, bf16[384,128]{1,0:T(8,128)(2,1)S(1)}, u32[]{:S(2)}, u32[]{:S(2)}) collective-permute-start(bf16[384,128]{1,0:T(8,128)(2,1)S(1)} %get-tuple-element.29.refs_0_), channel_id=1, source_target_pairs={{0,2},{1,3},{2,0},{3,1},{4,6},{5,7},{6,4},{7,5},{8,10},{9,11},{10,... | collective-permute-start | bytes 294920 | tf_op jit(solution)/shard_map/ppermute | solution.py:69
  25.9 3.1 %collective-permute-done.10.refs_3_ = bf16[384,128]{1,0:T(8,128)(2,1)S(1)} collective-permute-done((bf16[384,128]{1,0:T(8,128)(2,1)S(1)}, bf16[384,128]{1,0:T(8,128)(2,1)S(1)}, u32[]{:S(2)}, u32[]{:S(2)}) %collective-permute-start.10) | collective-permute-done | bytes 98336 | tf_op jit(solution)/shard_map/ppermute | solution.py:69
  29.0 3.0 %collective-permute-done.9.refs_2_ = bf16[384,128]{1,0:T(8,128)(2,1)S(1)} collective-permute-done((bf16[384,128]{1,0:T(8,128)(2,1)S(1)}, bf16[384,128]{1,0:T(8,128)(2,1)S(1)}, u32[]{:S(2)}, u32[]{:S(2)}) %collective-permute-start.9) | collective-permute-done | bytes 98336 | tf_op jit(solution)/shard_map/ppermute | solution.py:69
  32.0 0.0 collective-permute-done.8.refs_1_
  32.0 0.6 %backward.1 = (bf16[272,128]{1,0:T(8,128)(2,1)S(1)}, bf16[272,128]{1,0:T(8,128)(2,1)S(1)}, bf16[272,128]{1,0:T(8,128)(2,1)S(1)}, bf16[272,128]{1,0:T(8,128)(2,1)S(1)}, f32[32,512]{1,0:T(8,128)S(1)}) custom-call(bf16[384,128]{1,0:T(8,128)(2,1)S(1)} %get-tuple-element.29.refs_0_, bf16[384,128]{1,0:T(8,128)(2,1)S(1)} %collective-permute-done.8.refs_1_, ...), custom_call_target="tpu_custom_call" | custom-call | tf_op jit(solution)/shard_map/backward/pallas_call | solution.py:308
  32.6 0.1 collective-permute-start.11
  32.7 1.9 %collective-permute-start.12 = (bf16[272,128]{1,0:T(8,128)(2,1)S(1)}, bf16[272,128]{1,0:T(8,128)(2,1)S(1)}, u32[]{:S(2)}, u32[]{:S(2)}) collective-permute-start(bf16[272,128]{1,0:T(8,128)(2,1)S(1)} %get-tuple-element.32), channel_id=1, source_target_pairs={{0,16},{8,24},{16,0},{24,8},{1,17},{9,25},{17,1},{25,9},{2,18},{10... | collective-permute-start | bytes 208904 | tf_op jit(solution)/shard_map/ppermute | solution.py:69
  34.6 0.1 collective-permute-start.13
  34.7 0.6 %activate.1 = f32[128,128]{1,0:T(8,128)} custom-call(f32[128,128]{1,0:T(8,128)S(1)} %get-tuple-element.28.pre), custom_call_target="tpu_custom_call" | custom-call | tf_op jit(solution)/shard_map/activate/pallas_call | solution.py:256
  35.3 0.0 collective-permute-done.11.refs_1_
  35.3 2.1 %collective-permute-done.12.refs_2_ = bf16[272,128]{1,0:T(8,128)(2,1)S(1)} collective-permute-done((bf16[272,128]{1,0:T(8,128)(2,1)S(1)}, bf16[272,128]{1,0:T(8,128)(2,1)S(1)}, u32[]{:S(2)}, u32[]{:S(2)}) %collective-permute-start.12) | collective-permute-done | bytes 69664 | tf_op jit(solution)/shard_map/ppermute | solution.py:69
  37.4 1.4 %collective-permute-done.13.refs_3_ = bf16[272,128]{1,0:T(8,128)(2,1)S(1)} collective-permute-done((bf16[272,128]{1,0:T(8,128)(2,1)S(1)}, bf16[272,128]{1,0:T(8,128)(2,1)S(1)}, u32[]{:S(2)}, u32[]{:S(2)}) %collective-permute-start.13) | collective-permute-done | bytes 69664 | tf_op jit(solution)/shard_map/ppermute | solution.py:69
  38.7 0.7 %final.1 = (bf16[32,512]{1,0:T(8,128)(2,1)}, f32[128,128]{1,0:T(8,128)}, f32[1,128]{1,0:T(1,128)}) custom-call(bf16[272,128]{1,0:T(8,128)(2,1)S(1)} %get-tuple-element.30.refs_0_, bf16[272,128]{1,0:T(8,128)(2,1)S(1)} %collective-permute-done.11.refs_1_, bf16[272,128]{1,0:T(8,128)(2,1)S(1)} %collective-permute-done.12.refs_2_, ...), custom_call_target="tpu_custom_call" | custom-call | tf_op jit(solution)/shard_map/final/pallas_call | solution.py:349
  (1 shorter events, 0.0 us)
Async XLA Ops:
  0.6 5.3 %collective-permute-start.2 = (bf16[32,512]{1,0:T(8,128)(2,1)}, bf16[32,512]{1,0:T(8,128)(2,1)S(1)}, u32[]{:S(2)}, u32[]{:S(2)}) collective-permute-start(bf16[32,512]{1,0:T(8,128)(2,1)} %bitcast.6), channel_id=1, source_target_pairs={{0,24},{8,16},{16,8},{24,0},{1,25},{9,17},{17,9},{25,1},{2,26},{10... | collective-permute-start | bytes 98312 | tf_op jit(solution)/shard_map/ppermute | solution.py:69
  3.1 4.2 %collective-permute-start.1 = (bf16[32,512]{1,0:T(8,128)(2,1)}, bf16[32,512]{1,0:T(8,128)(2,1)S(1)}, u32[]{:S(2)}, u32[]{:S(2)}) collective-permute-start(bf16[32,512]{1,0:T(8,128)(2,1)} %bitcast.7), channel_id=1, source_target_pairs={{0,16},{8,24},{16,0},{24,8},{1,17},{9,25},{17,1},{25,9},{2,18},{10... | collective-permute-start | bytes 98312 | tf_op jit(solution)/shard_map/ppermute | solution.py:69
  3.7 3.5 %collective-permute-start = (bf16[32,512]{1,0:T(8,128)(2,1)}, bf16[32,512]{1,0:T(8,128)(2,1)S(1)}, u32[]{:S(2)}, u32[]{:S(2)}) collective-permute-start(bf16[32,512]{1,0:T(8,128)(2,1)} %bitcast.8), channel_id=1, source_target_pairs={{0,8},{8,0},{16,24},{24,16},{1,9},{9,1},{17,25},{25,17},{2,10},{10... | collective-permute-start | bytes 98312 | tf_op jit(solution)/shard_map/ppermute | solution.py:69
  4.4 2.9 %copy-start.2 = (bf16[512,32]{0,1:T(8,128)(2,1)S(1)}, bf16[512,32]{0,1:T(8,128)(2,1)}, u32[]{:S(2)}) copy-start(bf16[512,32]{0,1:T(8,128)(2,1)} %param.9) | copy-start | bytes 98308
  7.3 4.6 %copy-start.1 = (f32[128,128]{1,0:T(8,128)S(1)}, f32[128,128]{1,0:T(8,128)}, u32[]{:S(2)}) copy-start(f32[128,128]{1,0:T(8,128)} %refs_4_.2) | copy-start | bytes 196612
  7.6 7.4 %collective-permute-start.4 = (bf16[128,256]{1,0:T(8,128)(2,1)S(1)}, bf16[128,256]{1,0:T(8,128)(2,1)S(1)}, u32[]{:S(2)}, u32[]{:S(2)}) collective-permute-start(bf16[128,256]{1,0:T(8,128)(2,1)S(1)} %get-tuple-element.24), channel_id=1, source_target_pairs={{0,4},{1,5},{2,6},{3,7},{4,0},{5,1},{6,2},{7,3},{8,12},{9,13},{10,... | collective-permute-start | bytes 196616 | tf_op jit(solution)/shard_map/ppermute | solution.py:69
  10.3 6.2 %collective-permute-start.5 = (bf16[128,256]{1,0:T(8,128)(2,1)S(1)}, bf16[128,256]{1,0:T(8,128)(2,1)S(1)}, u32[]{:S(2)}, u32[]{:S(2)}) collective-permute-start(bf16[128,256]{1,0:T(8,128)(2,1)S(1)} %get-tuple-element.25), channel_id=1, source_target_pairs={{0,6},{1,7},{2,4},{3,5},{4,2},{5,3},{6,0},{7,1},{8,14},{9,15},{10,... | collective-permute-start | bytes 196616 | tf_op jit(solution)/shard_map/ppermute | solution.py:69
  11.7 5.0 %collective-permute-start.3 = (bf16[128,256]{1,0:T(8,128)(2,1)S(1)}, bf16[128,256]{1,0:T(8,128)(2,1)S(1)}, u32[]{:S(2)}, u32[]{:S(2)}) collective-permute-start(bf16[128,256]{1,0:T(8,128)(2,1)S(1)} %get-tuple-element.23), channel_id=1, source_target_pairs={{0,2},{1,3},{2,0},{3,1},{4,6},{5,7},{6,4},{7,5},{8,10},{9,11},{10,... | collective-permute-start | bytes 196616 | tf_op jit(solution)/shard_map/ppermute | solution.py:69
  11.9 6.3 %collective-permute-start.7 = (f32[128,128]{1,0:T(8,128)S(1)}, f32[128,128]{1,0:T(8,128)S(1)}, u32[]{:S(2)}, u32[]{:S(2)}) collective-permute-start(f32[128,128]{1,0:T(8,128)S(1)} %copy-done.1), channel_id=1, source_target_pairs={{0,1},{1,0},{2,3},{3,2},{4,5},{5,4},{6,7},{7,6},{8,9},{9,8},{10,11... | collective-permute-start | bytes 196616 | tf_op jit(solution)/shard_map/ppermute | solution.py:74
  16.6 4.4 %copy-start = (bf16[128,128]{1,0:T(8,128)(2,1)S(1)}, bf16[128,128]{1,0:T(8,128)(2,1)}, u32[]{:S(2)}) copy-start(bf16[128,128]{1,0:T(8,128)(2,1)} %refs_4_.3) | copy-start | bytes 98308
  16.7 4.3 %collective-permute-start.6 = (bf16[128,256]{1,0:T(8,128)(2,1)S(1)}, bf16[128,256]{1,0:T(8,128)(2,1)S(1)}, u32[]{:S(2)}, u32[]{:S(2)}) collective-permute-start(bf16[128,256]{1,0:T(8,128)(2,1)S(1)} %add.1.refs_0_), channel_id=1, source_target_pairs={{0,1},{1,0},{2,3},{3,2},{4,5},{5,4},{6,7},{7,6},{8,9},{9,8},{10,11... | collective-permute-start | bytes 196616 | tf_op jit(solution)/shard_map/ppermute | solution.py:74
  21.5 7.6 %collective-permute-start.10 = (bf16[384,128]{1,0:T(8,128)(2,1)S(1)}, bf16[384,128]{1,0:T(8,128)(2,1)S(1)}, u32[]{:S(2)}, u32[]{:S(2)}) collective-permute-start(bf16[384,128]{1,0:T(8,128)(2,1)S(1)} %get-tuple-element.29.refs_0_), channel_id=1, source_target_pairs={{0,6},{1,7},{2,4},{3,5},{4,2},{5,3},{6,0},{7,1},{8,14},{9,15},{10,... | collective-permute-start | bytes 294920 | tf_op jit(solution)/shard_map/ppermute | solution.py:69
  24.5 7.5 %collective-permute-start.9 = (bf16[384,128]{1,0:T(8,128)(2,1)S(1)}, bf16[384,128]{1,0:T(8,128)(2,1)S(1)}, u32[]{:S(2)}, u32[]{:S(2)}) collective-permute-start(bf16[384,128]{1,0:T(8,128)(2,1)S(1)} %get-tuple-element.29.refs_0_), channel_id=1, source_target_pairs={{0,4},{1,5},{2,6},{3,7},{4,0},{5,1},{6,2},{7,3},{8,12},{9,13},{10,... | collective-permute-start | bytes 294920 | tf_op jit(solution)/shard_map/ppermute | solution.py:69
  24.5 7.5 %collective-permute-start.8 = (bf16[384,128]{1,0:T(8,128)(2,1)S(1)}, bf16[384,128]{1,0:T(8,128)(2,1)S(1)}, u32[]{:S(2)}, u32[]{:S(2)}) collective-permute-start(bf16[384,128]{1,0:T(8,128)(2,1)S(1)} %get-tuple-element.29.refs_0_), channel_id=1, source_target_pairs={{0,2},{1,3},{2,0},{3,1},{4,6},{5,7},{6,4},{7,5},{8,10},{9,11},{10,... | collective-permute-start | bytes 294920 | tf_op jit(solution)/shard_map/ppermute | solution.py:69
  32.6 2.7 %collective-permute-start.11 = (bf16[272,128]{1,0:T(8,128)(2,1)S(1)}, bf16[272,128]{1,0:T(8,128)(2,1)S(1)}, u32[]{:S(2)}, u32[]{:S(2)}) collective-permute-start(bf16[272,128]{1,0:T(8,128)(2,1)S(1)} %get-tuple-element.31), channel_id=1, source_target_pairs={{0,8},{8,0},{16,24},{24,16},{1,9},{9,1},{17,25},{25,17},{2,10},{10... | collective-permute-start | bytes 208904 | tf_op jit(solution)/shard_map/ppermute | solution.py:69
  32.7 4.7 %collective-permute-start.12 = (bf16[272,128]{1,0:T(8,128)(2,1)S(1)}, bf16[272,128]{1,0:T(8,128)(2,1)S(1)}, u32[]{:S(2)}, u32[]{:S(2)}) collective-permute-start(bf16[272,128]{1,0:T(8,128)(2,1)S(1)} %get-tuple-element.32), channel_id=1, source_target_pairs={{0,16},{8,24},{16,0},{24,8},{1,17},{9,25},{17,1},{25,9},{2,18},{10... | collective-permute-start | bytes 208904 | tf_op jit(solution)/shard_map/ppermute | solution.py:69
  34.6 4.1 %collective-permute-start.13 = (bf16[272,128]{1,0:T(8,128)(2,1)S(1)}, bf16[272,128]{1,0:T(8,128)(2,1)S(1)}, u32[]{:S(2)}, u32[]{:S(2)}) collective-permute-start(bf16[272,128]{1,0:T(8,128)(2,1)S(1)} %get-tuple-element.33), channel_id=1, source_target_pairs={{0,24},{8,16},{16,8},{24,0},{1,25},{9,17},{17,9},{25,1},{2,26},{10... | collective-permute-start | bytes 208904 | tf_op jit(solution)/shard_map/ppermute | solution.py:69

commit v6 on v5

--- a/solution.py
+++ b/solution.py
@@ -63,15 +63,15 @@
     return (me + size - step) % size
 
 
-def exchange(value, axis, step, near=1):
-    far = lax.axis_size(axis) // near
-    pairs = [(i * near + j, partner(i, step, far) * near + j) for i in range(far) for j in range(near)]
+def exchange(value, axis, step, members):
+    size = lax.axis_size(axis)
+    pairs = [(i, i // members * members + partner(i % members, step, members)) for i in range(size)]
     return lax.ppermute(value, axis, pairs)
 
 
-def exchange_near(value, axis, near):
+def exchange_twin(value, axis, members):
     size = lax.axis_size(axis)
-    return lax.ppermute(value, axis, [(i, i // near * near + (near - 1 - i % near)) for i in range(size)])
+    return lax.ppermute(value, axis, [(i, (i + members) % size) for i in range(size)])
 
 
 def band_kernel(limit, rows, cols, ids, values, bias, band, bias_out, sums, scaled, here, row, col, sems):
@@ -146,11 +146,11 @@
     )(limit, *[pltpu.with_memory_space_constraint(a, pltpu.HBM) for a in (rows, cols, ids, values, bias)])
 
 
-def forward_kernel(size, near, *refs):
+def forward_kernel(size, members, *refs):
     parts, (band, kept), messages, (panel, sums) = refs[:size], refs[size : size + 2], refs[size + 2 : -2], refs[-2:]
     me = lax.axis_index("row")
-    mine = lax.axis_index("col") // near
-    far, _, own = sums.shape
+    mine = lax.rem(lax.axis_index("col"), members)
+    owners, _, own = sums.shape
     width = parts[0].shape[0]
     for step, part in enumerate(parts):
         slot = pl.multiple_of(source(me, step, size) * width, width)
@@ -164,22 +164,24 @@
             sums[index * (many // own) + part] = got[:, part * own : (part + 1) * own]
 
     each(band.shape[1] // many, piece)
-    kept[...] = sums[mine]
-    for step, message in enumerate(messages):
-        message[...] = sums[partner(mine, step + 1, far)].astype(bf16)
-
-
-def forward(parts, band, far, near):
+    for step, message in enumerate((kept,) + messages):
+        place = partner(mine, step, members)
+        for twin in range(owners // members):
+            message[:, twin * own : (twin + 1) * own] = sums[place + twin * members].astype(message.dtype)
+
+
+def forward(parts, band, owners, members):
     hidden = parts[0].shape[0] * len(parts)
     nodes, total = band.shape
-    block = (hidden, total // far)
-    return pl.pallas_call(
-        functools.partial(forward_kernel, len(parts), near),
-        out_shape=(struct(block, f32),) + (struct(block, bf16),) * (far - 1),
+    block = (hidden, total // members)
+    sums = struct((owners, hidden, total // owners), f32)
+    return pl.pallas_call(
+        functools.partial(forward_kernel, len(parts), members),
+        out_shape=(struct(block, f32),) + (struct(block, bf16),) * (members - 1),
         in_specs=[vmem()] * (len(parts) + 1),
-        out_specs=(vmem(),) * far,
-        scratch_shapes=[pltpu.VMEM((hidden, nodes), f32), pltpu.VMEM((far,) + block, f32)],
-        compiler_params=room(band, struct((far,) + block, f32)),
+        out_specs=(vmem(),) * members,
+        scratch_shapes=[pltpu.VMEM((hidden, nodes), f32), pltpu.VMEM(sums.shape, f32)],
+        compiler_params=room(band, sums),
         name="forward",
     )(*parts, band)
 
@@ -209,16 +211,16 @@
     return jnp.where(row == 0, high, jnp.where(row == 1, line - high, 0.0))
 
 
-def own_kernel(near, *refs):
-    sums, (weight, bias), cotangents = refs[:near], refs[near : near + 2], refs[near + 2 : 2 * near + 2]
-    pre_out, message, wide_pre, given = refs[2 * near + 2 :]
-    mine = lax.rem(lax.axis_index("col"), near)
+def own_kernel(members, twins, *refs):
+    sums, (weight, bias), cotangents = refs[:twins], refs[twins : twins + 2], refs[twins + 2 : 2 * twins + 2]
+    pre_out, message, wide_pre, given = refs[2 * twins + 2 :]
+    mine = lax.axis_index("col") // members
     own = cotangents[0].shape[0]
     total = sums[0][...].astype(f32)
     for part in sums[1:]:
         total = total + part[...].astype(f32)
     for index, part in enumerate(cotangents):
-        place = mine if index == 0 else near - 1 - mine
+        place = mine if index == 0 else twins - 1 - mine
         given[pl.ds(pl.multiple_of(place * own, own), own), :] = part[...]
     high = total.astype(bf16)
     low = (total - high.astype(f32)).astype(bf16)
@@ -233,14 +235,14 @@
     pre_out[...] = wide_pre[pl.ds(pl.multiple_of(mine * own, own), own), :]
 
 
-def own_rows(sums, weight, bias, cotangents):
-    near = len(sums)
+def own_rows(sums, weight, bias, cotangents, members):
+    twins = len(sums)
     hidden, rows = sums[0].shape
     own = cotangents[0].shape[0]
     return pl.pallas_call(
-        functools.partial(own_kernel, near),
+        functools.partial(own_kernel, members, twins),
         out_shape=(struct((own, hidden), f32), struct((rows + hidden, hidden), bf16)),
-        in_specs=[vmem()] * (2 * near + 2),
+        in_specs=[vmem()] * (2 * twins + 2),
         out_specs=(vmem(),) * 2,
         scratch_shapes=[pltpu.VMEM((rows, hidden), f32), pltpu.VMEM((rows, hidden), f32)],
         compiler_params=room(*sums),
@@ -263,20 +265,22 @@
     )(pre)
 
 
-def backward_kernel(size, far, near, *refs):
-    got, (weight, band), messages = refs[:far], refs[far : far + 2], refs[far + 2 : far + 2 + size]
-    kept, rows, slots, back, grads, packed = refs[far + 2 + size :]
+def backward_kernel(size, members, twins, *refs):
+    got, (weight, band), messages = refs[:members], refs[members : members + 2], refs[members + 2 : members + 2 + size]
+    kept, rows, slots, back, grads, packed = refs[members + 2 + size :]
     hidden = weight.shape[0]
-    own = got[0].shape[0] - hidden
+    own = rows.shape[0] // (members * twins)
     width, nodes = kept.shape
     me = lax.axis_index("row")
-    mine = lax.axis_index("col") // near
+    mine = lax.rem(lax.axis_index("col"), members)
     for step, part in enumerate(got):
-        place = source(mine, step, far)
-        rows[pl.ds(pl.multiple_of(place * own, own), own), :] = part[:own, :]
-        slots[place] = part[own:, :].astype(f32)
+        place = source(mine, step, members)
+        for twin in range(twins):
+            spot = pl.multiple_of((place + twin * members) * own, own)
+            rows[pl.ds(spot, own), :] = part[twin * own : (twin + 1) * own, :]
+        slots[place] = part[twins * own :, :].astype(f32)
     weight_part = slots[0]
-    for index in range(1, far):
+    for index in range(1, members):
         weight_part = weight_part + slots[index]
     back[...] = dot(weight[...], rows[...], 1, 1).astype(bf16)
     many = min(wide, nodes)
@@ -299,20 +303,20 @@
         messages[step][...] = packed[...].astype(bf16)
 
 
-def backward(got, weight, band, size, near):
-    far = len(got)
+def backward(got, weight, band, size, twins):
+    members = len(got)
     hidden = weight.shape[0]
     nodes, total = band.shape
     width = hidden // size
     message = struct((width * (nodes // hidden) + hidden + tail, hidden), bf16)
     return pl.pallas_call(
-        functools.partial(backward_kernel, size, far, near),
+        functools.partial(backward_kernel, size, members, twins),
         out_shape=(message,) * size + (struct((width, nodes), f32),),
-        in_specs=[vmem()] * (far + 2),
+        in_specs=[vmem()] * (members + 2),
         out_specs=(vmem(),) * (size + 1),
         scratch_shapes=[
             pltpu.VMEM((total, hidden), bf16),
-            pltpu.VMEM((far, hidden, hidden), f32),
+            pltpu.VMEM((members, hidden, hidden), f32),
             pltpu.VMEM((hidden, total), bf16),
             pltpu.VMEM((hidden, nodes), f32),
             pltpu.VMEM(message.shape, f32),
@@ -371,30 +375,30 @@
     tile_size = neighbours.shape[-1]
     hidden = weight.shape[1]
     size, owners = lax.axis_size("row"), lax.axis_size("col")
-    near = 2 if owners % 2 == 0 else 1
-    far = owners // near
+    twins = 2 if owners % 2 == 0 else 1
+    members = owners // twins
     blocks_own = cotangent.shape[0] // tile_size
     row_blocks = blocks_own * owners
     col_blocks = blocks_own * size
     turned = features.T
-    parts = [turned] + [exchange(turned, "row", step) for step in range(1, size)]
+    parts = [turned] + [exchange(turned, "row", step, size) for step in range(1, size)]
     band, bias = make_band(
         tile_count, tile_rows, tile_cols, neighbours, edge_weights, bias_vector, row_blocks, col_blocks
     )
-    kept, *messages = forward(parts, band, far, near)
-    got = [exchange(message, "col", step + 1, near) for step, message in enumerate(messages)]
+    kept, *messages = forward(parts, band, owners, members)
+    got = [exchange(message, "col", step + 1, members) for step, message in enumerate(messages)]
     cotangents = [cotangent]
-    if near > 1:
+    if twins > 1:
         other, messages[0] = lax.optimization_barrier((cotangent, messages[0]))
-        cotangents.append(exchange_near(other, "col", near))
+        cotangents.append(exchange_twin(other, "col", members))
     sums = [add(kept, got)]
-    if near > 1:
-        sums.append(exchange_near(sums[0], "col", near))
-    pre, message = own_rows(sums, weight, bias, cotangents)
+    if twins > 1:
+        sums.append(exchange_twin(sums[0], "col", members))
+    pre, message = own_rows(sums, weight, bias, cotangents, members)
     activations = activate(pre)
-    got = [message] + [exchange(message, "col", step, near) for step in range(1, far)]
-    *messages, kept = backward(got, weight, band, size, near)
-    messages = [messages[0]] + [exchange(messages[step], "row", step) for step in range(1, size)]
+    got = [message] + [exchange(message, "col", step, members) for step in range(1, members)]
+    *messages, kept = backward(got, weight, band, size, twins)
+    messages = [messages[0]] + [exchange(messages[step], "row", step, size) for step in range(1, size)]
     node_count = cotangent.shape[0] * size * owners
     grad_features, grad_weight, grad_bias = final(messages, kept, hidden, float(node_count) ** (-0.5))
     return (activations, grad_features.T, grad_weight, grad_bias.reshape(hidden))

time: 39.5 us -> 36.4 us (0.922)
  waiting for transfers between devices: 16.9 us -> 12.5 us
  starting transfers between devices: 16.9 us -> 17.8 us
    ppermute x12, waiting for transfers between devices: 14.1 us -> 10.1 us  [exchange(): return lax.ppermute(value, axis, pairs)]
    ppermute x2, starting transfers between devices: 3.04 us -> 5.62 us  [exchange_twin(): lax.ppermute(value, axis, [(i, (i + members) % size) for i in range(size)])]
    ppermute x12, starting transfers between devices: 13.9 us -> 12.2 us  [exchange(): return lax.ppermute(value, axis, pairs)]
    ppermute x2, waiting for transfers between devices: 2.78 us -> 2.38 us  [exchange_twin(): lax.ppermute(value, axis, [(i, (i + members) % size) for i in range(size)])]
  transfers between devices with their start and end apart: 14 -> 14, of which waited for: 9 -> 9; matrix products, arithmetic and copies ran while one was open for 0% -> 0% of each run, Pallas kernels for 6% -> 7%
where the time goes in v6:
time: 36.4 us; the launch traced here: 36.2 us
  starting transfers between devices  17.8 us (49%)
  waiting for transfers between devices  12.5 us (34%)
  Pallas kernels  4.55 us (12%)
  between operations  1.36 us (4%)
    ppermute x12, starting transfers between devices, exchange(): return lax.ppermute(value, axis, pairs)  12.2 us
    ppermute x12, waiting for transfers between devices, exchange(): return lax.ppermute(value, axis, pairs)  10.1 us
    ppermute x2, starting transfers between devices, exchange_twin(): lax.ppermute(value, axis, [(i, (i + members) % size) for i in range(size)])  5.62 us
    ppermute x2, waiting for transfers between devices, exchange_twin(): lax.ppermute(value, axis, [(i, (i + members) % size) for i in range(size)])  2.38 us
    pallas_call x1, Pallas kernels, make_band(): pl.pallas_call(band_kernel, out_shape=(out, struct(bias.shape, f32)), in_...  1.74 us
  transfers between devices with their start and end apart: 14, of which 9 were waited for; matrix products, arithmetic and copies ran while one was open for 0% of the time, Pallas kernels for 7%

profile of v6, /device:TPU:0, one launch (start us, length us, event | category | flops | bytes accessed | tf_op | source)
XLA Modules:
  0.0 36.2 jit_solution(7559762016201884000)
XLA Ops:
  0.6 2.5 %collective-permute-start.2 = (bf16[32,512]{1,0:T(8,128)(2,1)}, bf16[32,512]{1,0:T(8,128)(2,1)S(1)}, u32[]{:S(2)}, u32[]{:S(2)}) collective-permute-start(bf16[32,512]{1,0:T(8,128)(2,1)} %bitcast.6), channel_id=1, source_target_pairs={{0,24},{8,16},{16,8},{24,0},{1,25},{9,17},{17,9},{25,1},{2,26},{10... | collective-permute-start | bytes 98312 | tf_op jit(solution)/shard_map/ppermute | solution.py:69
  3.1 0.6 %collective-permute-start.1 = (bf16[32,512]{1,0:T(8,128)(2,1)}, bf16[32,512]{1,0:T(8,128)(2,1)S(1)}, u32[]{:S(2)}, u32[]{:S(2)}) collective-permute-start(bf16[32,512]{1,0:T(8,128)(2,1)} %bitcast.7), channel_id=1, source_target_pairs={{0,16},{8,24},{16,0},{24,8},{1,17},{9,25},{17,1},{25,9},{2,18},{10... | collective-permute-start | bytes 98312 | tf_op jit(solution)/shard_map/ppermute | solution.py:69
  3.7 0.0 collective-permute-start
  4.4 0.0 copy-start.2
  4.4 1.7 %band.1 = (bf16[512,1024]{1,0:T(8,128)(2,1)S(1)}, f32[1,128]{1,0:T(1,128)S(1)}) custom-call(s32[1,1]{1,0:T(1,128)S(6)} %copy.13.limit, s32[1,1,128]{2,1,0:T(1,128)} %rows.1, s32[1,1,128]{2,1,0:T(1,128)} %cols.1, s32[256,128]{1,0:T(8,128)} %bitcast.10, bf16[256,128]{1,0:T(8,128)(2,1)} %bitcast.11, f32[1,128]{1,0:T(1,128)} %bitcast.12), custom_call_target="tpu_custom_call" | custom-call | flops 33554432 | bytes 8388608 | tf_op jit(solution)/shard_map/band/pallas_call | solution.py:130
  6.2 0.0 collective-permute-done.2.refs_3_
  6.2 1.1 %collective-permute-done.1.refs_2_ = bf16[32,512]{1,0:T(8,128)(2,1)S(1)} collective-permute-done((bf16[32,512]{1,0:T(8,128)(2,1)}, bf16[32,512]{1,0:T(8,128)(2,1)S(1)}, u32[]{:S(2)}, u32[]{:S(2)}) %collective-permute-start.1) | collective-permute-done | bytes 32800 | tf_op jit(solution)/shard_map/ppermute | solution.py:69
  7.3 0.0 collective-permute-done.refs_1_
  7.3 0.0 copy-done.2
  7.3 0.0 copy-start.1
  7.3 0.4 %forward.1 = (f32[128,256]{1,0:T(8,128)S(1)}, bf16[128,256]{1,0:T(8,128)(2,1)S(1)}, bf16[128,256]{1,0:T(8,128)(2,1)S(1)}, bf16[128,256]{1,0:T(8,128)(2,1)S(1)}) custom-call(bf16[32,512]{1,0:T(8,128)(2,1)S(1)} %bitcast.9, bf16[32,512]{1,0:T(8,128)(2,1)S(1)} %collective-permute-done.refs_1_, bf16[32,512]{1,0:T(8,128)(2,1)S(1)} %collective-permute-done.1.refs_2_, ...), custom_call_target="tpu_custom_call" | custom-call | tf_op jit(solution)/shard_map/forward/pallas_call | solution.py:178
  7.7 1.7 %collective-permute-start.4 = (bf16[128,256]{1,0:T(8,128)(2,1)S(1)}, bf16[128,256]{1,0:T(8,128)(2,1)S(1)}, u32[]{:S(2)}, u32[]{:S(2)}) collective-permute-start(bf16[128,256]{1,0:T(8,128)(2,1)S(1)} %get-tuple-element.24), channel_id=1, source_target_pairs={{0,2},{1,3},{2,0},{3,1},{4,6},{5,7},{6,4},{7,5},{8,10},{9,11},{10,... | collective-permute-start | bytes 196616 | tf_op jit(solution)/shard_map/ppermute | solution.py:69
  9.3 1.4 %collective-permute-start.5 = (bf16[128,256]{1,0:T(8,128)(2,1)S(1)}, bf16[128,256]{1,0:T(8,128)(2,1)S(1)}, u32[]{:S(2)}, u32[]{:S(2)}) collective-permute-start(bf16[128,256]{1,0:T(8,128)(2,1)S(1)} %get-tuple-element.25), channel_id=1, source_target_pairs={{0,3},{1,2},{2,1},{3,0},{4,7},{5,6},{6,5},{7,4},{8,11},{9,10},{10,... | collective-permute-start | bytes 196616 | tf_op jit(solution)/shard_map/ppermute | solution.py:69
  10.7 0.5 %collective-permute-start.3 = (bf16[128,256]{1,0:T(8,128)(2,1)S(1)}, bf16[128,256]{1,0:T(8,128)(2,1)S(1)}, u32[]{:S(2)}, u32[]{:S(2)}) collective-permute-start(bf16[128,256]{1,0:T(8,128)(2,1)S(1)} %get-tuple-element.23), channel_id=1, source_target_pairs={{0,1},{1,0},{2,3},{3,2},{4,5},{5,4},{6,7},{7,6},{8,9},{9,8},{10,11... | collective-permute-start | bytes 196616 | tf_op jit(solution)/shard_map/ppermute | solution.py:69
  11.2 0.0 copy-done.1
  11.2 2.8 %collective-permute-start.7 = (f32[128,128]{1,0:T(8,128)S(1)}, f32[128,128]{1,0:T(8,128)S(1)}, u32[]{:S(2)}, u32[]{:S(2)}) collective-permute-start(f32[128,128]{1,0:T(8,128)S(1)} %copy-done.1), channel_id=1, source_target_pairs={{0,4},{1,5},{2,6},{3,7},{4,0},{5,1},{6,2},{7,3},{8,12},{9,13},{10,... | collective-permute-start | bytes 196616 | tf_op jit(solution)/shard_map/ppermute | solution.py:74
  14.0 0.0 collective-permute-done.4.refs_1_
  14.0 0.5 %collective-permute-done.5.refs_2_ = bf16[128,256]{1,0:T(8,128)(2,1)S(1)} collective-permute-done((bf16[128,256]{1,0:T(8,128)(2,1)S(1)}, bf16[128,256]{1,0:T(8,128)(2,1)S(1)}, u32[]{:S(2)}, u32[]{:S(2)}) %collective-permute-start.5) | collective-permute-done | bytes 65568 | tf_op jit(solution)/shard_map/ppermute | solution.py:69
  14.6 0.7 %collective-permute-done.3.refs_0_ = bf16[128,256]{1,0:T(8,128)(2,1)S(1)} collective-permute-done((bf16[128,256]{1,0:T(8,128)(2,1)S(1)}, bf16[128,256]{1,0:T(8,128)(2,1)S(1)}, u32[]{:S(2)}, u32[]{:S(2)}) %collective-permute-start.3) | collective-permute-done | bytes 65568 | tf_op jit(solution)/shard_map/ppermute | solution.py:69
  15.3 0.0 copy-start
  15.3 2.9 %collective-permute-start.6 = (bf16[128,256]{1,0:T(8,128)(2,1)S(1)}, bf16[128,256]{1,0:T(8,128)(2,1)S(1)}, u32[]{:S(2)}, u32[]{:S(2)}) collective-permute-start(bf16[128,256]{1,0:T(8,128)(2,1)S(1)} %add.1.refs_0_), channel_id=1, source_target_pairs={{0,4},{1,5},{2,6},{3,7},{4,0},{5,1},{6,2},{7,3},{8,12},{9,13},{10,... | collective-permute-start | bytes 196616 | tf_op jit(solution)/shard_map/ppermute | solution.py:74
  18.2 0.0 collective-permute-done.7.refs_5_
  18.2 2.4 %collective-permute-done.6.refs_1_ = bf16[128,256]{1,0:T(8,128)(2,1)S(1)} collective-permute-done((bf16[128,256]{1,0:T(8,128)(2,1)S(1)}, bf16[128,256]{1,0:T(8,128)(2,1)S(1)}, u32[]{:S(2)}, u32[]{:S(2)}) %collective-permute-start.6) | collective-permute-done | bytes 65568 | tf_op jit(solution)/shard_map/ppermute | solution.py:74
  20.5 0.0 copy-done
  20.5 0.4 %own_rows.1 = (f32[128,128]{1,0:T(8,128)S(1)}, bf16[384,128]{1,0:T(8,128)(2,1)S(1)}) custom-call(bf16[128,256]{1,0:T(8,128)(2,1)S(1)} %add.1.refs_0_, bf16[128,256]{1,0:T(8,128)(2,1)S(1)} %collective-permute-done.6.refs_1_, bf16[128,128]{1,0:T(8,128)(2,1)S(1)} %copy-done, f32[1,128]{1,0:T(1,128)S(1)} %get-tuple-element.26.refs_3_, f32[128,128]{1,0:T(8,128)S(1)} %copy-done.1, ...), custom_call_target="tpu_custom_call" | custom-call | tf_op jit(solution)/shard_map/own_rows/pallas_call | solution.py:242
  21.0 1.6 %collective-permute-start.10 = (bf16[384,128]{1,0:T(8,128)(2,1)S(1)}, bf16[384,128]{1,0:T(8,128)(2,1)S(1)}, u32[]{:S(2)}, u32[]{:S(2)}) collective-permute-start(bf16[384,128]{1,0:T(8,128)(2,1)S(1)} %get-tuple-element.29.refs_0_), channel_id=1, source_target_pairs={{0,3},{1,2},{2,1},{3,0},{4,7},{5,6},{6,5},{7,4},{8,11},{9,10},{10,... | collective-permute-start | bytes 294920 | tf_op jit(solution)/shard_map/ppermute | solution.py:69
  22.6 1.9 %collective-permute-start.9 = (bf16[384,128]{1,0:T(8,128)(2,1)S(1)}, bf16[384,128]{1,0:T(8,128)(2,1)S(1)}, u32[]{:S(2)}, u32[]{:S(2)}) collective-permute-start(bf16[384,128]{1,0:T(8,128)(2,1)S(1)} %get-tuple-element.29.refs_0_), channel_id=1, source_target_pairs={{0,2},{1,3},{2,0},{3,1},{4,6},{5,7},{6,4},{7,5},{8,10},{9,11},{10,... | collective-permute-start | bytes 294920 | tf_op jit(solution)/shard_map/ppermute | solution.py:69
  24.5 0.0 collective-permute-start.8
  24.5 2.1 %collective-permute-done.10.refs_3_ = bf16[384,128]{1,0:T(8,128)(2,1)S(1)} collective-permute-done((bf16[384,128]{1,0:T(8,128)(2,1)S(1)}, bf16[384,128]{1,0:T(8,128)(2,1)S(1)}, u32[]{:S(2)}, u32[]{:S(2)}) %collective-permute-start.10) | collective-permute-done | bytes 98336 | tf_op jit(solution)/shard_map/ppermute | solution.py:69
  26.6 1.6 %collective-permute-done.9.refs_2_ = bf16[384,128]{1,0:T(8,128)(2,1)S(1)} collective-permute-done((bf16[384,128]{1,0:T(8,128)(2,1)S(1)}, bf16[384,128]{1,0:T(8,128)(2,1)S(1)}, u32[]{:S(2)}, u32[]{:S(2)}) %collective-permute-start.9) | collective-permute-done | bytes 98336 | tf_op jit(solution)/shard_map/ppermute | solution.py:69
  28.2 1.0 %collective-permute-done.8.refs_1_ = bf16[384,128]{1,0:T(8,128)(2,1)S(1)} collective-permute-done((bf16[384,128]{1,0:T(8,128)(2,1)S(1)}, bf16[384,128]{1,0:T(8,128)(2,1)S(1)}, u32[]{:S(2)}, u32[]{:S(2)}) %collective-permute-start.8) | collective-permute-done | bytes 98336 | tf_op jit(solution)/shard_map/ppermute | solution.py:69
  29.1 0.6 %backward.1 = (bf16[272,128]{1,0:T(8,128)(2,1)S(1)}, bf16[272,128]{1,0:T(8,128)(2,1)S(1)}, bf16[272,128]{1,0:T(8,128)(2,1)S(1)}, bf16[272,128]{1,0:T(8,128)(2,1)S(1)}, f32[32,512]{1,0:T(8,128)S(1)}) custom-call(bf16[384,128]{1,0:T(8,128)(2,1)S(1)} %get-tuple-element.29.refs_0_, bf16[384,128]{1,0:T(8,128)(2,1)S(1)} %collective-permute-done.8.refs_1_, ...), custom_call_target="tpu_custom_call" | custom-call | tf_op jit(solution)/shard_map/backward/pallas_call | solution.py:312
  29.8 0.1 collective-permute-start.11
  29.9 1.2 %collective-permute-start.12 = (bf16[272,128]{1,0:T(8,128)(2,1)S(1)}, bf16[272,128]{1,0:T(8,128)(2,1)S(1)}, u32[]{:S(2)}, u32[]{:S(2)}) collective-permute-start(bf16[272,128]{1,0:T(8,128)(2,1)S(1)} %get-tuple-element.32), channel_id=1, source_target_pairs={{0,16},{8,24},{16,0},{24,8},{1,17},{9,25},{17,1},{25,9},{2,18},{10... | collective-permute-start | bytes 208904 | tf_op jit(solution)/shard_map/ppermute | solution.py:69
  31.0 0.7 %collective-permute-start.13 = (bf16[272,128]{1,0:T(8,128)(2,1)S(1)}, bf16[272,128]{1,0:T(8,128)(2,1)S(1)}, u32[]{:S(2)}, u32[]{:S(2)}) collective-permute-start(bf16[272,128]{1,0:T(8,128)(2,1)S(1)} %get-tuple-element.33), channel_id=1, source_target_pairs={{0,24},{8,16},{16,8},{24,0},{1,25},{9,17},{17,9},{25,1},{2,26},{10... | collective-permute-start | bytes 208904 | tf_op jit(solution)/shard_map/ppermute | solution.py:69
  31.7 0.6 %activate.1 = f32[128,128]{1,0:T(8,128)} custom-call(f32[128,128]{1,0:T(8,128)S(1)} %get-tuple-element.28.pre), custom_call_target="tpu_custom_call" | custom-call | tf_op jit(solution)/shard_map/activate/pallas_call | solution.py:258
  32.4 0.0 collective-permute-done.11.refs_1_
  32.4 2.5 %collective-permute-done.12.refs_2_ = bf16[272,128]{1,0:T(8,128)(2,1)S(1)} collective-permute-done((bf16[272,128]{1,0:T(8,128)(2,1)S(1)}, bf16[272,128]{1,0:T(8,128)(2,1)S(1)}, u32[]{:S(2)}, u32[]{:S(2)}) %collective-permute-start.12) | collective-permute-done | bytes 69664 | tf_op jit(solution)/shard_map/ppermute | solution.py:69
  34.9 0.6 %collective-permute-done.13.refs_3_ = bf16[272,128]{1,0:T(8,128)(2,1)S(1)} collective-permute-done((bf16[272,128]{1,0:T(8,128)(2,1)S(1)}, bf16[272,128]{1,0:T(8,128)(2,1)S(1)}, u32[]{:S(2)}, u32[]{:S(2)}) %collective-permute-start.13) | collective-permute-done | bytes 69664 | tf_op jit(solution)/shard_map/ppermute | solution.py:69
  35.5 0.7 %final.1 = (bf16[32,512]{1,0:T(8,128)(2,1)}, f32[128,128]{1,0:T(8,128)}, f32[1,128]{1,0:T(1,128)}) custom-call(bf16[272,128]{1,0:T(8,128)(2,1)S(1)} %get-tuple-element.30.refs_0_, bf16[272,128]{1,0:T(8,128)(2,1)S(1)} %collective-permute-done.11.refs_1_, bf16[272,128]{1,0:T(8,128)(2,1)S(1)} %collective-permute-done.12.refs_2_, ...), custom_call_target="tpu_custom_call" | custom-call | tf_op jit(solution)/shard_map/final/pallas_call | solution.py:353
  (1 shorter events, 0.0 us)
Async XLA Ops:
  0.6 5.6 %collective-permute-start.2 = (bf16[32,512]{1,0:T(8,128)(2,1)}, bf16[32,512]{1,0:T(8,128)(2,1)S(1)}, u32[]{:S(2)}, u32[]{:S(2)}) collective-permute-start(bf16[32,512]{1,0:T(8,128)(2,1)} %bitcast.6), channel_id=1, source_target_pairs={{0,24},{8,16},{16,8},{24,0},{1,25},{9,17},{17,9},{25,1},{2,26},{10... | collective-permute-start | bytes 98312 | tf_op jit(solution)/shard_map/ppermute | solution.py:69
  3.1 4.2 %collective-permute-start.1 = (bf16[32,512]{1,0:T(8,128)(2,1)}, bf16[32,512]{1,0:T(8,128)(2,1)S(1)}, u32[]{:S(2)}, u32[]{:S(2)}) collective-permute-start(bf16[32,512]{1,0:T(8,128)(2,1)} %bitcast.7), channel_id=1, source_target_pairs={{0,16},{8,24},{16,0},{24,8},{1,17},{9,25},{17,1},{25,9},{2,18},{10... | collective-permute-start | bytes 98312 | tf_op jit(solution)/shard_map/ppermute | solution.py:69
  3.7 3.5 %collective-permute-start = (bf16[32,512]{1,0:T(8,128)(2,1)}, bf16[32,512]{1,0:T(8,128)(2,1)S(1)}, u32[]{:S(2)}, u32[]{:S(2)}) collective-permute-start(bf16[32,512]{1,0:T(8,128)(2,1)} %bitcast.8), channel_id=1, source_target_pairs={{0,8},{8,0},{16,24},{24,16},{1,9},{9,1},{17,25},{25,17},{2,10},{10... | collective-permute-start | bytes 98312 | tf_op jit(solution)/shard_map/ppermute | solution.py:69
  4.4 2.9 %copy-start.2 = (bf16[512,32]{0,1:T(8,128)(2,1)S(1)}, bf16[512,32]{0,1:T(8,128)(2,1)}, u32[]{:S(2)}) copy-start(bf16[512,32]{0,1:T(8,128)(2,1)} %param.9) | copy-start | bytes 98308
  7.3 3.9 %copy-start.1 = (f32[128,128]{1,0:T(8,128)S(1)}, f32[128,128]{1,0:T(8,128)}, u32[]{:S(2)}) copy-start(f32[128,128]{1,0:T(8,128)} %refs_4_.2) | copy-start | bytes 196612
  7.7 6.3 %collective-permute-start.4 = (bf16[128,256]{1,0:T(8,128)(2,1)S(1)}, bf16[128,256]{1,0:T(8,128)(2,1)S(1)}, u32[]{:S(2)}, u32[]{:S(2)}) collective-permute-start(bf16[128,256]{1,0:T(8,128)(2,1)S(1)} %get-tuple-element.24), channel_id=1, source_target_pairs={{0,2},{1,3},{2,0},{3,1},{4,6},{5,7},{6,4},{7,5},{8,10},{9,11},{10,... | collective-permute-start | bytes 196616 | tf_op jit(solution)/shard_map/ppermute | solution.py:69
  9.3 5.2 %collective-permute-start.5 = (bf16[128,256]{1,0:T(8,128)(2,1)S(1)}, bf16[128,256]{1,0:T(8,128)(2,1)S(1)}, u32[]{:S(2)}, u32[]{:S(2)}) collective-permute-start(bf16[128,256]{1,0:T(8,128)(2,1)S(1)} %get-tuple-element.25), channel_id=1, source_target_pairs={{0,3},{1,2},{2,1},{3,0},{4,7},{5,6},{6,5},{7,4},{8,11},{9,10},{10,... | collective-permute-start | bytes 196616 | tf_op jit(solution)/shard_map/ppermute | solution.py:69
  10.7 4.6 %collective-permute-start.3 = (bf16[128,256]{1,0:T(8,128)(2,1)S(1)}, bf16[128,256]{1,0:T(8,128)(2,1)S(1)}, u32[]{:S(2)}, u32[]{:S(2)}) collective-permute-start(bf16[128,256]{1,0:T(8,128)(2,1)S(1)} %get-tuple-element.23), channel_id=1, source_target_pairs={{0,1},{1,0},{2,3},{3,2},{4,5},{5,4},{6,7},{7,6},{8,9},{9,8},{10,11... | collective-permute-start | bytes 196616 | tf_op jit(solution)/shard_map/ppermute | solution.py:69
  11.2 6.9 %collective-permute-start.7 = (f32[128,128]{1,0:T(8,128)S(1)}, f32[128,128]{1,0:T(8,128)S(1)}, u32[]{:S(2)}, u32[]{:S(2)}) collective-permute-start(f32[128,128]{1,0:T(8,128)S(1)} %copy-done.1), channel_id=1, source_target_pairs={{0,4},{1,5},{2,6},{3,7},{4,0},{5,1},{6,2},{7,3},{8,12},{9,13},{10,... | collective-permute-start | bytes 196616 | tf_op jit(solution)/shard_map/ppermute | solution.py:74
  15.3 5.3 %copy-start = (bf16[128,128]{1,0:T(8,128)(2,1)S(1)}, bf16[128,128]{1,0:T(8,128)(2,1)}, u32[]{:S(2)}) copy-start(bf16[128,128]{1,0:T(8,128)(2,1)} %refs_4_.3) | copy-start | bytes 98308
  15.3 5.2 %collective-permute-start.6 = (bf16[128,256]{1,0:T(8,128)(2,1)S(1)}, bf16[128,256]{1,0:T(8,128)(2,1)S(1)}, u32[]{:S(2)}, u32[]{:S(2)}) collective-permute-start(bf16[128,256]{1,0:T(8,128)(2,1)S(1)} %add.1.refs_0_), channel_id=1, source_target_pairs={{0,4},{1,5},{2,6},{3,7},{4,0},{5,1},{6,2},{7,3},{8,12},{9,13},{10,... | collective-permute-start | bytes 196616 | tf_op jit(solution)/shard_map/ppermute | solution.py:74
  21.0 5.6 %collective-permute-start.10 = (bf16[384,128]{1,0:T(8,128)(2,1)S(1)}, bf16[384,128]{1,0:T(8,128)(2,1)S(1)}, u32[]{:S(2)}, u32[]{:S(2)}) collective-permute-start(bf16[384,128]{1,0:T(8,128)(2,1)S(1)} %get-tuple-element.29.refs_0_), channel_id=1, source_target_pairs={{0,3},{1,2},{2,1},{3,0},{4,7},{5,6},{6,5},{7,4},{8,11},{9,10},{10,... | collective-permute-start | bytes 294920 | tf_op jit(solution)/shard_map/ppermute | solution.py:69
  22.6 5.6 %collective-permute-start.9 = (bf16[384,128]{1,0:T(8,128)(2,1)S(1)}, bf16[384,128]{1,0:T(8,128)(2,1)S(1)}, u32[]{:S(2)}, u32[]{:S(2)}) collective-permute-start(bf16[384,128]{1,0:T(8,128)(2,1)S(1)} %get-tuple-element.29.refs_0_), channel_id=1, source_target_pairs={{0,2},{1,3},{2,0},{3,1},{4,6},{5,7},{6,4},{7,5},{8,10},{9,11},{10,... | collective-permute-start | bytes 294920 | tf_op jit(solution)/shard_map/ppermute | solution.py:69
  24.5 4.6 %collective-permute-start.8 = (bf16[384,128]{1,0:T(8,128)(2,1)S(1)}, bf16[384,128]{1,0:T(8,128)(2,1)S(1)}, u32[]{:S(2)}, u32[]{:S(2)}) collective-permute-start(bf16[384,128]{1,0:T(8,128)(2,1)S(1)} %get-tuple-element.29.refs_0_), channel_id=1, source_target_pairs={{0,1},{1,0},{2,3},{3,2},{4,5},{5,4},{6,7},{7,6},{8,9},{9,8},{10,11... | collective-permute-start | bytes 294920 | tf_op jit(solution)/shard_map/ppermute | solution.py:69
  29.8 2.6 %collective-permute-start.11 = (bf16[272,128]{1,0:T(8,128)(2,1)S(1)}, bf16[272,128]{1,0:T(8,128)(2,1)S(1)}, u32[]{:S(2)}, u32[]{:S(2)}) collective-permute-start(bf16[272,128]{1,0:T(8,128)(2,1)S(1)} %get-tuple-element.31), channel_id=1, source_target_pairs={{0,8},{8,0},{16,24},{24,16},{1,9},{9,1},{17,25},{25,17},{2,10},{10... | collective-permute-start | bytes 208904 | tf_op jit(solution)/shard_map/ppermute | solution.py:69
  29.9 5.0 %collective-permute-start.12 = (bf16[272,128]{1,0:T(8,128)(2,1)S(1)}, bf16[272,128]{1,0:T(8,128)(2,1)S(1)}, u32[]{:S(2)}, u32[]{:S(2)}) collective-permute-start(bf16[272,128]{1,0:T(8,128)(2,1)S(1)} %get-tuple-element.32), channel_id=1, source_target_pairs={{0,16},{8,24},{16,0},{24,8},{1,17},{9,25},{17,1},{25,9},{2,18},{10... | collective-permute-start | bytes 208904 | tf_op jit(solution)/shard_map/ppermute | solution.py:69
  31.0 4.5 %collective-permute-start.13 = (bf16[272,128]{1,0:T(8,128)(2,1)S(1)}, bf16[272,128]{1,0:T(8,128)(2,1)S(1)}, u32[]{:S(2)}, u32[]{:S(2)}) collective-permute-start(bf16[272,128]{1,0:T(8,128)(2,1)S(1)} %get-tuple-element.33), channel_id=1, source_target_pairs={{0,24},{8,16},{16,8},{24,0},{1,25},{9,17},{17,9},{25,1},{2,26},{10... | collective-permute-start | bytes 208904 | tf_op jit(solution)/shard_map/ppermute | solution.py:69

commit v7 on v6

--- a/solution.py
+++ b/solution.py
@@ -74,7 +74,7 @@
     return lax.ppermute(value, axis, [(i, (i + members) % size) for i in range(size)])
 
 
-def band_kernel(limit, rows, cols, ids, values, bias, band, bias_out, sums, scaled, here, row, col, sems):
+def band_kernel(place, limit, rows, cols, ids, values, bias, band, bias_out, sums, scaled, here, row, col, sems):
     blocks, tile, _ = sums.shape
     row_blocks = band.shape[1] // tile
     slots = rows.shape[-1]
@@ -113,13 +113,19 @@
     lax.fori_loop(0, (limit[0, 0] + several - 1) // several, group, 0)
 
     def put(index):
-        c, r = index // row_blocks, index % row_blocks
+        c, r = index // row_blocks, place(index % row_blocks)
         band[pl.ds(start_of(c, tile), tile), pl.ds(start_of(r, tile), tile)] = sums[index].astype(bf16)
 
     each(blocks, put)
 
 
-def make_band(limit, rows, cols, ids, values, bias, row_blocks, col_blocks):
+def make_band(limit, rows, cols, ids, values, bias, row_blocks, col_blocks, members, twins):
+    blocks_own = row_blocks // (members * twins)
+
+    def place(block):
+        owner = block // blocks_own
+        return (owner % members * twins + owner // members) * blocks_own + block % blocks_own
+
     tile = ids.shape[-1]
     lines = ids.shape[-3] * ids.shape[-2]
     ids = ids.reshape(lines, tile)
@@ -128,7 +134,7 @@
     out = struct((col_blocks * tile, row_blocks * tile), bf16)
     sums = struct((col_blocks * row_blocks, tile, tile), f32)
     return pl.pallas_call(
-        band_kernel,
+        functools.partial(band_kernel, place),
         out_shape=(out, struct(bias.shape, f32)),
         in_specs=[smem()] + [pl.BlockSpec(memory_space=pltpu.HBM)] * 5,
         out_specs=(vmem(), vmem()),
@@ -146,11 +152,11 @@
     )(limit, *[pltpu.with_memory_space_constraint(a, pltpu.HBM) for a in (rows, cols, ids, values, bias)])
 
 
-def forward_kernel(size, members, *refs):
+def forward_kernel(size, *refs):
     parts, (band, kept), messages, (panel, sums) = refs[:size], refs[size : size + 2], refs[size + 2 : -2], refs[-2:]
     me = lax.axis_index("row")
+    members, _, own = sums.shape
     mine = lax.rem(lax.axis_index("col"), members)
-    owners, _, own = sums.shape
     width = parts[0].shape[0]
     for step, part in enumerate(parts):
         slot = pl.multiple_of(source(me, step, size) * width, width)
@@ -164,19 +170,18 @@
             sums[index * (many // own) + part] = got[:, part * own : (part + 1) * own]
 
     each(band.shape[1] // many, piece)
-    for step, message in enumerate((kept,) + messages):
-        place = partner(mine, step, members)
-        for twin in range(owners // members):
-            message[:, twin * own : (twin + 1) * own] = sums[place + twin * members].astype(message.dtype)
-
-
-def forward(parts, band, owners, members):
+    kept[...] = sums[mine]
+    for step, message in enumerate(messages):
+        message[...] = sums[partner(mine, step + 1, members)].astype(bf16)
+
+
+def forward(parts, band, members):
     hidden = parts[0].shape[0] * len(parts)
     nodes, total = band.shape
     block = (hidden, total // members)
-    sums = struct((owners, hidden, total // owners), f32)
-    return pl.pallas_call(
-        functools.partial(forward_kernel, len(parts), members),
+    sums = struct((members,) + block, f32)
+    return pl.pallas_call(
+        functools.partial(forward_kernel, len(parts)),
         out_shape=(struct(block, f32),) + (struct(block, bf16),) * (members - 1),
         in_specs=[vmem()] * (len(parts) + 1),
         out_specs=(vmem(),) * members,
@@ -211,43 +216,59 @@
     return jnp.where(row == 0, high, jnp.where(row == 1, line - high, 0.0))
 
 
+def apply_kernel(sums, weight, out):
+    out[...] = dot(sums[...], weight[...], 0, 0)
+
+
+def apply_weight(sums, weight):
+    return pl.pallas_call(
+        apply_kernel,
+        out_shape=struct((sums.shape[1], weight.shape[1]), f32),
+        in_specs=[vmem()] * 2,
+        out_specs=vmem(),
+        compiler_params=room(sums),
+        name="apply_weight",
+    )(sums, weight)
+
+
 def own_kernel(members, twins, *refs):
-    sums, (weight, bias), cotangents = refs[:twins], refs[twins : twins + 2], refs[twins + 2 : 2 * twins + 2]
-    pre_out, message, wide_pre, given = refs[2 * twins + 2 :]
+    sums, (weight, bias, first), cotangents = refs[:twins], refs[twins : twins + 3], refs[twins + 3 : 2 * twins + 3]
+    pre_out, message, wide_pre, given = refs[2 * twins + 3 :]
     mine = lax.axis_index("col") // members
     own = cotangents[0].shape[0]
-    total = sums[0][...].astype(f32)
-    for part in sums[1:]:
-        total = total + part[...].astype(f32)
     for index, part in enumerate(cotangents):
         place = mine if index == 0 else twins - 1 - mine
         given[pl.ds(pl.multiple_of(place * own, own), own), :] = part[...]
-    high = total.astype(bf16)
-    low = (total - high.astype(f32)).astype(bf16)
-    pre = dot(high, weight[...], 0, 0) + dot(low, weight[...], 0, 0) + bias[...]
+    pre = first[...]
+    for part in sums[1:]:
+        pre = pre + dot(part[...], weight[...], 0, 0)
+    pre = pre + bias[...]
     wide_pre[...] = pre
     squashed = jax.nn.sigmoid(pre)
     grad = given[...] * squashed * (1.0 + pre * (1.0 - squashed))
     grad = grad.astype(bf16)
     rows = grad.shape[0]
     message[:rows, :] = grad
-    message[rows:, :] = (dot(high, grad) + dot(low, grad)).astype(bf16)
+    weight_part = dot(sums[0][...], grad)
+    for part in sums[1:]:
+        weight_part = weight_part + dot(part[...], grad)
+    message[rows:, :] = weight_part.astype(bf16)
     pre_out[...] = wide_pre[pl.ds(pl.multiple_of(mine * own, own), own), :]
 
 
-def own_rows(sums, weight, bias, cotangents, members):
+def own_rows(sums, weight, bias, first, cotangents, members):
     twins = len(sums)
     hidden, rows = sums[0].shape
     own = cotangents[0].shape[0]
     return pl.pallas_call(
         functools.partial(own_kernel, members, twins),
         out_shape=(struct((own, hidden), f32), struct((rows + hidden, hidden), bf16)),
-        in_specs=[vmem()] * (2 * twins + 2),
+        in_specs=[vmem()] * (2 * twins + 3),
         out_specs=(vmem(),) * 2,
         scratch_shapes=[pltpu.VMEM((rows, hidden), f32), pltpu.VMEM((rows, hidden), f32)],
         compiler_params=room(*sums),
         name="own_rows",
-    )(*sums, weight, bias, *cotangents)
+    )(*sums, weight, bias, first, *cotangents)
 
 
 def activate_kernel(pre, act):
@@ -265,34 +286,51 @@
     )(pre)
 
 
-def backward_kernel(size, members, twins, *refs):
-    got, (weight, band), messages = refs[:members], refs[members : members + 2], refs[members + 2 : members + 2 + size]
-    kept, rows, slots, back, grads, packed = refs[members + 2 + size :]
+def group_of(members):
+    return 2 if members % 2 == 0 and members & (members - 1) == 0 else 1
+
+
+def group_product(parts, first, weight, band, rows, mine, members):
+    group = len(parts)
+    own = rows.shape[0] // group
+    base = source(mine, first, members) // group * group
+    for index, part in enumerate(parts):
+        spot = pl.multiple_of((source(mine, first + index, members) - base) * own, own)
+        rows[pl.ds(spot, own), :] = part[:own, :]
+    back = dot(weight[...], rows[...], 1, 1).astype(bf16)
+    wide_own = group * own
+    return dot(back, band[:, pl.ds(pl.multiple_of(base * own, wide_own), wide_own)], 1, 1)
+
+
+def early_kernel(group, members, *refs):
+    parts, (weight, band, out, rows) = refs[:group], refs[group:]
+    mine = lax.rem(lax.axis_index("col"), members)
+    out[...] = group_product(parts, 0, weight, band, rows, mine, members)
+
+
+def backward_kernel(size, group, members, *refs):
+    got, (weight, band, early), messages = refs[:members], refs[members : members + 3], refs[members + 3 :][:size]
+    kept, rows, slots, lines, grads, packed = refs[members + 3 + size :]
     hidden = weight.shape[0]
-    own = rows.shape[0] // (members * twins)
+    own = got[0].shape[0] - hidden
     width, nodes = kept.shape
     me = lax.axis_index("row")
     mine = lax.rem(lax.axis_index("col"), members)
     for step, part in enumerate(got):
         place = source(mine, step, members)
-        for twin in range(twins):
-            spot = pl.multiple_of((place + twin * members) * own, own)
-            rows[pl.ds(spot, own), :] = part[twin * own : (twin + 1) * own, :]
-        slots[place] = part[twins * own :, :].astype(f32)
-    weight_part = slots[0]
+        slots[place] = part[own:, :].astype(f32)
+        lines[place] = jnp.sum(part[:own, :].astype(f32), axis=0, keepdims=True)
+    weight_part, bias_part = slots[0], lines[0]
     for index in range(1, members):
         weight_part = weight_part + slots[index]
-    back[...] = dot(weight[...], rows[...], 1, 1).astype(bf16)
-    many = min(wide, nodes)
-
-    def piece(index):
-        place = pl.ds(start_of(index, many), many)
-        grads[:, place] = dot(back[...], band[place, :], 1, 1)
-
-    each(nodes // many, piece)
+        bias_part = bias_part + lines[index]
+    total = early[...]
+    for first in range(group, members, group):
+        total = total + group_product(got[first : first + group], first, weight, band, rows, mine, members)
+    grads[...] = total
     split = nodes // hidden
     packed[split * width : split * width + hidden, :] = weight_part
-    packed[split * width + hidden :, :] = pair_rows(jnp.sum(rows[...].astype(f32), axis=0, keepdims=True))
+    packed[split * width + hidden :, :] = pair_rows(bias_part)
     for step in range(size):
         slot = pl.multiple_of(partner(me, step, size) * width, width)
         block = grads[pl.ds(slot, width), :]
@@ -303,27 +341,38 @@
         messages[step][...] = packed[...].astype(bf16)
 
 
-def backward(got, weight, band, size, twins):
+def backward(got, weight, band, size):
     members = len(got)
+    group = group_of(members)
     hidden = weight.shape[0]
     nodes, total = band.shape
     width = hidden // size
+    rows = pltpu.VMEM((total // members * group, hidden), bf16)
+    early = pl.pallas_call(
+        functools.partial(early_kernel, group, members),
+        out_shape=struct((hidden, nodes), f32),
+        in_specs=[vmem()] * (group + 2),
+        out_specs=vmem(),
+        scratch_shapes=[rows],
+        compiler_params=room(band, *got),
+        name="early",
+    )(*got[:group], weight, band)
     message = struct((width * (nodes // hidden) + hidden + tail, hidden), bf16)
     return pl.pallas_call(
-        functools.partial(backward_kernel, size, members, twins),
+        functools.partial(backward_kernel, size, group, members),
         out_shape=(message,) * size + (struct((width, nodes), f32),),
-        in_specs=[vmem()] * (members + 2),
+        in_specs=[vmem()] * (members + 3),
         out_specs=(vmem(),) * (size + 1),
         scratch_shapes=[
-            pltpu.VMEM((total, hidden), bf16),
+            rows,
             pltpu.VMEM((members, hidden, hidden), f32),
-            pltpu.VMEM((hidden, total), bf16),
+            pltpu.VMEM((members, 1, hidden), f32),
             pltpu.VMEM((hidden, nodes), f32),
             pltpu.VMEM(message.shape, f32),
         ],
         compiler_params=room(band, *got),
         name="backward",
-    )(*got, weight, band)
+    )(*got, weight, band, early)
 
 
 def final_kernel(size, shrink, *refs):
@@ -383,9 +432,9 @@
     turned = features.T
     parts = [turned] + [exchange(turned, "row", step, size) for step in range(1, size)]
     band, bias = make_band(
-        tile_count, tile_rows, tile_cols, neighbours, edge_weights, bias_vector, row_blocks, col_blocks
+        tile_count, tile_rows, tile_cols, neighbours, edge_weights, bias_vector, row_blocks, col_blocks, members, twins
     )
-    kept, *messages = forward(parts, band, owners, members)
+    kept, *messages = forward(parts, band, members)
     got = [exchange(message, "col", step + 1, members) for step, message in enumerate(messages)]
     cotangents = [cotangent]
     if twins > 1:
@@ -394,10 +443,11 @@
     sums = [add(kept, got)]
     if twins > 1:
         sums.append(exchange_twin(sums[0], "col", members))
-    pre, message = own_rows(sums, weight, bias, cotangents, members)
+    first = apply_weight(sums[0], weight)
+    pre, message = own_rows(sums, weight, bias, first, cotangents, members)
     activations = activate(pre)
     got = [message] + [exchange(message, "col", step, members) for step in range(1, members)]
-    *messages, kept = backward(got, weight, band, size, twins)
+    *messages, kept = backward(got, weight, band, size)
     messages = [messages[0]] + [exchange(messages[step], "row", step, size) for step in range(1, size)]
     node_count = cotangent.shape[0] * size * owners
     grad_features, grad_weight, grad_bias = final(messages, kept, hidden, float(node_count) ** (-0.5))

time: 36.4 us -> 35.6 us (0.978)
  waiting for transfers between devices: 12.5 us -> 11.5 us
    ppermute x12, waiting for transfers between devices: 10.1 us -> 9.32 us  [exchange(): return lax.ppermute(value, axis, pairs)]
    pallas_call x3 -> x5, Pallas kernels: 2.74 us -> 3.13 us  [the longest x1 1.74 us: make_band(): pl.pallas_call(functools.partial(band_kernel, place), out_shape=(out, str...]
  transfers between devices with their start and end apart: 14 -> 14, of which waited for: 9 -> 8; matrix products, arithmetic and copies ran while one was open for 0% -> 0% of each run, Pallas kernels for 7% -> 8%
where the time goes in v7:
time: 35.6 us; the launch traced here: 35.5 us
  starting transfers between devices  17.7 us (50%)
  waiting for transfers between devices  11.5 us (32%)
  Pallas kernels  4.88 us (14%)
  between operations  1.38 us (4%)
    ppermute x12, starting transfers between devices, exchange(): return lax.ppermute(value, axis, pairs)  12.3 us
    ppermute x12, waiting for transfers between devices, exchange(): return lax.ppermute(value, axis, pairs)  9.32 us
    ppermute x2, starting transfers between devices, exchange_twin(): lax.ppermute(value, axis, [(i, (i + members) % size) for i in range(size)])  5.45 us
    ppermute x2, waiting for transfers between devices, exchange_twin(): lax.ppermute(value, axis, [(i, (i + members) % size) for i in range(size)])  2.18 us
    pallas_call x1, Pallas kernels, make_band(): pl.pallas_call(functools.partial(band_kernel, place), out_shape=(out, str...  1.74 us
  transfers between devices with their start and end apart: 14, of which 8 were waited for; matrix products, arithmetic and copies ran while one was open for 0% of the time, Pallas kernels for 8%

profile of v7, /device:TPU:0, one launch (start us, length us, event | category | flops | bytes accessed | tf_op | source)
XLA Modules:
  0.0 35.5 jit_solution(7338525473439375069)
XLA Ops:
  0.6 2.5 %collective-permute-start.2 = (bf16[32,512]{1,0:T(8,128)(2,1)}, bf16[32,512]{1,0:T(8,128)(2,1)S(1)}, u32[]{:S(2)}, u32[]{:S(2)}) collective-permute-start(bf16[32,512]{1,0:T(8,128)(2,1)} %bitcast.6), channel_id=1, source_target_pairs={{0,24},{8,16},{16,8},{24,0},{1,25},{9,17},{17,9},{25,1},{2,26},{10... | collective-permute-start | bytes 98312 | tf_op jit(solution)/shard_map/ppermute | solution.py:69
  3.1 0.6 %collective-permute-start.1 = (bf16[32,512]{1,0:T(8,128)(2,1)}, bf16[32,512]{1,0:T(8,128)(2,1)S(1)}, u32[]{:S(2)}, u32[]{:S(2)}) collective-permute-start(bf16[32,512]{1,0:T(8,128)(2,1)} %bitcast.7), channel_id=1, source_target_pairs={{0,16},{8,24},{16,0},{24,8},{1,17},{9,25},{17,1},{25,9},{2,18},{10... | collective-permute-start | bytes 98312 | tf_op jit(solution)/shard_map/ppermute | solution.py:69
  3.7 0.0 collective-permute-start
  4.4 0.0 copy-start.2
  4.4 1.7 %band.1 = (bf16[512,1024]{1,0:T(8,128)(2,1)S(1)}, f32[1,128]{1,0:T(1,128)S(1)}) custom-call(s32[1,1]{1,0:T(1,128)S(6)} %copy.13.limit, s32[1,1,128]{2,1,0:T(1,128)} %rows.1, s32[1,1,128]{2,1,0:T(1,128)} %cols.1, s32[256,128]{1,0:T(8,128)} %bitcast.10, bf16[256,128]{1,0:T(8,128)(2,1)} %bitcast.11, f32[1,128]{1,0:T(1,128)} %bitcast.12), custom_call_target="tpu_custom_call" | custom-call | flops 33554432 | bytes 8388608 | tf_op jit(solution)/shard_map/band/pallas_call | solution.py:136
  6.2 0.0 collective-permute-done.2.refs_3_
  6.2 1.1 %collective-permute-done.1.refs_2_ = bf16[32,512]{1,0:T(8,128)(2,1)S(1)} collective-permute-done((bf16[32,512]{1,0:T(8,128)(2,1)}, bf16[32,512]{1,0:T(8,128)(2,1)S(1)}, u32[]{:S(2)}, u32[]{:S(2)}) %collective-permute-start.1) | collective-permute-done | bytes 32800 | tf_op jit(solution)/shard_map/ppermute | solution.py:69
  7.3 0.0 collective-permute-done.refs_1_
  7.3 0.0 copy-done.2
  7.3 0.0 copy-start.1
  7.3 0.4 %forward.1 = (f32[128,256]{1,0:T(8,128)S(1)}, bf16[128,256]{1,0:T(8,128)(2,1)S(1)}, bf16[128,256]{1,0:T(8,128)(2,1)S(1)}, bf16[128,256]{1,0:T(8,128)(2,1)S(1)}) custom-call(bf16[32,512]{1,0:T(8,128)(2,1)S(1)} %bitcast.9, bf16[32,512]{1,0:T(8,128)(2,1)S(1)} %collective-permute-done.refs_1_, bf16[32,512]{1,0:T(8,128)(2,1)S(1)} %collective-permute-done.1.refs_2_, ...), custom_call_target="tpu_custom_call" | custom-call | tf_op jit(solution)/shard_map/forward/pallas_call | solution.py:183
  7.7 1.6 %collective-permute-start.4 = (bf16[128,256]{1,0:T(8,128)(2,1)S(1)}, bf16[128,256]{1,0:T(8,128)(2,1)S(1)}, u32[]{:S(2)}, u32[]{:S(2)}) collective-permute-start(bf16[128,256]{1,0:T(8,128)(2,1)S(1)} %get-tuple-element.24), channel_id=1, source_target_pairs={{0,2},{1,3},{2,0},{3,1},{4,6},{5,7},{6,4},{7,5},{8,10},{9,11},{10,... | collective-permute-start | bytes 196616 | tf_op jit(solution)/shard_map/ppermute | solution.py:69
  9.3 1.4 %collective-permute-start.5 = (bf16[128,256]{1,0:T(8,128)(2,1)S(1)}, bf16[128,256]{1,0:T(8,128)(2,1)S(1)}, u32[]{:S(2)}, u32[]{:S(2)}) collective-permute-start(bf16[128,256]{1,0:T(8,128)(2,1)S(1)} %get-tuple-element.25), channel_id=1, source_target_pairs={{0,3},{1,2},{2,1},{3,0},{4,7},{5,6},{6,5},{7,4},{8,11},{9,10},{10,... | collective-permute-start | bytes 196616 | tf_op jit(solution)/shard_map/ppermute | solution.py:69
  10.7 0.5 %collective-permute-start.3 = (bf16[128,256]{1,0:T(8,128)(2,1)S(1)}, bf16[128,256]{1,0:T(8,128)(2,1)S(1)}, u32[]{:S(2)}, u32[]{:S(2)}) collective-permute-start(bf16[128,256]{1,0:T(8,128)(2,1)S(1)} %get-tuple-element.23), channel_id=1, source_target_pairs={{0,1},{1,0},{2,3},{3,2},{4,5},{5,4},{6,7},{7,6},{8,9},{9,8},{10,11... | collective-permute-start | bytes 196616 | tf_op jit(solution)/shard_map/ppermute | solution.py:69
  11.2 0.0 copy-done.1
  11.2 2.6 %collective-permute-start.7 = (f32[128,128]{1,0:T(8,128)S(1)}, f32[128,128]{1,0:T(8,128)S(1)}, u32[]{:S(2)}, u32[]{:S(2)}) collective-permute-start(f32[128,128]{1,0:T(8,128)S(1)} %copy-done.1), channel_id=1, source_target_pairs={{0,4},{1,5},{2,6},{3,7},{4,0},{5,1},{6,2},{7,3},{8,12},{9,13},{10,... | collective-permute-start | bytes 196616 | tf_op jit(solution)/shard_map/ppermute | solution.py:74
  13.8 0.0 collective-permute-done.4.refs_1_
  13.8 0.7 %collective-permute-done.5.refs_2_ = bf16[128,256]{1,0:T(8,128)(2,1)S(1)} collective-permute-done((bf16[128,256]{1,0:T(8,128)(2,1)S(1)}, bf16[128,256]{1,0:T(8,128)(2,1)S(1)}, u32[]{:S(2)}, u32[]{:S(2)}) %collective-permute-start.5) | collective-permute-done | bytes 65568 | tf_op jit(solution)/shard_map/ppermute | solution.py:69
  14.5 0.7 %collective-permute-done.3.refs_0_ = bf16[128,256]{1,0:T(8,128)(2,1)S(1)} collective-permute-done((bf16[128,256]{1,0:T(8,128)(2,1)S(1)}, bf16[128,256]{1,0:T(8,128)(2,1)S(1)}, u32[]{:S(2)}, u32[]{:S(2)}) %collective-permute-start.3) | collective-permute-done | bytes 65568 | tf_op jit(solution)/shard_map/ppermute | solution.py:69
  15.3 0.0 copy-start
  15.3 2.9 %collective-permute-start.6 = (bf16[128,256]{1,0:T(8,128)(2,1)S(1)}, bf16[128,256]{1,0:T(8,128)(2,1)S(1)}, u32[]{:S(2)}, u32[]{:S(2)}) collective-permute-start(bf16[128,256]{1,0:T(8,128)(2,1)S(1)} %add.1.sums.refs_0_), channel_id=1, source_target_pairs={{0,4},{1,5},{2,6},{3,7},{4,0},{5,1},{6,2},{7,3},{8,12},{9,13},{10,... | collective-permute-start | bytes 196616 | tf_op jit(solution)/shard_map/ppermute | solution.py:74
  18.1 0.0 copy-done
  18.1 0.2 apply_weight.1.refs_4_
  18.3 0.0 collective-permute-done.7.refs_6_
  18.3 2.2 %collective-permute-done.6.refs_1_ = bf16[128,256]{1,0:T(8,128)(2,1)S(1)} collective-permute-done((bf16[128,256]{1,0:T(8,128)(2,1)S(1)}, bf16[128,256]{1,0:T(8,128)(2,1)S(1)}, u32[]{:S(2)}, u32[]{:S(2)}) %collective-permute-start.6) | collective-permute-done | bytes 65568 | tf_op jit(solution)/shard_map/ppermute | solution.py:74
  20.5 0.4 %own_rows.1 = (f32[128,128]{1,0:T(8,128)S(1)}, bf16[384,128]{1,0:T(8,128)(2,1)S(1)}) custom-call(bf16[128,256]{1,0:T(8,128)(2,1)S(1)} %add.1.sums.refs_0_, bf16[128,256]{1,0:T(8,128)(2,1)S(1)} %collective-permute-done.6.refs_1_, bf16[128,128]{1,0:T(8,128)(2,1)S(1)} %copy-done, f32[1,128]{1,0:T(1,128)S(1)} %get-tuple-element.26.refs_3_, ...), custom_call_target="tpu_custom_call" | custom-call | tf_op jit(solution)/shard_map/own_rows/pallas_call | solution.py:263
  20.9 2.1 %collective-permute-start.8 = (bf16[384,128]{1,0:T(8,128)(2,1)S(1)}, bf16[384,128]{1,0:T(8,128)(2,1)S(1)}, u32[]{:S(2)}, u32[]{:S(2)}) collective-permute-start(bf16[384,128]{1,0:T(8,128)(2,1)S(1)} %get-tuple-element.29.refs_0_), channel_id=1, source_target_pairs={{0,1},{1,0},{2,3},{3,2},{4,5},{5,4},{6,7},{7,6},{8,9},{9,8},{10,11... | collective-permute-start | bytes 294920 | tf_op jit(solution)/shard_map/ppermute | solution.py:69
  23.0 0.7 %collective-permute-start.10 = (bf16[384,128]{1,0:T(8,128)(2,1)S(1)}, bf16[384,128]{1,0:T(8,128)(2,1)S(1)}, u32[]{:S(2)}, u32[]{:S(2)}) collective-permute-start(bf16[384,128]{1,0:T(8,128)(2,1)S(1)} %get-tuple-element.29.refs_0_), channel_id=1, source_target_pairs={{0,3},{1,2},{2,1},{3,0},{4,7},{5,6},{6,5},{7,4},{8,11},{9,10},{10,... | collective-permute-start | bytes 294920 | tf_op jit(solution)/shard_map/ppermute | solution.py:69
  23.7 0.8 %collective-permute-start.9 = (bf16[384,128]{1,0:T(8,128)(2,1)S(1)}, bf16[384,128]{1,0:T(8,128)(2,1)S(1)}, u32[]{:S(2)}, u32[]{:S(2)}) collective-permute-start(bf16[384,128]{1,0:T(8,128)(2,1)S(1)} %get-tuple-element.29.refs_0_), channel_id=1, source_target_pairs={{0,2},{1,3},{2,0},{3,1},{4,6},{5,7},{6,4},{7,5},{8,10},{9,11},{10,... | collective-permute-start | bytes 294920 | tf_op jit(solution)/shard_map/ppermute | solution.py:69
  24.5 1.1 %collective-permute-done.8.refs_1_ = bf16[384,128]{1,0:T(8,128)(2,1)S(1)} collective-permute-done((bf16[384,128]{1,0:T(8,128)(2,1)S(1)}, bf16[384,128]{1,0:T(8,128)(2,1)S(1)}, u32[]{:S(2)}, u32[]{:S(2)}) %collective-permute-start.8) | collective-permute-done | bytes 98336 | tf_op jit(solution)/shard_map/ppermute | solution.py:69
  25.6 0.4 %early.1.refs_6_ = f32[128,512]{1,0:T(8,128)S(1)} custom-call(bf16[384,128]{1,0:T(8,128)(2,1)S(1)} %get-tuple-element.29.refs_0_, bf16[384,128]{1,0:T(8,128)(2,1)S(1)} %collective-permute-done.8.refs_1_, bf16[128,128]{1,0:T(8,128)(2,1)S(1)} %copy-done, bf16[512,1024]{1,0:T(8,128)(2,1)S(1)} %get-tuple-element.21.refs_4_.refs_3_.refs_5_), custom_call_target="tpu_custom_call" | custom-call | tf_op jit(solution)/shard_map/early/pallas_call | solution.py:351
  26.0 2.5 %collective-permute-done.10.refs_3_ = bf16[384,128]{1,0:T(8,128)(2,1)S(1)} collective-permute-done((bf16[384,128]{1,0:T(8,128)(2,1)S(1)}, bf16[384,128]{1,0:T(8,128)(2,1)S(1)}, u32[]{:S(2)}, u32[]{:S(2)}) %collective-permute-start.10) | collective-permute-done | bytes 98336 | tf_op jit(solution)/shard_map/ppermute | solution.py:69
  28.5 0.0 collective-permute-done.9.refs_2_
  28.5 0.4 %backward.1 = (bf16[272,128]{1,0:T(8,128)(2,1)S(1)}, bf16[272,128]{1,0:T(8,128)(2,1)S(1)}, bf16[272,128]{1,0:T(8,128)(2,1)S(1)}, bf16[272,128]{1,0:T(8,128)(2,1)S(1)}, f32[32,512]{1,0:T(8,128)S(1)}) custom-call(bf16[384,128]{1,0:T(8,128)(2,1)S(1)} %get-tuple-element.29.refs_0_, bf16[384,128]{1,0:T(8,128)(2,1)S(1)} %collective-permute-done.8.refs_1_, ...), custom_call_target="tpu_custom_call" | custom-call | tf_op jit(solution)/shard_map/backward/pallas_call | solution.py:361
  29.0 0.1 collective-permute-start.11
  29.1 1.3 %collective-permute-start.12 = (bf16[272,128]{1,0:T(8,128)(2,1)S(1)}, bf16[272,128]{1,0:T(8,128)(2,1)S(1)}, u32[]{:S(2)}, u32[]{:S(2)}) collective-permute-start(bf16[272,128]{1,0:T(8,128)(2,1)S(1)} %get-tuple-element.32), channel_id=1, source_target_pairs={{0,16},{8,24},{16,0},{24,8},{1,17},{9,25},{17,1},{25,9},{2,18},{10... | collective-permute-start | bytes 208904 | tf_op jit(solution)/shard_map/ppermute | solution.py:69
  30.4 0.6 %collective-permute-start.13 = (bf16[272,128]{1,0:T(8,128)(2,1)S(1)}, bf16[272,128]{1,0:T(8,128)(2,1)S(1)}, u32[]{:S(2)}, u32[]{:S(2)}) collective-permute-start(bf16[272,128]{1,0:T(8,128)(2,1)S(1)} %get-tuple-element.33), channel_id=1, source_target_pairs={{0,24},{8,16},{16,8},{24,0},{1,25},{9,17},{17,9},{25,1},{2,26},{10... | collective-permute-start | bytes 208904 | tf_op jit(solution)/shard_map/ppermute | solution.py:69
  30.9 0.6 %activate.1 = f32[128,128]{1,0:T(8,128)} custom-call(f32[128,128]{1,0:T(8,128)S(1)} %get-tuple-element.28.pre), custom_call_target="tpu_custom_call" | custom-call | tf_op jit(solution)/shard_map/activate/pallas_call | solution.py:279
  31.6 0.0 collective-permute-done.11.refs_1_
  31.6 2.4 %collective-permute-done.12.refs_2_ = bf16[272,128]{1,0:T(8,128)(2,1)S(1)} collective-permute-done((bf16[272,128]{1,0:T(8,128)(2,1)S(1)}, bf16[272,128]{1,0:T(8,128)(2,1)S(1)}, u32[]{:S(2)}, u32[]{:S(2)}) %collective-permute-start.12) | collective-permute-done | bytes 69664 | tf_op jit(solution)/shard_map/ppermute | solution.py:69
  34.0 0.8 %collective-permute-done.13.refs_3_ = bf16[272,128]{1,0:T(8,128)(2,1)S(1)} collective-permute-done((bf16[272,128]{1,0:T(8,128)(2,1)S(1)}, bf16[272,128]{1,0:T(8,128)(2,1)S(1)}, u32[]{:S(2)}, u32[]{:S(2)}) %collective-permute-start.13) | collective-permute-done | bytes 69664 | tf_op jit(solution)/shard_map/ppermute | solution.py:69
  34.8 0.7 %final.1 = (bf16[32,512]{1,0:T(8,128)(2,1)}, f32[128,128]{1,0:T(8,128)}, f32[1,128]{1,0:T(1,128)}) custom-call(bf16[272,128]{1,0:T(8,128)(2,1)S(1)} %get-tuple-element.30.refs_0_, bf16[272,128]{1,0:T(8,128)(2,1)S(1)} %collective-permute-done.11.refs_1_, bf16[272,128]{1,0:T(8,128)(2,1)S(1)} %collective-permute-done.12.refs_2_, ...), custom_call_target="tpu_custom_call" | custom-call | tf_op jit(solution)/shard_map/final/pallas_call | solution.py:402
  (1 shorter events, 0.0 us)
Async XLA Ops:
  0.6 5.6 %collective-permute-start.2 = (bf16[32,512]{1,0:T(8,128)(2,1)}, bf16[32,512]{1,0:T(8,128)(2,1)S(1)}, u32[]{:S(2)}, u32[]{:S(2)}) collective-permute-start(bf16[32,512]{1,0:T(8,128)(2,1)} %bitcast.6), channel_id=1, source_target_pairs={{0,24},{8,16},{16,8},{24,0},{1,25},{9,17},{17,9},{25,1},{2,26},{10... | collective-permute-start | bytes 98312 | tf_op jit(solution)/shard_map/ppermute | solution.py:69
  3.1 4.2 %collective-permute-start.1 = (bf16[32,512]{1,0:T(8,128)(2,1)}, bf16[32,512]{1,0:T(8,128)(2,1)S(1)}, u32[]{:S(2)}, u32[]{:S(2)}) collective-permute-start(bf16[32,512]{1,0:T(8,128)(2,1)} %bitcast.7), channel_id=1, source_target_pairs={{0,16},{8,24},{16,0},{24,8},{1,17},{9,25},{17,1},{25,9},{2,18},{10... | collective-permute-start | bytes 98312 | tf_op jit(solution)/shard_map/ppermute | solution.py:69
  3.7 3.5 %collective-permute-start = (bf16[32,512]{1,0:T(8,128)(2,1)}, bf16[32,512]{1,0:T(8,128)(2,1)S(1)}, u32[]{:S(2)}, u32[]{:S(2)}) collective-permute-start(bf16[32,512]{1,0:T(8,128)(2,1)} %bitcast.8), channel_id=1, source_target_pairs={{0,8},{8,0},{16,24},{24,16},{1,9},{9,1},{17,25},{25,17},{2,10},{10... | collective-permute-start | bytes 98312 | tf_op jit(solution)/shard_map/ppermute | solution.py:69
  4.4 2.9 %copy-start.2 = (bf16[512,32]{0,1:T(8,128)(2,1)S(1)}, bf16[512,32]{0,1:T(8,128)(2,1)}, u32[]{:S(2)}) copy-start(bf16[512,32]{0,1:T(8,128)(2,1)} %param.9) | copy-start | bytes 98308
  7.3 3.9 %copy-start.1 = (f32[128,128]{1,0:T(8,128)S(1)}, f32[128,128]{1,0:T(8,128)}, u32[]{:S(2)}) copy-start(f32[128,128]{1,0:T(8,128)} %refs_5_.1) | copy-start | bytes 196612
  7.7 6.2 %collective-permute-start.4 = (bf16[128,256]{1,0:T(8,128)(2,1)S(1)}, bf16[128,256]{1,0:T(8,128)(2,1)S(1)}, u32[]{:S(2)}, u32[]{:S(2)}) collective-permute-start(bf16[128,256]{1,0:T(8,128)(2,1)S(1)} %get-tuple-element.24), channel_id=1, source_target_pairs={{0,2},{1,3},{2,0},{3,1},{4,6},{5,7},{6,4},{7,5},{8,10},{9,11},{10,... | collective-permute-start | bytes 196616 | tf_op jit(solution)/shard_map/ppermute | solution.py:69
  9.3 5.2 %collective-permute-start.5 = (bf16[128,256]{1,0:T(8,128)(2,1)S(1)}, bf16[128,256]{1,0:T(8,128)(2,1)S(1)}, u32[]{:S(2)}, u32[]{:S(2)}) collective-permute-start(bf16[128,256]{1,0:T(8,128)(2,1)S(1)} %get-tuple-element.25), channel_id=1, source_target_pairs={{0,3},{1,2},{2,1},{3,0},{4,7},{5,6},{6,5},{7,4},{8,11},{9,10},{10,... | collective-permute-start | bytes 196616 | tf_op jit(solution)/shard_map/ppermute | solution.py:69
  10.7 4.6 %collective-permute-start.3 = (bf16[128,256]{1,0:T(8,128)(2,1)S(1)}, bf16[128,256]{1,0:T(8,128)(2,1)S(1)}, u32[]{:S(2)}, u32[]{:S(2)}) collective-permute-start(bf16[128,256]{1,0:T(8,128)(2,1)S(1)} %get-tuple-element.23), channel_id=1, source_target_pairs={{0,1},{1,0},{2,3},{3,2},{4,5},{5,4},{6,7},{7,6},{8,9},{9,8},{10,11... | collective-permute-start | bytes 196616 | tf_op jit(solution)/shard_map/ppermute | solution.py:69
  11.2 7.1 %collective-permute-start.7 = (f32[128,128]{1,0:T(8,128)S(1)}, f32[128,128]{1,0:T(8,128)S(1)}, u32[]{:S(2)}, u32[]{:S(2)}) collective-permute-start(f32[128,128]{1,0:T(8,128)S(1)} %copy-done.1), channel_id=1, source_target_pairs={{0,4},{1,5},{2,6},{3,7},{4,0},{5,1},{6,2},{7,3},{8,12},{9,13},{10,... | collective-permute-start | bytes 196616 | tf_op jit(solution)/shard_map/ppermute | solution.py:74
  15.3 2.9 %copy-start = (bf16[128,128]{1,0:T(8,128)(2,1)S(1)}, bf16[128,128]{1,0:T(8,128)(2,1)}, u32[]{:S(2)}) copy-start(bf16[128,128]{1,0:T(8,128)(2,1)} %refs_4_.1) | copy-start | bytes 98308
  15.3 5.2 %collective-permute-start.6 = (bf16[128,256]{1,0:T(8,128)(2,1)S(1)}, bf16[128,256]{1,0:T(8,128)(2,1)S(1)}, u32[]{:S(2)}, u32[]{:S(2)}) collective-permute-start(bf16[128,256]{1,0:T(8,128)(2,1)S(1)} %add.1.sums.refs_0_), channel_id=1, source_target_pairs={{0,4},{1,5},{2,6},{3,7},{4,0},{5,1},{6,2},{7,3},{8,12},{9,13},{10,... | collective-permute-start | bytes 196616 | tf_op jit(solution)/shard_map/ppermute | solution.py:74
  20.9 4.7 %collective-permute-start.8 = (bf16[384,128]{1,0:T(8,128)(2,1)S(1)}, bf16[384,128]{1,0:T(8,128)(2,1)S(1)}, u32[]{:S(2)}, u32[]{:S(2)}) collective-permute-start(bf16[384,128]{1,0:T(8,128)(2,1)S(1)} %get-tuple-element.29.refs_0_), channel_id=1, source_target_pairs={{0,1},{1,0},{2,3},{3,2},{4,5},{5,4},{6,7},{7,6},{8,9},{9,8},{10,11... | collective-permute-start | bytes 294920 | tf_op jit(solution)/shard_map/ppermute | solution.py:69
  23.0 5.5 %collective-permute-start.10 = (bf16[384,128]{1,0:T(8,128)(2,1)S(1)}, bf16[384,128]{1,0:T(8,128)(2,1)S(1)}, u32[]{:S(2)}, u32[]{:S(2)}) collective-permute-start(bf16[384,128]{1,0:T(8,128)(2,1)S(1)} %get-tuple-element.29.refs_0_), channel_id=1, source_target_pairs={{0,3},{1,2},{2,1},{3,0},{4,7},{5,6},{6,5},{7,4},{8,11},{9,10},{10,... | collective-permute-start | bytes 294920 | tf_op jit(solution)/shard_map/ppermute | solution.py:69
  23.7 4.8 %collective-permute-start.9 = (bf16[384,128]{1,0:T(8,128)(2,1)S(1)}, bf16[384,128]{1,0:T(8,128)(2,1)S(1)}, u32[]{:S(2)}, u32[]{:S(2)}) collective-permute-start(bf16[384,128]{1,0:T(8,128)(2,1)S(1)} %get-tuple-element.29.refs_0_), channel_id=1, source_target_pairs={{0,2},{1,3},{2,0},{3,1},{4,6},{5,7},{6,4},{7,5},{8,10},{9,11},{10,... | collective-permute-start | bytes 294920 | tf_op jit(solution)/shard_map/ppermute | solution.py:69
  29.0 2.6 %collective-permute-start.11 = (bf16[272,128]{1,0:T(8,128)(2,1)S(1)}, bf16[272,128]{1,0:T(8,128)(2,1)S(1)}, u32[]{:S(2)}, u32[]{:S(2)}) collective-permute-start(bf16[272,128]{1,0:T(8,128)(2,1)S(1)} %get-tuple-element.31), channel_id=1, source_target_pairs={{0,8},{8,0},{16,24},{24,16},{1,9},{9,1},{17,25},{25,17},{2,10},{10... | collective-permute-start | bytes 208904 | tf_op jit(solution)/shard_map/ppermute | solution.py:69
  29.1 4.9 %collective-permute-start.12 = (bf16[272,128]{1,0:T(8,128)(2,1)S(1)}, bf16[272,128]{1,0:T(8,128)(2,1)S(1)}, u32[]{:S(2)}, u32[]{:S(2)}) collective-permute-start(bf16[272,128]{1,0:T(8,128)(2,1)S(1)} %get-tuple-element.32), channel_id=1, source_target_pairs={{0,16},{8,24},{16,0},{24,8},{1,17},{9,25},{17,1},{25,9},{2,18},{10... | collective-permute-start | bytes 208904 | tf_op jit(solution)/shard_map/ppermute | solution.py:69
  30.4 4.4 %collective-permute-start.13 = (bf16[272,128]{1,0:T(8,128)(2,1)S(1)}, bf16[272,128]{1,0:T(8,128)(2,1)S(1)}, u32[]{:S(2)}, u32[]{:S(2)}) collective-permute-start(bf16[272,128]{1,0:T(8,128)(2,1)S(1)} %get-tuple-element.33), channel_id=1, source_target_pairs={{0,24},{8,16},{16,8},{24,0},{1,25},{9,17},{17,9},{25,1},{2,26},{10... | collective-permute-start | bytes 208904 | tf_op jit(solution)/shard_map/ppermute | solution.py:69

commit v8 on v7

--- a/solution.py
+++ b/solution.py
@@ -152,41 +152,34 @@
     )(limit, *[pltpu.with_memory_space_constraint(a, pltpu.HBM) for a in (rows, cols, ids, values, bias)])
 
 
-def forward_kernel(size, *refs):
-    parts, (band, kept), messages, (panel, sums) = refs[:size], refs[size : size + 2], refs[size + 2 : -2], refs[-2:]
+def forward_kernel(size, members, *refs):
+    parts, (band, kept), messages, panel = refs[:size], refs[size : size + 2], refs[size + 2 : -1], refs[-1]
     me = lax.axis_index("row")
-    members, _, own = sums.shape
     mine = lax.rem(lax.axis_index("col"), members)
     width = parts[0].shape[0]
+    own = kept.shape[1]
     for step, part in enumerate(parts):
         slot = pl.multiple_of(source(me, step, size) * width, width)
-        panel[pl.ds(slot, width), :] = part[...].astype(f32)
+        panel[pl.ds(slot, width), :] = part[...].astype(panel.dtype)
     left = panel[...].astype(bf16)
-    many = max(own, min(wide, band.shape[1]))
-
-    def piece(index):
-        got = dot(left, band[:, pl.ds(start_of(index, many), many)])
-        for part in range(many // own):
-            sums[index * (many // own) + part] = got[:, part * own : (part + 1) * own]
-
-    each(band.shape[1] // many, piece)
-    kept[...] = sums[mine]
-    for step, message in enumerate(messages):
-        message[...] = sums[partner(mine, step + 1, members)].astype(bf16)
+    for step, message in enumerate((kept,) + messages):
+        columns = pl.ds(pl.multiple_of(partner(mine, step, members) * own, own), own)
+        message[...] = dot(left, band[:, columns]).astype(message.dtype)
 
 
 def forward(parts, band, members):
-    hidden = parts[0].shape[0] * len(parts)
+    width = parts[0].shape[0]
+    hidden = width * len(parts)
     nodes, total = band.shape
     block = (hidden, total // members)
-    sums = struct((members,) + block, f32)
-    return pl.pallas_call(
-        functools.partial(forward_kernel, len(parts)),
+    panel = pltpu.VMEM((hidden, nodes), bf16 if width % 16 == 0 else f32)
+    return pl.pallas_call(
+        functools.partial(forward_kernel, len(parts), members),
         out_shape=(struct(block, f32),) + (struct(block, bf16),) * (members - 1),
         in_specs=[vmem()] * (len(parts) + 1),
         out_specs=(vmem(),) * members,
-        scratch_shapes=[pltpu.VMEM((hidden, nodes), f32), pltpu.VMEM(sums.shape, f32)],
-        compiler_params=room(band, sums),
+        scratch_shapes=[panel],
+        compiler_params=room(band),
         name="forward",
     )(*parts, band)
 
@@ -308,9 +301,10 @@
     out[...] = group_product(parts, 0, weight, band, rows, mine, members)
 
 
-def backward_kernel(size, group, members, *refs):
-    got, (weight, band, early), messages = refs[:members], refs[members : members + 3], refs[members + 3 :][:size]
+def backward_kernel(order, size, group, members, *refs):
+    given, (weight, band, early), messages = refs[:members], refs[members : members + 3], refs[members + 3 :][:size]
     kept, rows, slots, lines, grads, packed = refs[members + 3 + size :]
+    got = [given[order.index(step)] for step in range(members)]
     hidden = weight.shape[0]
     own = got[0].shape[0] - hidden
     width, nodes = kept.shape
@@ -344,6 +338,7 @@
 def backward(got, weight, band, size):
     members = len(got)
     group = group_of(members)
+    order = [0, *range(2, members), 1][:members]
     hidden = weight.shape[0]
     nodes, total = band.shape
     width = hidden // size
@@ -359,7 +354,7 @@
     )(*got[:group], weight, band)
     message = struct((width * (nodes // hidden) + hidden + tail, hidden), bf16)
     return pl.pallas_call(
-        functools.partial(backward_kernel, size, group, members),
+        functools.partial(backward_kernel, order, size, group, members),
         out_shape=(message,) * size + (struct((width, nodes), f32),),
         in_specs=[vmem()] * (members + 3),
         out_specs=(vmem(),) * (size + 1),
@@ -372,42 +367,54 @@
         ],
         compiler_params=room(band, *got),
         name="backward",
-    )(*got, weight, band, early)
-
-
-def final_kernel(size, shrink, *refs):
-    messages, (kept, features, weight, bias, slots) = refs[:size], refs[size:]
+    )(*[got[step] for step in order], weight, band, early)
+
+
+def final_kernel(order, size, shrink, *refs):
+    given, (kept, features_out, weight_out, bias_out, slots, features, weight, bias, sems) = refs[:size], refs[size:]
     width, nodes = kept.shape
     hidden = weight.shape[0]
     split = nodes // hidden
     me = lax.axis_index("row")
+    messages = [given[order.index(step)] for step in range(size)]
+    pairs = ((weight, weight_out), (bias, bias_out), (features, features_out))
+    copies = [pltpu.make_async_copy(a, b, sems.at[i]) for i, (a, b) in enumerate(pairs)]
     for step, message in enumerate(messages):
         slots[source(me, step, size)] = message[split * width :, :].astype(f32)
+    total = slots[0]
+    for index in range(1, size):
+        total = total + slots[index]
+    weight[...] = total[:hidden] * shrink
+    copies[0].start()
+    bias[...] = jnp.sum(total[hidden:], axis=0, keepdims=True) * shrink
+    copies[1].start()
     for index in range(split):
         place = slice(index * hidden, (index + 1) * hidden)
         total = kept[:, place]
         for message in messages[1:]:
             total = total + message[index * width : (index + 1) * width, :].astype(f32)
         features[:, place] = total.astype(bf16)
-    total = slots[0]
-    for index in range(1, size):
-        total = total + slots[index]
-    weight[...] = total[:hidden] * shrink
-    bias[...] = jnp.sum(total[hidden:], axis=0, keepdims=True) * shrink
+    copies[2].start()
+    for copy in copies:
+        copy.wait()
 
 
 def final(messages, kept, hidden, shrink):
     width, nodes = kept.shape
     size = len(messages)
-    return pl.pallas_call(
-        functools.partial(final_kernel, size, shrink),
-        out_shape=(struct((width, nodes), bf16), struct((hidden, hidden), f32), struct((1, hidden), f32)),
+    order = [0, *range(size - 1, 0, -1)]
+    outs = (struct((width, nodes), bf16), struct((hidden, hidden), f32), struct((1, hidden), f32))
+    return pl.pallas_call(
+        functools.partial(final_kernel, order, size, shrink),
+        out_shape=outs,
         in_specs=[vmem()] * (size + 1),
-        out_specs=(vmem(),) * 3,
-        scratch_shapes=[pltpu.VMEM((size, hidden + tail, hidden), f32)],
+        out_specs=(pl.BlockSpec(memory_space=pltpu.HBM),) * 3,
+        scratch_shapes=[pltpu.VMEM((size, hidden + tail, hidden), f32)]
+        + [pltpu.VMEM(out.shape, out.dtype) for out in outs]
+        + [pltpu.SemaphoreType.DMA((3,))],
         compiler_params=room(*messages),
         name="final",
-    )(*messages, kept)
+    )(*[messages[step] for step in order], kept)
 
 
 def shards(
@@ -440,7 +447,7 @@
     if twins > 1:
         other, messages[0] = lax.optimization_barrier((cotangent, messages[0]))
         cotangents.append(exchange_twin(other, "col", members))
-    sums = [add(kept, got)]
+    sums = [add(kept, got[::-1])]
     if twins > 1:
         sums.append(exchange_twin(sums[0], "col", members))
     first = apply_weight(sums[0], weight)

time: 35.6 us -> 35.6 us (level)
  waiting for transfers between devices: 11.5 us -> 12.1 us
  starting transfers between devices: 17.7 us -> 17.3 us
where the time goes in v8:
time: 35.6 us; the launch traced here: 35.3 us
  starting transfers between devices  17.3 us (49%)
  waiting for transfers between devices  12.1 us (34%)
  Pallas kernels  4.53 us (13%)
  between operations  1.38 us (4%)
    ppermute x12, starting transfers between devices, exchange(): return lax.ppermute(value, axis, pairs)  12.2 us
    ppermute x12, waiting for transfers between devices, exchange(): return lax.ppermute(value, axis, pairs)  9.63 us
    ppermute x2, starting transfers between devices, exchange_twin(): lax.ppermute(value, axis, [(i, (i + members) % size) for i in range(size)])  5.17 us
    ppermute x2, waiting for transfers between devices, exchange_twin(): lax.ppermute(value, axis, [(i, (i + members) % size) for i in range(size)])  2.45 us
    pallas_call x1, Pallas kernels, make_band(): pl.pallas_call(functools.partial(band_kernel, place), out_shape=(out, str...  1.4 us
    pallas_call x1, Pallas kernels, final(): pl.pallas_call(functools.partial(final_kernel, order, size, shrink), out_...  0.72 us
  transfers between devices with their start and end apart: 14, of which 8 were waited for; matrix products, arithmetic and copies ran while one was open for 0% of the time, Pallas kernels for 8%

profile of v8, /device:TPU:0, one launch (start us, length us, event | category | flops | bytes accessed | tf_op | source)
XLA Modules:
  0.0 35.3 jit_solution(14469362731101938926)
XLA Ops:
  0.6 2.5 %collective-permute-start.2 = (bf16[32,512]{1,0:T(8,128)(2,1)}, bf16[32,512]{1,0:T(8,128)(2,1)S(1)}, u32[]{:S(2)}, u32[]{:S(2)}) collective-permute-start(bf16[32,512]{1,0:T(8,128)(2,1)} %bitcast.6), channel_id=1, source_target_pairs={{0,24},{8,16},{16,8},{24,0},{1,25},{9,17},{17,9},{25,1},{2,26},{10... | collective-permute-start | bytes 98312 | tf_op jit(solution)/shard_map/ppermute | solution.py:69
  3.1 0.6 %collective-permute-start.1 = (bf16[32,512]{1,0:T(8,128)(2,1)}, bf16[32,512]{1,0:T(8,128)(2,1)S(1)}, u32[]{:S(2)}, u32[]{:S(2)}) collective-permute-start(bf16[32,512]{1,0:T(8,128)(2,1)} %bitcast.7), channel_id=1, source_target_pairs={{0,16},{8,24},{16,0},{24,8},{1,17},{9,25},{17,1},{25,9},{2,18},{10... | collective-permute-start | bytes 98312 | tf_op jit(solution)/shard_map/ppermute | solution.py:69
  3.7 0.0 collective-permute-start
  4.4 0.0 copy-start.2
  4.4 1.4 %band.1 = (bf16[512,1024]{1,0:T(8,128)(2,1)S(1)}, f32[1,128]{1,0:T(1,128)S(1)}) custom-call(s32[1,1]{1,0:T(1,128)S(6)} %copy.13.limit, s32[1,1,128]{2,1,0:T(1,128)} %rows.1, s32[1,1,128]{2,1,0:T(1,128)} %cols.1, s32[256,128]{1,0:T(8,128)} %bitcast.10, bf16[256,128]{1,0:T(8,128)(2,1)} %bitcast.11, f32[1,128]{1,0:T(1,128)} %bitcast.12), custom_call_target="tpu_custom_call" | custom-call | flops 33554432 | bytes 8388608 | tf_op jit(solution)/shard_map/band/pallas_call | solution.py:136
  5.9 0.0 collective-permute-done.2.refs_3_
  5.9 1.4 %collective-permute-done.1.refs_2_ = bf16[32,512]{1,0:T(8,128)(2,1)S(1)} collective-permute-done((bf16[32,512]{1,0:T(8,128)(2,1)}, bf16[32,512]{1,0:T(8,128)(2,1)S(1)}, u32[]{:S(2)}, u32[]{:S(2)}) %collective-permute-start.1) | collective-permute-done | bytes 32800 | tf_op jit(solution)/shard_map/ppermute | solution.py:69
  7.3 0.0 collective-permute-done.refs_1_
  7.3 0.0 copy-done.2
  7.3 0.0 copy-start.1
  7.3 0.3 forward.1
  7.6 2.6 %collective-permute-start.3 = (bf16[128,256]{1,0:T(8,128)(2,1)S(1)}, bf16[128,256]{1,0:T(8,128)(2,1)S(1)}, u32[]{:S(2)}, u32[]{:S(2)}) collective-permute-start(bf16[128,256]{1,0:T(8,128)(2,1)S(1)} %get-tuple-element.23), channel_id=1, source_target_pairs={{0,3},{1,2},{2,1},{3,0},{4,7},{5,6},{6,5},{7,4},{8,11},{9,10},{10,... | collective-permute-start | bytes 196616 | tf_op jit(solution)/shard_map/ppermute | solution.py:69
  10.2 0.4 %collective-permute-start.4 = (bf16[128,256]{1,0:T(8,128)(2,1)S(1)}, bf16[128,256]{1,0:T(8,128)(2,1)S(1)}, u32[]{:S(2)}, u32[]{:S(2)}) collective-permute-start(bf16[128,256]{1,0:T(8,128)(2,1)S(1)} %get-tuple-element.24), channel_id=1, source_target_pairs={{0,2},{1,3},{2,0},{3,1},{4,6},{5,7},{6,4},{7,5},{8,10},{9,11},{10,... | collective-permute-start | bytes 196616 | tf_op jit(solution)/shard_map/ppermute | solution.py:69
  10.7 0.5 %collective-permute-start.5 = (bf16[128,256]{1,0:T(8,128)(2,1)S(1)}, bf16[128,256]{1,0:T(8,128)(2,1)S(1)}, u32[]{:S(2)}, u32[]{:S(2)}) collective-permute-start(bf16[128,256]{1,0:T(8,128)(2,1)S(1)} %get-tuple-element.25), channel_id=1, source_target_pairs={{0,1},{1,0},{2,3},{3,2},{4,5},{5,4},{6,7},{7,6},{8,9},{9,8},{10,11... | collective-permute-start | bytes 196616 | tf_op jit(solution)/shard_map/ppermute | solution.py:69
  11.2 0.0 copy-done.1
  11.2 2.6 %collective-permute-start.7 = (f32[128,128]{1,0:T(8,128)S(1)}, f32[128,128]{1,0:T(8,128)S(1)}, u32[]{:S(2)}, u32[]{:S(2)}) collective-permute-start(f32[128,128]{1,0:T(8,128)S(1)} %copy-done.1), channel_id=1, source_target_pairs={{0,4},{1,5},{2,6},{3,7},{4,0},{5,1},{6,2},{7,3},{8,12},{9,13},{10,... | collective-permute-start | bytes 196616 | tf_op jit(solution)/shard_map/ppermute | solution.py:74
  13.8 0.0 collective-permute-done.3.refs_0_
  13.8 1.3 %collective-permute-done.4.refs_1_ = bf16[128,256]{1,0:T(8,128)(2,1)S(1)} collective-permute-done((bf16[128,256]{1,0:T(8,128)(2,1)S(1)}, bf16[128,256]{1,0:T(8,128)(2,1)S(1)}, u32[]{:S(2)}, u32[]{:S(2)}) %collective-permute-start.4) | collective-permute-done | bytes 65568 | tf_op jit(solution)/shard_map/ppermute | solution.py:69
  15.1 0.0 collective-permute-done.5.refs_2_
  15.1 0.0 copy-start
  15.1 2.6 %collective-permute-start.6 = (bf16[128,256]{1,0:T(8,128)(2,1)S(1)}, bf16[128,256]{1,0:T(8,128)(2,1)S(1)}, u32[]{:S(2)}, u32[]{:S(2)}) collective-permute-start(bf16[128,256]{1,0:T(8,128)(2,1)S(1)} %add.1.sums.refs_0_), channel_id=1, source_target_pairs={{0,4},{1,5},{2,6},{3,7},{4,0},{5,1},{6,2},{7,3},{8,12},{9,13},{10,... | collective-permute-start | bytes 196616 | tf_op jit(solution)/shard_map/ppermute | solution.py:74
  17.7 0.0 copy-done
  17.7 0.2 apply_weight.1.refs_4_
  17.9 0.0 collective-permute-done.7.refs_6_
  17.9 2.4 %collective-permute-done.6.refs_1_ = bf16[128,256]{1,0:T(8,128)(2,1)S(1)} collective-permute-done((bf16[128,256]{1,0:T(8,128)(2,1)S(1)}, bf16[128,256]{1,0:T(8,128)(2,1)S(1)}, u32[]{:S(2)}, u32[]{:S(2)}) %collective-permute-start.6) | collective-permute-done | bytes 65568 | tf_op jit(solution)/shard_map/ppermute | solution.py:74
  20.4 0.4 %own_rows.1 = (f32[128,128]{1,0:T(8,128)S(1)}, bf16[384,128]{1,0:T(8,128)(2,1)S(1)}) custom-call(bf16[128,256]{1,0:T(8,128)(2,1)S(1)} %add.1.sums.refs_0_, bf16[128,256]{1,0:T(8,128)(2,1)S(1)} %collective-permute-done.6.refs_1_, bf16[128,128]{1,0:T(8,128)(2,1)S(1)} %copy-done, f32[1,128]{1,0:T(1,128)S(1)} %get-tuple-element.26.refs_3_, ...), custom_call_target="tpu_custom_call" | custom-call | tf_op jit(solution)/shard_map/own_rows/pallas_call | solution.py:256
  20.7 0.5 %collective-permute-start.10 = (bf16[384,128]{1,0:T(8,128)(2,1)S(1)}, bf16[384,128]{1,0:T(8,128)(2,1)S(1)}, u32[]{:S(2)}, u32[]{:S(2)}) collective-permute-start(bf16[384,128]{1,0:T(8,128)(2,1)S(1)} %get-tuple-element.29.refs_0_), channel_id=1, source_target_pairs={{0,1},{1,0},{2,3},{3,2},{4,5},{5,4},{6,7},{7,6},{8,9},{9,8},{10,11... | collective-permute-start | bytes 294920 | tf_op jit(solution)/shard_map/ppermute | solution.py:69
  21.3 2.4 %collective-permute-start.9 = (bf16[384,128]{1,0:T(8,128)(2,1)S(1)}, bf16[384,128]{1,0:T(8,128)(2,1)S(1)}, u32[]{:S(2)}, u32[]{:S(2)}) collective-permute-start(bf16[384,128]{1,0:T(8,128)(2,1)S(1)} %get-tuple-element.29.refs_0_), channel_id=1, source_target_pairs={{0,3},{1,2},{2,1},{3,0},{4,7},{5,6},{6,5},{7,4},{8,11},{9,10},{10,... | collective-permute-start | bytes 294920 | tf_op jit(solution)/shard_map/ppermute | solution.py:69
  23.7 0.6 %collective-permute-start.8 = (bf16[384,128]{1,0:T(8,128)(2,1)S(1)}, bf16[384,128]{1,0:T(8,128)(2,1)S(1)}, u32[]{:S(2)}, u32[]{:S(2)}) collective-permute-start(bf16[384,128]{1,0:T(8,128)(2,1)S(1)} %get-tuple-element.29.refs_0_), channel_id=1, source_target_pairs={{0,2},{1,3},{2,0},{3,1},{4,6},{5,7},{6,4},{7,5},{8,10},{9,11},{10,... | collective-permute-start | bytes 294920 | tf_op jit(solution)/shard_map/ppermute | solution.py:69
  24.3 1.4 %collective-permute-done.10.refs_1_.refs_3_ = bf16[384,128]{1,0:T(8,128)(2,1)S(1)} collective-permute-done((bf16[384,128]{1,0:T(8,128)(2,1)S(1)}, bf16[384,128]{1,0:T(8,128)(2,1)S(1)}, u32[]{:S(2)}, u32[]{:S(2)}) %collective-permute-start.10) | collective-permute-done | bytes 98336 | tf_op jit(solution)/shard_map/ppermute | solution.py:69
  25.7 0.4 %early.1.refs_6_ = f32[128,512]{1,0:T(8,128)S(1)} custom-call(bf16[384,128]{1,0:T(8,128)(2,1)S(1)} %get-tuple-element.29.refs_0_, bf16[384,128]{1,0:T(8,128)(2,1)S(1)} %collective-permute-done.10.refs_1_.refs_3_, bf16[128,128]{1,0:T(8,128)(2,1)S(1)} %copy-done, bf16[512,1024]{1,0:T(8,128)(2,1)S(1)} %get-tuple-element.21.refs_4_.refs_3_.refs_5_), custom_call_target="tpu_custom_call" | custom-call | tf_op jit(solution)/shard_map/early/pallas_call | solution.py:346
  26.1 0.7 %collective-permute-done.9.refs_2_ = bf16[384,128]{1,0:T(8,128)(2,1)S(1)} collective-permute-done((bf16[384,128]{1,0:T(8,128)(2,1)S(1)}, bf16[384,128]{1,0:T(8,128)(2,1)S(1)}, u32[]{:S(2)}, u32[]{:S(2)}) %collective-permute-start.9) | collective-permute-done | bytes 98336 | tf_op jit(solution)/shard_map/ppermute | solution.py:69
  26.8 1.5 %collective-permute-done.8.refs_1_ = bf16[384,128]{1,0:T(8,128)(2,1)S(1)} collective-permute-done((bf16[384,128]{1,0:T(8,128)(2,1)S(1)}, bf16[384,128]{1,0:T(8,128)(2,1)S(1)}, u32[]{:S(2)}, u32[]{:S(2)}) %collective-permute-start.8) | collective-permute-done | bytes 98336 | tf_op jit(solution)/shard_map/ppermute | solution.py:69
  28.3 0.4 %backward.1 = (bf16[272,128]{1,0:T(8,128)(2,1)S(1)}, bf16[272,128]{1,0:T(8,128)(2,1)S(1)}, bf16[272,128]{1,0:T(8,128)(2,1)S(1)}, bf16[272,128]{1,0:T(8,128)(2,1)S(1)}, f32[32,512]{1,0:T(8,128)S(1)}) custom-call(bf16[384,128]{1,0:T(8,128)(2,1)S(1)} %get-tuple-element.29.refs_0_, bf16[384,128]{1,0:T(8,128)(2,1)S(1)} %collective-permute-done.8.refs_1_, ...), custom_call_target="tpu_custom_call" | custom-call | tf_op jit(solution)/shard_map/backward/pallas_call | solution.py:356
  28.8 0.1 collective-permute-start.11
  28.8 1.4 %collective-permute-start.12 = (bf16[272,128]{1,0:T(8,128)(2,1)S(1)}, bf16[272,128]{1,0:T(8,128)(2,1)S(1)}, u32[]{:S(2)}, u32[]{:S(2)}) collective-permute-start(bf16[272,128]{1,0:T(8,128)(2,1)S(1)} %get-tuple-element.32), channel_id=1, source_target_pairs={{0,16},{8,24},{16,0},{24,8},{1,17},{9,25},{17,1},{25,9},{2,18},{10... | collective-permute-start | bytes 208904 | tf_op jit(solution)/shard_map/ppermute | solution.py:69
  30.3 0.4 %collective-permute-start.13 = (bf16[272,128]{1,0:T(8,128)(2,1)S(1)}, bf16[272,128]{1,0:T(8,128)(2,1)S(1)}, u32[]{:S(2)}, u32[]{:S(2)}) collective-permute-start(bf16[272,128]{1,0:T(8,128)(2,1)S(1)} %get-tuple-element.33), channel_id=1, source_target_pairs={{0,8},{8,0},{16,24},{24,16},{1,9},{9,1},{17,25},{25,17},{2,10},{10... | collective-permute-start | bytes 208904 | tf_op jit(solution)/shard_map/ppermute | solution.py:69
  30.7 0.6 %activate.1 = f32[128,128]{1,0:T(8,128)} custom-call(f32[128,128]{1,0:T(8,128)S(1)} %get-tuple-element.28.pre), custom_call_target="tpu_custom_call" | custom-call | tf_op jit(solution)/shard_map/activate/pallas_call | solution.py:272
  31.3 2.0 %collective-permute-done.11.refs_1_ = bf16[272,128]{1,0:T(8,128)(2,1)S(1)} collective-permute-done((bf16[272,128]{1,0:T(8,128)(2,1)S(1)}, bf16[272,128]{1,0:T(8,128)(2,1)S(1)}, u32[]{:S(2)}, u32[]{:S(2)}) %collective-permute-start.11) | collective-permute-done | bytes 69664 | tf_op jit(solution)/shard_map/ppermute | solution.py:69
  33.3 1.3 %collective-permute-done.12.refs_2_ = bf16[272,128]{1,0:T(8,128)(2,1)S(1)} collective-permute-done((bf16[272,128]{1,0:T(8,128)(2,1)S(1)}, bf16[272,128]{1,0:T(8,128)(2,1)S(1)}, u32[]{:S(2)}, u32[]{:S(2)}) %collective-permute-start.12) | collective-permute-done | bytes 69664 | tf_op jit(solution)/shard_map/ppermute | solution.py:69
  34.6 0.0 collective-permute-done.13.refs_3_
  34.6 0.7 %final.1 = (bf16[32,512]{1,0:T(8,128)(2,1)}, f32[128,128]{1,0:T(8,128)}, f32[1,128]{1,0:T(1,128)}) custom-call(bf16[272,128]{1,0:T(8,128)(2,1)S(1)} %get-tuple-element.30.refs_0_, bf16[272,128]{1,0:T(8,128)(2,1)S(1)} %collective-permute-done.11.refs_1_, bf16[272,128]{1,0:T(8,128)(2,1)S(1)} %collective-permute-done.12.refs_2_, ...), custom_call_target="tpu_custom_call" | custom-call | tf_op jit(solution)/shard_map/final/pallas_call | solution.py:407
  (1 shorter events, 0.0 us)
Async XLA Ops:
  0.6 5.2 %collective-permute-start.2 = (bf16[32,512]{1,0:T(8,128)(2,1)}, bf16[32,512]{1,0:T(8,128)(2,1)S(1)}, u32[]{:S(2)}, u32[]{:S(2)}) collective-permute-start(bf16[32,512]{1,0:T(8,128)(2,1)} %bitcast.6), channel_id=1, source_target_pairs={{0,24},{8,16},{16,8},{24,0},{1,25},{9,17},{17,9},{25,1},{2,26},{10... | collective-permute-start | bytes 98312 | tf_op jit(solution)/shard_map/ppermute | solution.py:69
  3.1 4.2 %collective-permute-start.1 = (bf16[32,512]{1,0:T(8,128)(2,1)}, bf16[32,512]{1,0:T(8,128)(2,1)S(1)}, u32[]{:S(2)}, u32[]{:S(2)}) collective-permute-start(bf16[32,512]{1,0:T(8,128)(2,1)} %bitcast.7), channel_id=1, source_target_pairs={{0,16},{8,24},{16,0},{24,8},{1,17},{9,25},{17,1},{25,9},{2,18},{10... | collective-permute-start | bytes 98312 | tf_op jit(solution)/shard_map/ppermute | solution.py:69
  3.7 3.5 %collective-permute-start = (bf16[32,512]{1,0:T(8,128)(2,1)}, bf16[32,512]{1,0:T(8,128)(2,1)S(1)}, u32[]{:S(2)}, u32[]{:S(2)}) collective-permute-start(bf16[32,512]{1,0:T(8,128)(2,1)} %bitcast.8), channel_id=1, source_target_pairs={{0,8},{8,0},{16,24},{24,16},{1,9},{9,1},{17,25},{25,17},{2,10},{10... | collective-permute-start | bytes 98312 | tf_op jit(solution)/shard_map/ppermute | solution.py:69
  4.4 2.9 %copy-start.2 = (bf16[512,32]{0,1:T(8,128)(2,1)S(1)}, bf16[512,32]{0,1:T(8,128)(2,1)}, u32[]{:S(2)}) copy-start(bf16[512,32]{0,1:T(8,128)(2,1)} %param.9) | copy-start | bytes 98308
  7.3 3.9 %copy-start.1 = (f32[128,128]{1,0:T(8,128)S(1)}, f32[128,128]{1,0:T(8,128)}, u32[]{:S(2)}) copy-start(f32[128,128]{1,0:T(8,128)} %refs_5_.1) | copy-start | bytes 196612
  7.6 6.1 %collective-permute-start.3 = (bf16[128,256]{1,0:T(8,128)(2,1)S(1)}, bf16[128,256]{1,0:T(8,128)(2,1)S(1)}, u32[]{:S(2)}, u32[]{:S(2)}) collective-permute-start(bf16[128,256]{1,0:T(8,128)(2,1)S(1)} %get-tuple-element.23), channel_id=1, source_target_pairs={{0,3},{1,2},{2,1},{3,0},{4,7},{5,6},{6,5},{7,4},{8,11},{9,10},{10,... | collective-permute-start | bytes 196616 | tf_op jit(solution)/shard_map/ppermute | solution.py:69
  10.2 4.9 %collective-permute-start.4 = (bf16[128,256]{1,0:T(8,128)(2,1)S(1)}, bf16[128,256]{1,0:T(8,128)(2,1)S(1)}, u32[]{:S(2)}, u32[]{:S(2)}) collective-permute-start(bf16[128,256]{1,0:T(8,128)(2,1)S(1)} %get-tuple-element.24), channel_id=1, source_target_pairs={{0,2},{1,3},{2,0},{3,1},{4,6},{5,7},{6,4},{7,5},{8,10},{9,11},{10,... | collective-permute-start | bytes 196616 | tf_op jit(solution)/shard_map/ppermute | solution.py:69
  10.7 4.4 %collective-permute-start.5 = (bf16[128,256]{1,0:T(8,128)(2,1)S(1)}, bf16[128,256]{1,0:T(8,128)(2,1)S(1)}, u32[]{:S(2)}, u32[]{:S(2)}) collective-permute-start(bf16[128,256]{1,0:T(8,128)(2,1)S(1)} %get-tuple-element.25), channel_id=1, source_target_pairs={{0,1},{1,0},{2,3},{3,2},{4,5},{5,4},{6,7},{7,6},{8,9},{9,8},{10,11... | collective-permute-start | bytes 196616 | tf_op jit(solution)/shard_map/ppermute | solution.py:69
  11.2 6.7 %collective-permute-start.7 = (f32[128,128]{1,0:T(8,128)S(1)}, f32[128,128]{1,0:T(8,128)S(1)}, u32[]{:S(2)}, u32[]{:S(2)}) collective-permute-start(f32[128,128]{1,0:T(8,128)S(1)} %copy-done.1), channel_id=1, source_target_pairs={{0,4},{1,5},{2,6},{3,7},{4,0},{5,1},{6,2},{7,3},{8,12},{9,13},{10,... | collective-permute-start | bytes 196616 | tf_op jit(solution)/shard_map/ppermute | solution.py:74
  15.1 2.6 %copy-start = (bf16[128,128]{1,0:T(8,128)(2,1)S(1)}, bf16[128,128]{1,0:T(8,128)(2,1)}, u32[]{:S(2)}) copy-start(bf16[128,128]{1,0:T(8,128)(2,1)} %refs_4_.1) | copy-start | bytes 98308
  15.1 5.2 %collective-permute-start.6 = (bf16[128,256]{1,0:T(8,128)(2,1)S(1)}, bf16[128,256]{1,0:T(8,128)(2,1)S(1)}, u32[]{:S(2)}, u32[]{:S(2)}) collective-permute-start(bf16[128,256]{1,0:T(8,128)(2,1)S(1)} %add.1.sums.refs_0_), channel_id=1, source_target_pairs={{0,4},{1,5},{2,6},{3,7},{4,0},{5,1},{6,2},{7,3},{8,12},{9,13},{10,... | collective-permute-start | bytes 196616 | tf_op jit(solution)/shard_map/ppermute | solution.py:74
  20.7 5.0 %collective-permute-start.10 = (bf16[384,128]{1,0:T(8,128)(2,1)S(1)}, bf16[384,128]{1,0:T(8,128)(2,1)S(1)}, u32[]{:S(2)}, u32[]{:S(2)}) collective-permute-start(bf16[384,128]{1,0:T(8,128)(2,1)S(1)} %get-tuple-element.29.refs_0_), channel_id=1, source_target_pairs={{0,1},{1,0},{2,3},{3,2},{4,5},{5,4},{6,7},{7,6},{8,9},{9,8},{10,11... | collective-permute-start | bytes 294920 | tf_op jit(solution)/shard_map/ppermute | solution.py:69
  21.3 5.5 %collective-permute-start.9 = (bf16[384,128]{1,0:T(8,128)(2,1)S(1)}, bf16[384,128]{1,0:T(8,128)(2,1)S(1)}, u32[]{:S(2)}, u32[]{:S(2)}) collective-permute-start(bf16[384,128]{1,0:T(8,128)(2,1)S(1)} %get-tuple-element.29.refs_0_), channel_id=1, source_target_pairs={{0,3},{1,2},{2,1},{3,0},{4,7},{5,6},{6,5},{7,4},{8,11},{9,10},{10,... | collective-permute-start | bytes 294920 | tf_op jit(solution)/shard_map/ppermute | solution.py:69
  23.7 4.6 %collective-permute-start.8 = (bf16[384,128]{1,0:T(8,128)(2,1)S(1)}, bf16[384,128]{1,0:T(8,128)(2,1)S(1)}, u32[]{:S(2)}, u32[]{:S(2)}) collective-permute-start(bf16[384,128]{1,0:T(8,128)(2,1)S(1)} %get-tuple-element.29.refs_0_), channel_id=1, source_target_pairs={{0,2},{1,3},{2,0},{3,1},{4,6},{5,7},{6,4},{7,5},{8,10},{9,11},{10,... | collective-permute-start | bytes 294920 | tf_op jit(solution)/shard_map/ppermute | solution.py:69
  28.8 4.5 %collective-permute-start.11 = (bf16[272,128]{1,0:T(8,128)(2,1)S(1)}, bf16[272,128]{1,0:T(8,128)(2,1)S(1)}, u32[]{:S(2)}, u32[]{:S(2)}) collective-permute-start(bf16[272,128]{1,0:T(8,128)(2,1)S(1)} %get-tuple-element.31), channel_id=1, source_target_pairs={{0,24},{8,16},{16,8},{24,0},{1,25},{9,17},{17,9},{25,1},{2,26},{10... | collective-permute-start | bytes 208904 | tf_op jit(solution)/shard_map/ppermute | solution.py:69
  28.8 5.8 %collective-permute-start.12 = (bf16[272,128]{1,0:T(8,128)(2,1)S(1)}, bf16[272,128]{1,0:T(8,128)(2,1)S(1)}, u32[]{:S(2)}, u32[]{:S(2)}) collective-permute-start(bf16[272,128]{1,0:T(8,128)(2,1)S(1)} %get-tuple-element.32), channel_id=1, source_target_pairs={{0,16},{8,24},{16,0},{24,8},{1,17},{9,25},{17,1},{25,9},{2,18},{10... | collective-permute-start | bytes 208904 | tf_op jit(solution)/shard_map/ppermute | solution.py:69
  30.3 4.4 %collective-permute-start.13 = (bf16[272,128]{1,0:T(8,128)(2,1)S(1)}, bf16[272,128]{1,0:T(8,128)(2,1)S(1)}, u32[]{:S(2)}, u32[]{:S(2)}) collective-permute-start(bf16[272,128]{1,0:T(8,128)(2,1)S(1)} %get-tuple-element.33), channel_id=1, source_target_pairs={{0,8},{8,0},{16,24},{24,16},{1,9},{9,1},{17,25},{25,17},{2,10},{10... | collective-permute-start | bytes 208904 | tf_op jit(solution)/shard_map/ppermute | solution.py:69

commit v9 on v8

--- a/solution.py
+++ b/solution.py
@@ -9,6 +9,8 @@
 
 f32 = jnp.float32
 bf16 = jnp.bfloat16
+i16 = jnp.int16
+levels = 32736.0
 tail = 16
 wide = 1024
 grant = 8 * 2**20
@@ -51,6 +53,21 @@
     return index * size if isinstance(index, int) else pl.multiple_of(index * size, size)
 
 
+def code(value, out):
+    rows = value.shape[0]
+    top = jnp.max(jnp.max(jnp.abs(value), axis=0, keepdims=True), axis=1, keepdims=True)
+    power = jnp.ceil(jnp.log2(jnp.maximum(top, 1e-20)))
+    power = jnp.broadcast_to(power, (1, value.shape[1]))
+    out[:rows, :] = jnp.round(value * (jnp.exp2(-power) * levels)).astype(jnp.int32).astype(i16)
+    out[rows:, :] = jnp.broadcast_to(power, (tail, value.shape[1])).astype(jnp.int32).astype(i16)
+
+
+def decode(part):
+    whole = part[...].astype(jnp.int32).astype(f32)
+    rows = whole.shape[0] - tail
+    return whole[:rows] * (jnp.exp2(whole[rows : rows + 1]) * (1.0 / levels))
+
+
 def partner(me, step, size):
     if size & (size - 1) == 0:
         return me ^ step
@@ -74,16 +91,20 @@
     return lax.ppermute(value, axis, [(i, (i + members) % size) for i in range(size)])
 
 
-def band_kernel(place, limit, rows, cols, ids, values, bias, band, bias_out, sums, scaled, here, row, col, sems):
+def band_kernel(
+    place, limit, rows, cols, ids, values, bias, cotangent, band, bias_out, longer, sums, scaled, here, row, col, sems
+):
     blocks, tile, _ = sums.shape
     row_blocks = band.shape[1] // tile
     slots = rows.shape[-1]
     ids_here, values_here = here
     lanes = ids_here.shape[0] // slots
     pairs = ((ids, ids_here), (values, values_here), (rows, row), (cols, col), (bias, bias_out))
+    pairs = pairs + ((cotangent, longer.at[pl.ds(0, cotangent.shape[0]), :]),)
     copies = [pltpu.make_async_copy(a, b, sems.at[i]) for i, (a, b) in enumerate(pairs)]
     for copy in copies:
         copy.start()
+    longer[cotangent.shape[0] :, :] = jnp.zeros((tail, cotangent.shape[1]), f32)
 
     def clear(index):
         sums[index] = jnp.zeros((tile, tile), f32)
@@ -119,7 +140,7 @@
     each(blocks, put)
 
 
-def make_band(limit, rows, cols, ids, values, bias, row_blocks, col_blocks, members, twins):
+def make_band(limit, rows, cols, ids, values, bias, cotangent, row_blocks, col_blocks, members, twins):
     blocks_own = row_blocks // (members * twins)
 
     def place(block):
@@ -135,21 +156,21 @@
     sums = struct((col_blocks * row_blocks, tile, tile), f32)
     return pl.pallas_call(
         functools.partial(band_kernel, place),
-        out_shape=(out, struct(bias.shape, f32)),
-        in_specs=[smem()] + [pl.BlockSpec(memory_space=pltpu.HBM)] * 5,
-        out_specs=(vmem(), vmem()),
+        out_shape=(out, struct(bias.shape, f32), struct((cotangent.shape[0] + tail, cotangent.shape[1]), f32)),
+        in_specs=[smem()] + [pl.BlockSpec(memory_space=pltpu.HBM)] * 6,
+        out_specs=(vmem(),) * 3,
         scratch_shapes=[
             pltpu.VMEM(sums.shape, f32),
             pltpu.VMEM((lines, tile), f32),
             (pltpu.VMEM((lines, tile), jnp.int32), pltpu.VMEM((lines, tile), bf16)),
             pltpu.SMEM(rows.shape, jnp.int32),
             pltpu.SMEM(cols.shape, jnp.int32),
-            pltpu.SemaphoreType.DMA((5,)),
+            pltpu.SemaphoreType.DMA((6,)),
         ],
         compiler_params=pltpu.CompilerParams(vmem_limit_bytes=grant + sums.size * 4 + out.size * 2),
         cost_estimate=pl.CostEstimate(flops=8 * sums.size * 8, bytes_accessed=8 * 2**20, transcendentals=0),
         name="band",
-    )(limit, *[pltpu.with_memory_space_constraint(a, pltpu.HBM) for a in (rows, cols, ids, values, bias)])
+    )(limit, *[pltpu.with_memory_space_constraint(a, pltpu.HBM) for a in (rows, cols, ids, values, bias, cotangent)])
 
 
 def forward_kernel(size, members, *refs):
@@ -164,7 +185,11 @@
     left = panel[...].astype(bf16)
     for step, message in enumerate((kept,) + messages):
         columns = pl.ds(pl.multiple_of(partner(mine, step, members) * own, own), own)
-        message[...] = dot(left, band[:, columns]).astype(message.dtype)
+        got = dot(left, band[:, columns])
+        if step == 0:
+            kept[...] = got
+        else:
+            code(got, message)
 
 
 def forward(parts, band, members):
@@ -175,7 +200,7 @@
     panel = pltpu.VMEM((hidden, nodes), bf16 if width % 16 == 0 else f32)
     return pl.pallas_call(
         functools.partial(forward_kernel, len(parts), members),
-        out_shape=(struct(block, f32),) + (struct(block, bf16),) * (members - 1),
+        out_shape=(struct(block, f32),) + (struct((hidden + tail, block[1]), i16),) * (members - 1),
         in_specs=[vmem()] * (len(parts) + 1),
         out_specs=(vmem(),) * members,
         scratch_shapes=[panel],
@@ -188,14 +213,14 @@
     parts, out = refs[:-1], refs[-1]
     total = kept[...]
     for part in parts:
-        total = total + part[...].astype(f32)
-    out[...] = total.astype(bf16)
+        total = total + decode(part)
+    code(total, out)
 
 
 def add(kept, parts):
     return pl.pallas_call(
         add_kernel,
-        out_shape=struct(kept.shape, bf16),
+        out_shape=struct((kept.shape[0] + tail, kept.shape[1]), i16),
         in_specs=[vmem()] * (len(parts) + 1),
         out_specs=vmem(),
         compiler_params=room(kept),
@@ -209,69 +234,82 @@
     return jnp.where(row == 0, high, jnp.where(row == 1, line - high, 0.0))
 
 
-def apply_kernel(sums, weight, out):
-    out[...] = dot(sums[...], weight[...], 0, 0)
-
-
-def apply_weight(sums, weight):
-    return pl.pallas_call(
-        apply_kernel,
-        out_shape=struct((sums.shape[1], weight.shape[1]), f32),
-        in_specs=[vmem()] * 2,
-        out_specs=vmem(),
-        compiler_params=room(sums),
-        name="apply_weight",
-    )(sums, weight)
-
-
-def own_kernel(members, twins, *refs):
-    sums, (weight, bias, first), cotangents = refs[:twins], refs[twins : twins + 3], refs[twins + 3 : 2 * twins + 3]
-    pre_out, message, wide_pre, given = refs[2 * twins + 3 :]
+def parts_of(value):
+    high = value.astype(bf16)
+    return high, (value - high.astype(f32)).astype(bf16)
+
+
+def apply(value, weight):
+    high, low = parts_of(value)
+    return dot(high, weight[...], 0, 0) + dot(low, weight[...], 0, 0)
+
+
+def before_kernel(members, twins, *refs):
+    cotangents, (sums, weight, whole, first, given) = refs[:twins], refs[twins:]
     mine = lax.axis_index("col") // members
     own = cotangents[0].shape[0]
     for index, part in enumerate(cotangents):
         place = mine if index == 0 else twins - 1 - mine
-        given[pl.ds(pl.multiple_of(place * own, own), own), :] = part[...]
-    pre = first[...]
-    for part in sums[1:]:
-        pre = pre + dot(part[...], weight[...], 0, 0)
+        given[pl.ds(pl.multiple_of(place * own, own), own), :] = part[:own, :]
+    value = decode(sums)
+    whole[...] = value
+    first[...] = apply(value, weight)
+
+
+def before(cotangents, sums, weight, members):
+    hidden, rows = sums.shape[0] - tail, sums.shape[1]
+    product = struct((rows, weight.shape[1]), f32)
+    return pl.pallas_call(
+        functools.partial(before_kernel, members, len(cotangents)),
+        out_shape=(struct((hidden, rows), f32), product, product),
+        in_specs=[vmem()] * (len(cotangents) + 2),
+        out_specs=(vmem(),) * 3,
+        compiler_params=room(sums),
+        name="before",
+    )(*cotangents, sums, weight)
+
+
+def own_kernel(weight, bias, whole, first, given, *refs):
+    others, (pre_out, message) = refs[:-2], refs[-2:]
+    total, pre = whole[...], first[...]
+    for part in others:
+        value = decode(part)
+        total = total + value
+        pre = pre + apply(value, weight)
     pre = pre + bias[...]
-    wide_pre[...] = pre
+    pre_out[...] = pre
     squashed = jax.nn.sigmoid(pre)
     grad = given[...] * squashed * (1.0 + pre * (1.0 - squashed))
     grad = grad.astype(bf16)
     rows = grad.shape[0]
     message[:rows, :] = grad
-    weight_part = dot(sums[0][...], grad)
-    for part in sums[1:]:
-        weight_part = weight_part + dot(part[...], grad)
-    message[rows:, :] = weight_part.astype(bf16)
-    pre_out[...] = wide_pre[pl.ds(pl.multiple_of(mine * own, own), own), :]
-
-
-def own_rows(sums, weight, bias, first, cotangents, members):
-    twins = len(sums)
-    hidden, rows = sums[0].shape
-    own = cotangents[0].shape[0]
-    return pl.pallas_call(
-        functools.partial(own_kernel, members, twins),
-        out_shape=(struct((own, hidden), f32), struct((rows + hidden, hidden), bf16)),
-        in_specs=[vmem()] * (2 * twins + 3),
+    high, low = parts_of(total)
+    message[rows:, :] = (dot(high, grad) + dot(low, grad)).astype(bf16)
+
+
+def own_rows(whole, first, given, weight, bias, others):
+    hidden, rows = whole.shape
+    return pl.pallas_call(
+        own_kernel,
+        out_shape=(struct((rows, hidden), f32), struct((rows + hidden, hidden), bf16)),
+        in_specs=[vmem()] * (5 + len(others)),
         out_specs=(vmem(),) * 2,
-        scratch_shapes=[pltpu.VMEM((rows, hidden), f32), pltpu.VMEM((rows, hidden), f32)],
-        compiler_params=room(*sums),
+        compiler_params=room(whole),
         name="own_rows",
-    )(*sums, weight, bias, first, *cotangents)
-
-
-def activate_kernel(pre, act):
-    act[...] = pre[...] * jax.nn.sigmoid(pre[...])
-
-
-def activate(pre):
-    return pl.pallas_call(
-        activate_kernel,
-        out_shape=struct(pre.shape, f32),
+    )(weight, bias, whole, first, given, *others)
+
+
+def activate_kernel(members, pre, act):
+    own = act.shape[0]
+    mine = lax.axis_index("col") // members
+    kept = pre[pl.ds(pl.multiple_of(mine * own, own), own), :]
+    act[...] = kept * jax.nn.sigmoid(kept)
+
+
+def activate(pre, own, members):
+    return pl.pallas_call(
+        functools.partial(activate_kernel, members),
+        out_shape=struct((own, pre.shape[1]), f32),
         in_specs=[vmem()],
         out_specs=vmem(),
         compiler_params=room(pre),
@@ -438,21 +476,19 @@
     col_blocks = blocks_own * size
     turned = features.T
     parts = [turned] + [exchange(turned, "row", step, size) for step in range(1, size)]
-    band, bias = make_band(
-        tile_count, tile_rows, tile_cols, neighbours, edge_weights, bias_vector, row_blocks, col_blocks, members, twins
+    band, bias, longer = make_band(
+        tile_count, tile_rows, tile_cols, neighbours, edge_weights, bias_vector, cotangent, row_blocks, col_blocks, members, twins
     )
     kept, *messages = forward(parts, band, members)
     got = [exchange(message, "col", step + 1, members) for step, message in enumerate(messages)]
     cotangents = [cotangent]
     if twins > 1:
-        other, messages[0] = lax.optimization_barrier((cotangent, messages[0]))
-        cotangents.append(exchange_twin(other, "col", members))
-    sums = [add(kept, got[::-1])]
-    if twins > 1:
-        sums.append(exchange_twin(sums[0], "col", members))
-    first = apply_weight(sums[0], weight)
-    pre, message = own_rows(sums, weight, bias, first, cotangents, members)
-    activations = activate(pre)
+        cotangents.append(exchange_twin(longer, "col", members))
+    sums = add(kept, got[::-1])
+    others = [exchange_twin(sums, "col", members)] if twins > 1 else []
+    whole, first, given = before(cotangents, sums, weight, members)
+    pre, message = own_rows(whole, first, given, weight, bias, others)
+    activations = activate(pre, cotangent.shape[0], members)
     got = [message] + [exchange(message, "col", step, members) for step in range(1, members)]
     *messages, kept = backward(got, weight, band, size)
     messages = [messages[0]] + [exchange(messages[step], "row", step, size) for step in range(1, size)]

time: 35.6 us -> 36.5 us (1.025); the launches traced: 35.3 us -> 36.6 us
  waiting for transfers between devices: 12.1 us -> 12.8 us
  Pallas kernels: 4.53 us -> 5.04 us
    ppermute x2, waiting for transfers between devices: 2.45 us -> 3.21 us  [exchange_twin(): lax.ppermute(value, axis, [(i, (i + members) % size) for i in range(size)])]
where the time goes in v9:
time: 36.5 us; the launch traced here: 36.6 us
  starting transfers between devices  17.4 us (48%)
  waiting for transfers between devices  12.8 us (35%)
  Pallas kernels  5.04 us (14%)
  between operations  1.38 us (4%)
    ppermute x12, starting transfers between devices, exchange(): return lax.ppermute(value, axis, pairs)  12.2 us
    ppermute x12, waiting for transfers between devices, exchange(): return lax.ppermute(value, axis, pairs)  9.55 us
    ppermute x2, starting transfers between devices, exchange_twin(): lax.ppermute(value, axis, [(i, (i + members) % size) for i in range(size)])  5.24 us
    ppermute x2, waiting for transfers between devices, exchange_twin(): lax.ppermute(value, axis, [(i, (i + members) % size) for i in range(size)])  3.21 us
    pallas_call x1, Pallas kernels, make_band(): pl.pallas_call(functools.partial(band_kernel, place), out_shape=(out, str...  1.53 us
  transfers between devices with their start and end apart: 14, of which 8 were waited for; matrix products, arithmetic and copies ran while one was open for 0% of the time, Pallas kernels for 8%

profile of v9, /device:TPU:0, one launch (start us, length us, event | category | flops | bytes accessed | tf_op | source)
XLA Modules:
  0.0 36.6 jit_solution(5975775518935896172)
XLA Ops:
  0.6 2.5 %collective-permute-start.3 = (bf16[32,512]{1,0:T(8,128)(2,1)}, bf16[32,512]{1,0:T(8,128)(2,1)S(1)}, u32[]{:S(2)}, u32[]{:S(2)}) collective-permute-start(bf16[32,512]{1,0:T(8,128)(2,1)} %bitcast.6), channel_id=1, source_target_pairs={{0,24},{8,16},{16,8},{24,0},{1,25},{9,17},{17,9},{25,1},{2,26},{10... | collective-permute-start | bytes 98312 | tf_op jit(solution)/shard_map/ppermute | solution.py:86
  3.1 0.6 %collective-permute-start.2 = (bf16[32,512]{1,0:T(8,128)(2,1)}, bf16[32,512]{1,0:T(8,128)(2,1)S(1)}, u32[]{:S(2)}, u32[]{:S(2)}) collective-permute-start(bf16[32,512]{1,0:T(8,128)(2,1)} %bitcast.7), channel_id=1, source_target_pairs={{0,16},{8,24},{16,0},{24,8},{1,17},{9,25},{17,1},{25,9},{2,18},{10... | collective-permute-start | bytes 98312 | tf_op jit(solution)/shard_map/ppermute | solution.py:86
  3.7 0.0 collective-permute-start.1
  4.4 0.0 copy-start.2
  4.4 1.5 %band.1 = (bf16[512,1024]{1,0:T(8,128)(2,1)S(1)}, f32[1,128]{1,0:T(1,128)S(1)}, f32[144,128]{1,0:T(8,128)S(1)}) custom-call(s32[1,1]{1,0:T(1,128)S(6)} %copy.13.limit, s32[1,1,128]{2,1,0:T(1,128)} %rows.1, s32[1,1,128]{2,1,0:T(1,128)} %cols.1, s32[256,128]{1,0:T(8,128)} %bitcast.10, bf16[256,128]{1,0:T(8,128)(2,1)} %bitcast.11, f32[1,128]{1,0:T(1,128)} %bitcast.12, ...), custom_call_target="tpu_custom_call" | custom-call | flops 33554432 | bytes 8388608 | tf_op jit(solution)/shard_map/band/pallas_call | solution.py:157
  6.0 0.0 collective-permute-done.3.refs_3_
  6.0 1.3 %collective-permute-done.2.refs_2_ = bf16[32,512]{1,0:T(8,128)(2,1)S(1)} collective-permute-done((bf16[32,512]{1,0:T(8,128)(2,1)}, bf16[32,512]{1,0:T(8,128)(2,1)S(1)}, u32[]{:S(2)}, u32[]{:S(2)}) %collective-permute-start.2) | collective-permute-done | bytes 32800 | tf_op jit(solution)/shard_map/ppermute | solution.py:86
  7.3 0.0 collective-permute-done.1.refs_1_
  7.3 0.0 copy-done.2
  7.3 0.5 %forward.1 = (f32[128,256]{1,0:T(8,128)S(1)}, s16[144,256]{1,0:T(8,128)(2,1)S(1)}, s16[144,256]{1,0:T(8,128)(2,1)S(1)}, s16[144,256]{1,0:T(8,128)(2,1)S(1)}) custom-call(bf16[32,512]{1,0:T(8,128)(2,1)S(1)} %bitcast.9, bf16[32,512]{1,0:T(8,128)(2,1)S(1)} %collective-permute-done.1.refs_1_, bf16[32,512]{1,0:T(8,128)(2,1)S(1)} %collective-permute-done.2.refs_2_, ...), custom_call_target="tpu_custom_call" | custom-call | tf_op jit(solution)/shard_map/forward/pallas_call | solution.py:201
  7.8 2.6 %collective-permute-start.4 = (s16[144,256]{1,0:T(8,128)(2,1)S(1)}, s16[144,256]{1,0:T(8,128)(2,1)S(1)}, u32[]{:S(2)}, u32[]{:S(2)}) collective-permute-start(s16[144,256]{1,0:T(8,128)(2,1)S(1)} %get-tuple-element.28), channel_id=1, source_target_pairs={{0,3},{1,2},{2,1},{3,0},{4,7},{5,6},{6,5},{7,4},{8,11},{9,10},{10,... | collective-permute-start | bytes 221192 | tf_op jit(solution)/shard_map/ppermute | solution.py:86
  10.3 0.5 %collective-permute-start.5 = (s16[144,256]{1,0:T(8,128)(2,1)S(1)}, s16[144,256]{1,0:T(8,128)(2,1)S(1)}, u32[]{:S(2)}, u32[]{:S(2)}) collective-permute-start(s16[144,256]{1,0:T(8,128)(2,1)S(1)} %get-tuple-element.29), channel_id=1, source_target_pairs={{0,2},{1,3},{2,0},{3,1},{4,6},{5,7},{6,4},{7,5},{8,10},{9,11},{10,... | collective-permute-start | bytes 221192 | tf_op jit(solution)/shard_map/ppermute | solution.py:86
  10.8 0.5 %collective-permute-start.6 = (s16[144,256]{1,0:T(8,128)(2,1)S(1)}, s16[144,256]{1,0:T(8,128)(2,1)S(1)}, u32[]{:S(2)}, u32[]{:S(2)}) collective-permute-start(s16[144,256]{1,0:T(8,128)(2,1)S(1)} %get-tuple-element.30), channel_id=1, source_target_pairs={{0,1},{1,0},{2,3},{3,2},{4,5},{5,4},{6,7},{7,6},{8,9},{9,8},{10,11... | collective-permute-start | bytes 221192 | tf_op jit(solution)/shard_map/ppermute | solution.py:86
  11.3 2.6 %collective-permute-start = (f32[144,128]{1,0:T(8,128)S(1)}, f32[144,128]{1,0:T(8,128)S(1)}, u32[]{:S(2)}, u32[]{:S(2)}) collective-permute-start(f32[144,128]{1,0:T(8,128)S(1)} %get-tuple-element.25), channel_id=1, source_target_pairs={{0,4},{1,5},{2,6},{3,7},{4,0},{5,1},{6,2},{7,3},{8,12},{9,13},{10,... | collective-permute-start | bytes 221192 | tf_op jit(solution)/shard_map/ppermute | solution.py:91
  13.9 0.0 collective-permute-done.4.refs_0_
  13.9 1.6 %collective-permute-done.5.refs_1_ = s16[144,256]{1,0:T(8,128)(2,1)S(1)} collective-permute-done((s16[144,256]{1,0:T(8,128)(2,1)S(1)}, s16[144,256]{1,0:T(8,128)(2,1)S(1)}, u32[]{:S(2)}, u32[]{:S(2)}) %collective-permute-start.5) | collective-permute-done | bytes 73760 | tf_op jit(solution)/shard_map/ppermute | solution.py:86
  15.5 0.0 collective-permute-done.6.refs_2_
  15.5 0.0 copy-start
  15.5 0.0 copy-start.1
  15.5 0.2 add.1.refs_2_
  15.7 2.6 %collective-permute-start.7 = (s16[144,256]{1,0:T(8,128)(2,1)S(1)}, s16[144,256]{1,0:T(8,128)(2,1)S(1)}, u32[]{:S(2)}, u32[]{:S(2)}) collective-permute-start(s16[144,256]{1,0:T(8,128)(2,1)S(1)} %add.1.refs_2_), channel_id=1, source_target_pairs={{0,4},{1,5},{2,6},{3,7},{4,0},{5,1},{6,2},{7,3},{8,12},{9,13},{10,... | collective-permute-start | bytes 221192 | tf_op jit(solution)/shard_map/ppermute | solution.py:91
  18.3 0.0 collective-permute-done.refs_1_
  18.3 0.0 copy-done
  18.3 0.0 copy-done.1
  18.3 0.2 before.1
  18.6 3.2 %collective-permute-done.7.refs_0_ = s16[144,256]{1,0:T(8,128)(2,1)S(1)} collective-permute-done((s16[144,256]{1,0:T(8,128)(2,1)S(1)}, s16[144,256]{1,0:T(8,128)(2,1)S(1)}, u32[]{:S(2)}, u32[]{:S(2)}) %collective-permute-start.7) | collective-permute-done | bytes 73760 | tf_op jit(solution)/shard_map/ppermute | solution.py:91
  21.8 0.5 %own_rows.1 = (f32[256,128]{1,0:T(8,128)S(1)}, bf16[384,128]{1,0:T(8,128)(2,1)S(1)}) custom-call(bf16[128,128]{1,0:T(8,128)(2,1)S(1)} %copy-done, f32[1,128]{1,0:T(1,128)S(1)} %get-tuple-element.24.bias, f32[128,256]{1,0:T(8,128)S(1)} %get-tuple-element.31.whole, f32[256,128]{1,0:T(8,128)S(1)} %get-tuple-element.32.first, ...), custom_call_target="tpu_custom_call" | custom-call | tf_op jit(solution)/shard_map/own_rows/pallas_call | solution.py:292
  22.2 0.1 collective-permute-start.10
  22.3 2.0 %collective-permute-start.9 = (bf16[384,128]{1,0:T(8,128)(2,1)S(1)}, bf16[384,128]{1,0:T(8,128)(2,1)S(1)}, u32[]{:S(2)}, u32[]{:S(2)}) collective-permute-start(bf16[384,128]{1,0:T(8,128)(2,1)S(1)} %get-tuple-element.35.refs_0_), channel_id=1, source_target_pairs={{0,3},{1,2},{2,1},{3,0},{4,7},{5,6},{6,5},{7,4},{8,11},{9,10},{10,... | collective-permute-start | bytes 294920 | tf_op jit(solution)/shard_map/ppermute | solution.py:86
  24.3 1.5 %collective-permute-start.8 = (bf16[384,128]{1,0:T(8,128)(2,1)S(1)}, bf16[384,128]{1,0:T(8,128)(2,1)S(1)}, u32[]{:S(2)}, u32[]{:S(2)}) collective-permute-start(bf16[384,128]{1,0:T(8,128)(2,1)S(1)} %get-tuple-element.35.refs_0_), channel_id=1, source_target_pairs={{0,2},{1,3},{2,0},{3,1},{4,6},{5,7},{6,4},{7,5},{8,10},{9,11},{10,... | collective-permute-start | bytes 294920 | tf_op jit(solution)/shard_map/ppermute | solution.py:86
  25.8 1.1 %collective-permute-done.10.refs_1_.refs_3_ = bf16[384,128]{1,0:T(8,128)(2,1)S(1)} collective-permute-done((bf16[384,128]{1,0:T(8,128)(2,1)S(1)}, bf16[384,128]{1,0:T(8,128)(2,1)S(1)}, u32[]{:S(2)}, u32[]{:S(2)}) %collective-permute-start.10) | collective-permute-done | bytes 98336 | tf_op jit(solution)/shard_map/ppermute | solution.py:86
  26.9 0.4 %early.1.refs_6_ = f32[128,512]{1,0:T(8,128)S(1)} custom-call(bf16[384,128]{1,0:T(8,128)(2,1)S(1)} %get-tuple-element.35.refs_0_, bf16[384,128]{1,0:T(8,128)(2,1)S(1)} %collective-permute-done.10.refs_1_.refs_3_, bf16[128,128]{1,0:T(8,128)(2,1)S(1)} %copy-done, bf16[512,1024]{1,0:T(8,128)(2,1)S(1)} %get-tuple-element.26.refs_4_.refs_3_.refs_5_), custom_call_target="tpu_custom_call" | custom-call | tf_op jit(solution)/shard_map/early/pallas_call | solution.py:384
  27.3 0.6 %collective-permute-done.9.refs_2_ = bf16[384,128]{1,0:T(8,128)(2,1)S(1)} collective-permute-done((bf16[384,128]{1,0:T(8,128)(2,1)S(1)}, bf16[384,128]{1,0:T(8,128)(2,1)S(1)}, u32[]{:S(2)}, u32[]{:S(2)}) %collective-permute-start.9) | collective-permute-done | bytes 98336 | tf_op jit(solution)/shard_map/ppermute | solution.py:86
  28.0 1.5 %collective-permute-done.8.refs_1_ = bf16[384,128]{1,0:T(8,128)(2,1)S(1)} collective-permute-done((bf16[384,128]{1,0:T(8,128)(2,1)S(1)}, bf16[384,128]{1,0:T(8,128)(2,1)S(1)}, u32[]{:S(2)}, u32[]{:S(2)}) %collective-permute-start.8) | collective-permute-done | bytes 98336 | tf_op jit(solution)/shard_map/ppermute | solution.py:86
  29.4 0.4 %backward.1 = (bf16[272,128]{1,0:T(8,128)(2,1)S(1)}, bf16[272,128]{1,0:T(8,128)(2,1)S(1)}, bf16[272,128]{1,0:T(8,128)(2,1)S(1)}, bf16[272,128]{1,0:T(8,128)(2,1)S(1)}, f32[32,512]{1,0:T(8,128)S(1)}) custom-call(bf16[384,128]{1,0:T(8,128)(2,1)S(1)} %get-tuple-element.35.refs_0_, bf16[384,128]{1,0:T(8,128)(2,1)S(1)} %collective-permute-done.8.refs_1_, ...), custom_call_target="tpu_custom_call" | custom-call | tf_op jit(solution)/shard_map/backward/pallas_call | solution.py:394
  29.9 0.2 collective-permute-start.11
  30.0 1.6 %collective-permute-start.12 = (bf16[272,128]{1,0:T(8,128)(2,1)S(1)}, bf16[272,128]{1,0:T(8,128)(2,1)S(1)}, u32[]{:S(2)}, u32[]{:S(2)}) collective-permute-start(bf16[272,128]{1,0:T(8,128)(2,1)S(1)} %get-tuple-element.38), channel_id=1, source_target_pairs={{0,16},{8,24},{16,0},{24,8},{1,17},{9,25},{17,1},{25,9},{2,18},{10... | collective-permute-start | bytes 208904 | tf_op jit(solution)/shard_map/ppermute | solution.py:86
  31.6 0.2 collective-permute-start.13
  31.8 0.6 %activate.1 = f32[128,128]{1,0:T(8,128)} custom-call(f32[256,128]{1,0:T(8,128)S(1)} %get-tuple-element.34.pre), custom_call_target="tpu_custom_call" | custom-call | tf_op jit(solution)/shard_map/activate/pallas_call | solution.py:310
  32.5 1.8 %collective-permute-done.11.refs_1_ = bf16[272,128]{1,0:T(8,128)(2,1)S(1)} collective-permute-done((bf16[272,128]{1,0:T(8,128)(2,1)S(1)}, bf16[272,128]{1,0:T(8,128)(2,1)S(1)}, u32[]{:S(2)}, u32[]{:S(2)}) %collective-permute-start.11) | collective-permute-done | bytes 69664 | tf_op jit(solution)/shard_map/ppermute | solution.py:86
  34.2 1.7 %collective-permute-done.12.refs_2_ = bf16[272,128]{1,0:T(8,128)(2,1)S(1)} collective-permute-done((bf16[272,128]{1,0:T(8,128)(2,1)S(1)}, bf16[272,128]{1,0:T(8,128)(2,1)S(1)}, u32[]{:S(2)}, u32[]{:S(2)}) %collective-permute-start.12) | collective-permute-done | bytes 69664 | tf_op jit(solution)/shard_map/ppermute | solution.py:86
  35.9 0.0 collective-permute-done.13.refs_3_
  35.9 0.7 %final.1 = (bf16[32,512]{1,0:T(8,128)(2,1)}, f32[128,128]{1,0:T(8,128)}, f32[1,128]{1,0:T(1,128)}) custom-call(bf16[272,128]{1,0:T(8,128)(2,1)S(1)} %get-tuple-element.36.refs_0_, bf16[272,128]{1,0:T(8,128)(2,1)S(1)} %collective-permute-done.11.refs_1_, bf16[272,128]{1,0:T(8,128)(2,1)S(1)} %collective-permute-done.12.refs_2_, ...), custom_call_target="tpu_custom_call" | custom-call | tf_op jit(solution)/shard_map/final/pallas_call | solution.py:445
Async XLA Ops:
  0.6 5.3 %collective-permute-start.3 = (bf16[32,512]{1,0:T(8,128)(2,1)}, bf16[32,512]{1,0:T(8,128)(2,1)S(1)}, u32[]{:S(2)}, u32[]{:S(2)}) collective-permute-start(bf16[32,512]{1,0:T(8,128)(2,1)} %bitcast.6), channel_id=1, source_target_pairs={{0,24},{8,16},{16,8},{24,0},{1,25},{9,17},{17,9},{25,1},{2,26},{10... | collective-permute-start | bytes 98312 | tf_op jit(solution)/shard_map/ppermute | solution.py:86
  3.1 4.2 %collective-permute-start.2 = (bf16[32,512]{1,0:T(8,128)(2,1)}, bf16[32,512]{1,0:T(8,128)(2,1)S(1)}, u32[]{:S(2)}, u32[]{:S(2)}) collective-permute-start(bf16[32,512]{1,0:T(8,128)(2,1)} %bitcast.7), channel_id=1, source_target_pairs={{0,16},{8,24},{16,0},{24,8},{1,17},{9,25},{17,1},{25,9},{2,18},{10... | collective-permute-start | bytes 98312 | tf_op jit(solution)/shard_map/ppermute | solution.py:86
  3.7 3.5 %collective-permute-start.1 = (bf16[32,512]{1,0:T(8,128)(2,1)}, bf16[32,512]{1,0:T(8,128)(2,1)S(1)}, u32[]{:S(2)}, u32[]{:S(2)}) collective-permute-start(bf16[32,512]{1,0:T(8,128)(2,1)} %bitcast.8), channel_id=1, source_target_pairs={{0,8},{8,0},{16,24},{24,16},{1,9},{9,1},{17,25},{25,17},{2,10},{10... | collective-permute-start | bytes 98312 | tf_op jit(solution)/shard_map/ppermute | solution.py:86
  4.4 2.9 %copy-start.2 = (bf16[512,32]{0,1:T(8,128)(2,1)S(1)}, bf16[512,32]{0,1:T(8,128)(2,1)}, u32[]{:S(2)}) copy-start(bf16[512,32]{0,1:T(8,128)(2,1)} %param.9) | copy-start | bytes 98308
  7.8 6.1 %collective-permute-start.4 = (s16[144,256]{1,0:T(8,128)(2,1)S(1)}, s16[144,256]{1,0:T(8,128)(2,1)S(1)}, u32[]{:S(2)}, u32[]{:S(2)}) collective-permute-start(s16[144,256]{1,0:T(8,128)(2,1)S(1)} %get-tuple-element.28), channel_id=1, source_target_pairs={{0,3},{1,2},{2,1},{3,0},{4,7},{5,6},{6,5},{7,4},{8,11},{9,10},{10,... | collective-permute-start | bytes 221192 | tf_op jit(solution)/shard_map/ppermute | solution.py:86
  10.3 5.2 %collective-permute-start.5 = (s16[144,256]{1,0:T(8,128)(2,1)S(1)}, s16[144,256]{1,0:T(8,128)(2,1)S(1)}, u32[]{:S(2)}, u32[]{:S(2)}) collective-permute-start(s16[144,256]{1,0:T(8,128)(2,1)S(1)} %get-tuple-element.29), channel_id=1, source_target_pairs={{0,2},{1,3},{2,0},{3,1},{4,6},{5,7},{6,4},{7,5},{8,10},{9,11},{10,... | collective-permute-start | bytes 221192 | tf_op jit(solution)/shard_map/ppermute | solution.py:86
  10.8 4.7 %collective-permute-start.6 = (s16[144,256]{1,0:T(8,128)(2,1)S(1)}, s16[144,256]{1,0:T(8,128)(2,1)S(1)}, u32[]{:S(2)}, u32[]{:S(2)}) collective-permute-start(s16[144,256]{1,0:T(8,128)(2,1)S(1)} %get-tuple-element.30), channel_id=1, source_target_pairs={{0,1},{1,0},{2,3},{3,2},{4,5},{5,4},{6,7},{7,6},{8,9},{9,8},{10,11... | collective-permute-start | bytes 221192 | tf_op jit(solution)/shard_map/ppermute | solution.py:86
  11.3 7.0 %collective-permute-start = (f32[144,128]{1,0:T(8,128)S(1)}, f32[144,128]{1,0:T(8,128)S(1)}, u32[]{:S(2)}, u32[]{:S(2)}) collective-permute-start(f32[144,128]{1,0:T(8,128)S(1)} %get-tuple-element.25), channel_id=1, source_target_pairs={{0,4},{1,5},{2,6},{3,7},{4,0},{5,1},{6,2},{7,3},{8,12},{9,13},{10,... | collective-permute-start | bytes 221192 | tf_op jit(solution)/shard_map/ppermute | solution.py:91
  15.5 2.8 %copy-start = (bf16[128,128]{1,0:T(8,128)(2,1)S(1)}, bf16[128,128]{1,0:T(8,128)(2,1)}, u32[]{:S(2)}) copy-start(bf16[128,128]{1,0:T(8,128)(2,1)} %refs_4_.1) | copy-start | bytes 98308
  15.5 2.8 %copy-start.1 = (f32[128,128]{1,0:T(8,128)S(1)}, f32[128,128]{1,0:T(8,128)}, u32[]{:S(2)}) copy-start(f32[128,128]{1,0:T(8,128)} %refs_0_.1) | copy-start | bytes 196612
  15.7 6.1 %collective-permute-start.7 = (s16[144,256]{1,0:T(8,128)(2,1)S(1)}, s16[144,256]{1,0:T(8,128)(2,1)S(1)}, u32[]{:S(2)}, u32[]{:S(2)}) collective-permute-start(s16[144,256]{1,0:T(8,128)(2,1)S(1)} %add.1.refs_2_), channel_id=1, source_target_pairs={{0,4},{1,5},{2,6},{3,7},{4,0},{5,1},{6,2},{7,3},{8,12},{9,13},{10,... | collective-permute-start | bytes 221192 | tf_op jit(solution)/shard_map/ppermute | solution.py:91
  22.2 4.7 %collective-permute-start.10 = (bf16[384,128]{1,0:T(8,128)(2,1)S(1)}, bf16[384,128]{1,0:T(8,128)(2,1)S(1)}, u32[]{:S(2)}, u32[]{:S(2)}) collective-permute-start(bf16[384,128]{1,0:T(8,128)(2,1)S(1)} %get-tuple-element.35.refs_0_), channel_id=1, source_target_pairs={{0,1},{1,0},{2,3},{3,2},{4,5},{5,4},{6,7},{7,6},{8,9},{9,8},{10,11... | collective-permute-start | bytes 294920 | tf_op jit(solution)/shard_map/ppermute | solution.py:86
  22.3 5.7 %collective-permute-start.9 = (bf16[384,128]{1,0:T(8,128)(2,1)S(1)}, bf16[384,128]{1,0:T(8,128)(2,1)S(1)}, u32[]{:S(2)}, u32[]{:S(2)}) collective-permute-start(bf16[384,128]{1,0:T(8,128)(2,1)S(1)} %get-tuple-element.35.refs_0_), channel_id=1, source_target_pairs={{0,3},{1,2},{2,1},{3,0},{4,7},{5,6},{6,5},{7,4},{8,11},{9,10},{10,... | collective-permute-start | bytes 294920 | tf_op jit(solution)/shard_map/ppermute | solution.py:86
  24.3 5.1 %collective-permute-start.8 = (bf16[384,128]{1,0:T(8,128)(2,1)S(1)}, bf16[384,128]{1,0:T(8,128)(2,1)S(1)}, u32[]{:S(2)}, u32[]{:S(2)}) collective-permute-start(bf16[384,128]{1,0:T(8,128)(2,1)S(1)} %get-tuple-element.35.refs_0_), channel_id=1, source_target_pairs={{0,2},{1,3},{2,0},{3,1},{4,6},{5,7},{6,4},{7,5},{8,10},{9,11},{10,... | collective-permute-start | bytes 294920 | tf_op jit(solution)/shard_map/ppermute | solution.py:86
  29.9 4.4 %collective-permute-start.11 = (bf16[272,128]{1,0:T(8,128)(2,1)S(1)}, bf16[272,128]{1,0:T(8,128)(2,1)S(1)}, u32[]{:S(2)}, u32[]{:S(2)}) collective-permute-start(bf16[272,128]{1,0:T(8,128)(2,1)S(1)} %get-tuple-element.37), channel_id=1, source_target_pairs={{0,24},{8,16},{16,8},{24,0},{1,25},{9,17},{17,9},{25,1},{2,26},{10... | collective-permute-start | bytes 208904 | tf_op jit(solution)/shard_map/ppermute | solution.py:86
  30.0 5.9 %collective-permute-start.12 = (bf16[272,128]{1,0:T(8,128)(2,1)S(1)}, bf16[272,128]{1,0:T(8,128)(2,1)S(1)}, u32[]{:S(2)}, u32[]{:S(2)}) collective-permute-start(bf16[272,128]{1,0:T(8,128)(2,1)S(1)} %get-tuple-element.38), channel_id=1, source_target_pairs={{0,16},{8,24},{16,0},{24,8},{1,17},{9,25},{17,1},{25,9},{2,18},{10... | collective-permute-start | bytes 208904 | tf_op jit(solution)/shard_map/ppermute | solution.py:86
  31.6 4.3 %collective-permute-start.13 = (bf16[272,128]{1,0:T(8,128)(2,1)S(1)}, bf16[272,128]{1,0:T(8,128)(2,1)S(1)}, u32[]{:S(2)}, u32[]{:S(2)}) collective-permute-start(bf16[272,128]{1,0:T(8,128)(2,1)S(1)} %get-tuple-element.39), channel_id=1, source_target_pairs={{0,8},{8,0},{16,24},{24,16},{1,9},{9,1},{17,25},{25,17},{2,10},{10... | collective-permute-start | bytes 208904 | tf_op jit(solution)/shard_map/ppermute | solution.py:86

commit v10 on v9

--- a/solution.py
+++ b/solution.py
@@ -55,9 +55,8 @@
 
 def code(value, out):
     rows = value.shape[0]
-    top = jnp.max(jnp.max(jnp.abs(value), axis=0, keepdims=True), axis=1, keepdims=True)
+    top = jnp.max(jnp.abs(value), axis=0, keepdims=True)
     power = jnp.ceil(jnp.log2(jnp.maximum(top, 1e-20)))
-    power = jnp.broadcast_to(power, (1, value.shape[1]))
     out[:rows, :] = jnp.round(value * (jnp.exp2(-power) * levels)).astype(jnp.int32).astype(i16)
     out[rows:, :] = jnp.broadcast_to(power, (tail, value.shape[1])).astype(jnp.int32).astype(i16)
 

time: 36.5 us -> 35.7 us (0.978)
  waiting for transfers between devices: 12.8 us -> 11.6 us
    ppermute x12, waiting for transfers between devices: 9.55 us -> 8.58 us  [exchange(): return lax.ppermute(value, axis, pairs)]
where the time goes in v10:
time: 35.7 us; the launch traced here: 35.6 us
  starting transfers between devices  17.6 us (49%)
  waiting for transfers between devices  11.6 us (32%)
  Pallas kernels  4.99 us (14%)
  between operations  1.38 us (4%)
    ppermute x12, starting transfers between devices, exchange(): return lax.ppermute(value, axis, pairs)  12.2 us
    ppermute x12, waiting for transfers between devices, exchange(): return lax.ppermute(value, axis, pairs)  8.58 us
    ppermute x2, starting transfers between devices, exchange_twin(): lax.ppermute(value, axis, [(i, (i + members) % size) for i in range(size)])  5.38 us
    ppermute x2, waiting for transfers between devices, exchange_twin(): lax.ppermute(value, axis, [(i, (i + members) % size) for i in range(size)])  3.07 us
    pallas_call x1, Pallas kernels, make_band(): pl.pallas_call(functools.partial(band_kernel, place), out_shape=(out, str...  1.62 us
    pallas_call x1, Pallas kernels, final(): pl.pallas_call(functools.partial(final_kernel, order, size, shrink), out_...  0.72 us
  transfers between devices with their start and end apart: 14, of which 8 were waited for; matrix products, arithmetic and copies ran while one was open for 0% of the time, Pallas kernels for 8%

profile of v10, /device:TPU:0, one launch (start us, length us, event | category | flops | bytes accessed | tf_op | source)
XLA Modules:
  0.0 35.6 jit_solution(8903773073075502929)
XLA Ops:
  0.6 2.5 %collective-permute-start.3 = (bf16[32,512]{1,0:T(8,128)(2,1)}, bf16[32,512]{1,0:T(8,128)(2,1)S(1)}, u32[]{:S(2)}, u32[]{:S(2)}) collective-permute-start(bf16[32,512]{1,0:T(8,128)(2,1)} %bitcast.6), channel_id=1, source_target_pairs={{0,24},{8,16},{16,8},{24,0},{1,25},{9,17},{17,9},{25,1},{2,26},{10... | collective-permute-start | bytes 98312 | tf_op jit(solution)/shard_map/ppermute | solution.py:85
  3.1 0.6 %collective-permute-start.2 = (bf16[32,512]{1,0:T(8,128)(2,1)}, bf16[32,512]{1,0:T(8,128)(2,1)S(1)}, u32[]{:S(2)}, u32[]{:S(2)}) collective-permute-start(bf16[32,512]{1,0:T(8,128)(2,1)} %bitcast.7), channel_id=1, source_target_pairs={{0,16},{8,24},{16,0},{24,8},{1,17},{9,25},{17,1},{25,9},{2,18},{10... | collective-permute-start | bytes 98312 | tf_op jit(solution)/shard_map/ppermute | solution.py:85
  3.7 0.0 collective-permute-start.1
  4.4 0.0 copy-start.2
  4.4 1.6 %band.1 = (bf16[512,1024]{1,0:T(8,128)(2,1)S(1)}, f32[1,128]{1,0:T(1,128)S(1)}, f32[144,128]{1,0:T(8,128)S(1)}) custom-call(s32[1,1]{1,0:T(1,128)S(6)} %copy.13.limit, s32[1,1,128]{2,1,0:T(1,128)} %rows.1, s32[1,1,128]{2,1,0:T(1,128)} %cols.1, s32[256,128]{1,0:T(8,128)} %bitcast.10, bf16[256,128]{1,0:T(8,128)(2,1)} %bitcast.11, f32[1,128]{1,0:T(1,128)} %bitcast.12, ...), custom_call_target="tpu_custom_call" | custom-call | flops 33554432 | bytes 8388608 | tf_op jit(solution)/shard_map/band/pallas_call | solution.py:156
  6.1 0.0 collective-permute-done.3.refs_3_
  6.1 1.2 %collective-permute-done.2.refs_2_ = bf16[32,512]{1,0:T(8,128)(2,1)S(1)} collective-permute-done((bf16[32,512]{1,0:T(8,128)(2,1)}, bf16[32,512]{1,0:T(8,128)(2,1)S(1)}, u32[]{:S(2)}, u32[]{:S(2)}) %collective-permute-start.2) | collective-permute-done | bytes 32800 | tf_op jit(solution)/shard_map/ppermute | solution.py:85
  7.3 0.0 collective-permute-done.1.refs_1_
  7.3 0.0 copy-done.2
  7.3 0.4 %forward.1 = (f32[128,256]{1,0:T(8,128)S(1)}, s16[144,256]{1,0:T(8,128)(2,1)S(1)}, s16[144,256]{1,0:T(8,128)(2,1)S(1)}, s16[144,256]{1,0:T(8,128)(2,1)S(1)}) custom-call(bf16[32,512]{1,0:T(8,128)(2,1)S(1)} %bitcast.9, bf16[32,512]{1,0:T(8,128)(2,1)S(1)} %collective-permute-done.1.refs_1_, bf16[32,512]{1,0:T(8,128)(2,1)S(1)} %collective-permute-done.2.refs_2_, ...), custom_call_target="tpu_custom_call" | custom-call | tf_op jit(solution)/shard_map/forward/pallas_call | solution.py:200
  7.7 2.6 %collective-permute-start.4 = (s16[144,256]{1,0:T(8,128)(2,1)S(1)}, s16[144,256]{1,0:T(8,128)(2,1)S(1)}, u32[]{:S(2)}, u32[]{:S(2)}) collective-permute-start(s16[144,256]{1,0:T(8,128)(2,1)S(1)} %get-tuple-element.28), channel_id=1, source_target_pairs={{0,3},{1,2},{2,1},{3,0},{4,7},{5,6},{6,5},{7,4},{8,11},{9,10},{10,... | collective-permute-start | bytes 221192 | tf_op jit(solution)/shard_map/ppermute | solution.py:85
  10.2 0.5 %collective-permute-start.5 = (s16[144,256]{1,0:T(8,128)(2,1)S(1)}, s16[144,256]{1,0:T(8,128)(2,1)S(1)}, u32[]{:S(2)}, u32[]{:S(2)}) collective-permute-start(s16[144,256]{1,0:T(8,128)(2,1)S(1)} %get-tuple-element.29), channel_id=1, source_target_pairs={{0,2},{1,3},{2,0},{3,1},{4,6},{5,7},{6,4},{7,5},{8,10},{9,11},{10,... | collective-permute-start | bytes 221192 | tf_op jit(solution)/shard_map/ppermute | solution.py:85
  10.7 0.5 %collective-permute-start.6 = (s16[144,256]{1,0:T(8,128)(2,1)S(1)}, s16[144,256]{1,0:T(8,128)(2,1)S(1)}, u32[]{:S(2)}, u32[]{:S(2)}) collective-permute-start(s16[144,256]{1,0:T(8,128)(2,1)S(1)} %get-tuple-element.30), channel_id=1, source_target_pairs={{0,1},{1,0},{2,3},{3,2},{4,5},{5,4},{6,7},{7,6},{8,9},{9,8},{10,11... | collective-permute-start | bytes 221192 | tf_op jit(solution)/shard_map/ppermute | solution.py:85
  11.2 2.6 %collective-permute-start = (f32[144,128]{1,0:T(8,128)S(1)}, f32[144,128]{1,0:T(8,128)S(1)}, u32[]{:S(2)}, u32[]{:S(2)}) collective-permute-start(f32[144,128]{1,0:T(8,128)S(1)} %get-tuple-element.25), channel_id=1, source_target_pairs={{0,4},{1,5},{2,6},{3,7},{4,0},{5,1},{6,2},{7,3},{8,12},{9,13},{10,... | collective-permute-start | bytes 221192 | tf_op jit(solution)/shard_map/ppermute | solution.py:90
  13.8 0.0 collective-permute-done.4.refs_0_
  13.8 1.6 %collective-permute-done.5.refs_1_ = s16[144,256]{1,0:T(8,128)(2,1)S(1)} collective-permute-done((s16[144,256]{1,0:T(8,128)(2,1)S(1)}, s16[144,256]{1,0:T(8,128)(2,1)S(1)}, u32[]{:S(2)}, u32[]{:S(2)}) %collective-permute-start.5) | collective-permute-done | bytes 73760 | tf_op jit(solution)/shard_map/ppermute | solution.py:85
  15.4 0.0 collective-permute-done.6.refs_2_
  15.4 0.0 copy-start
  15.4 0.0 copy-start.1
  15.4 0.1 add.1.refs_2_
  15.5 2.8 %collective-permute-start.7 = (s16[144,256]{1,0:T(8,128)(2,1)S(1)}, s16[144,256]{1,0:T(8,128)(2,1)S(1)}, u32[]{:S(2)}, u32[]{:S(2)}) collective-permute-start(s16[144,256]{1,0:T(8,128)(2,1)S(1)} %add.1.refs_2_), channel_id=1, source_target_pairs={{0,4},{1,5},{2,6},{3,7},{4,0},{5,1},{6,2},{7,3},{8,12},{9,13},{10,... | collective-permute-start | bytes 221192 | tf_op jit(solution)/shard_map/ppermute | solution.py:90
  18.3 0.0 collective-permute-done.refs_1_
  18.3 0.0 copy-done
  18.3 0.0 copy-done.1
  18.3 0.2 before.1
  18.6 3.1 %collective-permute-done.7.refs_0_ = s16[144,256]{1,0:T(8,128)(2,1)S(1)} collective-permute-done((s16[144,256]{1,0:T(8,128)(2,1)S(1)}, s16[144,256]{1,0:T(8,128)(2,1)S(1)}, u32[]{:S(2)}, u32[]{:S(2)}) %collective-permute-start.7) | collective-permute-done | bytes 73760 | tf_op jit(solution)/shard_map/ppermute | solution.py:90
  21.6 0.5 %own_rows.1 = (f32[256,128]{1,0:T(8,128)S(1)}, bf16[384,128]{1,0:T(8,128)(2,1)S(1)}) custom-call(bf16[128,128]{1,0:T(8,128)(2,1)S(1)} %copy-done, f32[1,128]{1,0:T(1,128)S(1)} %get-tuple-element.24.bias, f32[128,256]{1,0:T(8,128)S(1)} %get-tuple-element.31.whole, f32[256,128]{1,0:T(8,128)S(1)} %get-tuple-element.32.first, ...), custom_call_target="tpu_custom_call" | custom-call | tf_op jit(solution)/shard_map/own_rows/pallas_call | solution.py:291
  22.1 0.7 %collective-permute-start.10 = (bf16[384,128]{1,0:T(8,128)(2,1)S(1)}, bf16[384,128]{1,0:T(8,128)(2,1)S(1)}, u32[]{:S(2)}, u32[]{:S(2)}) collective-permute-start(bf16[384,128]{1,0:T(8,128)(2,1)S(1)} %get-tuple-element.35.refs_0_), channel_id=1, source_target_pairs={{0,1},{1,0},{2,3},{3,2},{4,5},{5,4},{6,7},{7,6},{8,9},{9,8},{10,11... | collective-permute-start | bytes 294920 | tf_op jit(solution)/shard_map/ppermute | solution.py:85
  22.8 1.3 %collective-permute-start.9 = (bf16[384,128]{1,0:T(8,128)(2,1)S(1)}, bf16[384,128]{1,0:T(8,128)(2,1)S(1)}, u32[]{:S(2)}, u32[]{:S(2)}) collective-permute-start(bf16[384,128]{1,0:T(8,128)(2,1)S(1)} %get-tuple-element.35.refs_0_), channel_id=1, source_target_pairs={{0,3},{1,2},{2,1},{3,0},{4,7},{5,6},{6,5},{7,4},{8,11},{9,10},{10,... | collective-permute-start | bytes 294920 | tf_op jit(solution)/shard_map/ppermute | solution.py:85
  24.1 1.5 %collective-permute-start.8 = (bf16[384,128]{1,0:T(8,128)(2,1)S(1)}, bf16[384,128]{1,0:T(8,128)(2,1)S(1)}, u32[]{:S(2)}, u32[]{:S(2)}) collective-permute-start(bf16[384,128]{1,0:T(8,128)(2,1)S(1)} %get-tuple-element.35.refs_0_), channel_id=1, source_target_pairs={{0,2},{1,3},{2,0},{3,1},{4,6},{5,7},{6,4},{7,5},{8,10},{9,11},{10,... | collective-permute-start | bytes 294920 | tf_op jit(solution)/shard_map/ppermute | solution.py:85
  25.6 1.3 %collective-permute-done.10.refs_1_.refs_3_ = bf16[384,128]{1,0:T(8,128)(2,1)S(1)} collective-permute-done((bf16[384,128]{1,0:T(8,128)(2,1)S(1)}, bf16[384,128]{1,0:T(8,128)(2,1)S(1)}, u32[]{:S(2)}, u32[]{:S(2)}) %collective-permute-start.10) | collective-permute-done | bytes 98336 | tf_op jit(solution)/shard_map/ppermute | solution.py:85
  26.9 0.4 %early.1.refs_6_ = f32[128,512]{1,0:T(8,128)S(1)} custom-call(bf16[384,128]{1,0:T(8,128)(2,1)S(1)} %get-tuple-element.35.refs_0_, bf16[384,128]{1,0:T(8,128)(2,1)S(1)} %collective-permute-done.10.refs_1_.refs_3_, bf16[128,128]{1,0:T(8,128)(2,1)S(1)} %copy-done, bf16[512,1024]{1,0:T(8,128)(2,1)S(1)} %get-tuple-element.26.refs_4_.refs_3_.refs_5_), custom_call_target="tpu_custom_call" | custom-call | tf_op jit(solution)/shard_map/early/pallas_call | solution.py:383
  27.3 1.0 %collective-permute-done.9.refs_2_ = bf16[384,128]{1,0:T(8,128)(2,1)S(1)} collective-permute-done((bf16[384,128]{1,0:T(8,128)(2,1)S(1)}, bf16[384,128]{1,0:T(8,128)(2,1)S(1)}, u32[]{:S(2)}, u32[]{:S(2)}) %collective-permute-start.9) | collective-permute-done | bytes 98336 | tf_op jit(solution)/shard_map/ppermute | solution.py:85
  28.3 0.9 %collective-permute-done.8.refs_1_ = bf16[384,128]{1,0:T(8,128)(2,1)S(1)} collective-permute-done((bf16[384,128]{1,0:T(8,128)(2,1)S(1)}, bf16[384,128]{1,0:T(8,128)(2,1)S(1)}, u32[]{:S(2)}, u32[]{:S(2)}) %collective-permute-start.8) | collective-permute-done | bytes 98336 | tf_op jit(solution)/shard_map/ppermute | solution.py:85
  29.3 0.4 %backward.1 = (bf16[272,128]{1,0:T(8,128)(2,1)S(1)}, bf16[272,128]{1,0:T(8,128)(2,1)S(1)}, bf16[272,128]{1,0:T(8,128)(2,1)S(1)}, bf16[272,128]{1,0:T(8,128)(2,1)S(1)}, f32[32,512]{1,0:T(8,128)S(1)}) custom-call(bf16[384,128]{1,0:T(8,128)(2,1)S(1)} %get-tuple-element.35.refs_0_, bf16[384,128]{1,0:T(8,128)(2,1)S(1)} %collective-permute-done.8.refs_1_, ...), custom_call_target="tpu_custom_call" | custom-call | tf_op jit(solution)/shard_map/backward/pallas_call | solution.py:393
  29.7 0.1 collective-permute-start.11
  29.8 1.0 %collective-permute-start.12 = (bf16[272,128]{1,0:T(8,128)(2,1)S(1)}, bf16[272,128]{1,0:T(8,128)(2,1)S(1)}, u32[]{:S(2)}, u32[]{:S(2)}) collective-permute-start(bf16[272,128]{1,0:T(8,128)(2,1)S(1)} %get-tuple-element.38), channel_id=1, source_target_pairs={{0,16},{8,24},{16,0},{24,8},{1,17},{9,25},{17,1},{25,9},{2,18},{10... | collective-permute-start | bytes 208904 | tf_op jit(solution)/shard_map/ppermute | solution.py:85
  30.8 0.8 %collective-permute-start.13 = (bf16[272,128]{1,0:T(8,128)(2,1)S(1)}, bf16[272,128]{1,0:T(8,128)(2,1)S(1)}, u32[]{:S(2)}, u32[]{:S(2)}) collective-permute-start(bf16[272,128]{1,0:T(8,128)(2,1)S(1)} %get-tuple-element.39), channel_id=1, source_target_pairs={{0,8},{8,0},{16,24},{24,16},{1,9},{9,1},{17,25},{25,17},{2,10},{10... | collective-permute-start | bytes 208904 | tf_op jit(solution)/shard_map/ppermute | solution.py:85
  31.6 0.6 %activate.1 = f32[128,128]{1,0:T(8,128)} custom-call(f32[256,128]{1,0:T(8,128)S(1)} %get-tuple-element.34.pre), custom_call_target="tpu_custom_call" | custom-call | tf_op jit(solution)/shard_map/activate/pallas_call | solution.py:309
  32.3 1.9 %collective-permute-done.11.refs_1_ = bf16[272,128]{1,0:T(8,128)(2,1)S(1)} collective-permute-done((bf16[272,128]{1,0:T(8,128)(2,1)S(1)}, bf16[272,128]{1,0:T(8,128)(2,1)S(1)}, u32[]{:S(2)}, u32[]{:S(2)}) %collective-permute-start.11) | collective-permute-done | bytes 69664 | tf_op jit(solution)/shard_map/ppermute | solution.py:85
  34.2 0.7 %collective-permute-done.12.refs_2_ = bf16[272,128]{1,0:T(8,128)(2,1)S(1)} collective-permute-done((bf16[272,128]{1,0:T(8,128)(2,1)S(1)}, bf16[272,128]{1,0:T(8,128)(2,1)S(1)}, u32[]{:S(2)}, u32[]{:S(2)}) %collective-permute-start.12) | collective-permute-done | bytes 69664 | tf_op jit(solution)/shard_map/ppermute | solution.py:85
  34.9 0.0 collective-permute-done.13.refs_3_
  34.9 0.7 %final.1 = (bf16[32,512]{1,0:T(8,128)(2,1)}, f32[128,128]{1,0:T(8,128)}, f32[1,128]{1,0:T(1,128)}) custom-call(bf16[272,128]{1,0:T(8,128)(2,1)S(1)} %get-tuple-element.36.refs_0_, bf16[272,128]{1,0:T(8,128)(2,1)S(1)} %collective-permute-done.11.refs_1_, bf16[272,128]{1,0:T(8,128)(2,1)S(1)} %collective-permute-done.12.refs_2_, ...), custom_call_target="tpu_custom_call" | custom-call | tf_op jit(solution)/shard_map/final/pallas_call | solution.py:444
Async XLA Ops:
  0.6 5.4 %collective-permute-start.3 = (bf16[32,512]{1,0:T(8,128)(2,1)}, bf16[32,512]{1,0:T(8,128)(2,1)S(1)}, u32[]{:S(2)}, u32[]{:S(2)}) collective-permute-start(bf16[32,512]{1,0:T(8,128)(2,1)} %bitcast.6), channel_id=1, source_target_pairs={{0,24},{8,16},{16,8},{24,0},{1,25},{9,17},{17,9},{25,1},{2,26},{10... | collective-permute-start | bytes 98312 | tf_op jit(solution)/shard_map/ppermute | solution.py:85
  3.1 4.2 %collective-permute-start.2 = (bf16[32,512]{1,0:T(8,128)(2,1)}, bf16[32,512]{1,0:T(8,128)(2,1)S(1)}, u32[]{:S(2)}, u32[]{:S(2)}) collective-permute-start(bf16[32,512]{1,0:T(8,128)(2,1)} %bitcast.7), channel_id=1, source_target_pairs={{0,16},{8,24},{16,0},{24,8},{1,17},{9,25},{17,1},{25,9},{2,18},{10... | collective-permute-start | bytes 98312 | tf_op jit(solution)/shard_map/ppermute | solution.py:85
  3.7 3.5 %collective-permute-start.1 = (bf16[32,512]{1,0:T(8,128)(2,1)}, bf16[32,512]{1,0:T(8,128)(2,1)S(1)}, u32[]{:S(2)}, u32[]{:S(2)}) collective-permute-start(bf16[32,512]{1,0:T(8,128)(2,1)} %bitcast.8), channel_id=1, source_target_pairs={{0,8},{8,0},{16,24},{24,16},{1,9},{9,1},{17,25},{25,17},{2,10},{10... | collective-permute-start | bytes 98312 | tf_op jit(solution)/shard_map/ppermute | solution.py:85
  4.4 2.9 %copy-start.2 = (bf16[512,32]{0,1:T(8,128)(2,1)S(1)}, bf16[512,32]{0,1:T(8,128)(2,1)}, u32[]{:S(2)}) copy-start(bf16[512,32]{0,1:T(8,128)(2,1)} %param.9) | copy-start | bytes 98308
  7.7 6.1 %collective-permute-start.4 = (s16[144,256]{1,0:T(8,128)(2,1)S(1)}, s16[144,256]{1,0:T(8,128)(2,1)S(1)}, u32[]{:S(2)}, u32[]{:S(2)}) collective-permute-start(s16[144,256]{1,0:T(8,128)(2,1)S(1)} %get-tuple-element.28), channel_id=1, source_target_pairs={{0,3},{1,2},{2,1},{3,0},{4,7},{5,6},{6,5},{7,4},{8,11},{9,10},{10,... | collective-permute-start | bytes 221192 | tf_op jit(solution)/shard_map/ppermute | solution.py:85
  10.2 5.2 %collective-permute-start.5 = (s16[144,256]{1,0:T(8,128)(2,1)S(1)}, s16[144,256]{1,0:T(8,128)(2,1)S(1)}, u32[]{:S(2)}, u32[]{:S(2)}) collective-permute-start(s16[144,256]{1,0:T(8,128)(2,1)S(1)} %get-tuple-element.29), channel_id=1, source_target_pairs={{0,2},{1,3},{2,0},{3,1},{4,6},{5,7},{6,4},{7,5},{8,10},{9,11},{10,... | collective-permute-start | bytes 221192 | tf_op jit(solution)/shard_map/ppermute | solution.py:85
  10.7 4.7 %collective-permute-start.6 = (s16[144,256]{1,0:T(8,128)(2,1)S(1)}, s16[144,256]{1,0:T(8,128)(2,1)S(1)}, u32[]{:S(2)}, u32[]{:S(2)}) collective-permute-start(s16[144,256]{1,0:T(8,128)(2,1)S(1)} %get-tuple-element.30), channel_id=1, source_target_pairs={{0,1},{1,0},{2,3},{3,2},{4,5},{5,4},{6,7},{7,6},{8,9},{9,8},{10,11... | collective-permute-start | bytes 221192 | tf_op jit(solution)/shard_map/ppermute | solution.py:85
  11.2 7.1 %collective-permute-start = (f32[144,128]{1,0:T(8,128)S(1)}, f32[144,128]{1,0:T(8,128)S(1)}, u32[]{:S(2)}, u32[]{:S(2)}) collective-permute-start(f32[144,128]{1,0:T(8,128)S(1)} %get-tuple-element.25), channel_id=1, source_target_pairs={{0,4},{1,5},{2,6},{3,7},{4,0},{5,1},{6,2},{7,3},{8,12},{9,13},{10,... | collective-permute-start | bytes 221192 | tf_op jit(solution)/shard_map/ppermute | solution.py:90
  15.4 2.9 %copy-start = (bf16[128,128]{1,0:T(8,128)(2,1)S(1)}, bf16[128,128]{1,0:T(8,128)(2,1)}, u32[]{:S(2)}) copy-start(bf16[128,128]{1,0:T(8,128)(2,1)} %refs_4_.1) | copy-start | bytes 98308
  15.4 2.9 %copy-start.1 = (f32[128,128]{1,0:T(8,128)S(1)}, f32[128,128]{1,0:T(8,128)}, u32[]{:S(2)}) copy-start(f32[128,128]{1,0:T(8,128)} %refs_0_.1) | copy-start | bytes 196612
  15.5 6.1 %collective-permute-start.7 = (s16[144,256]{1,0:T(8,128)(2,1)S(1)}, s16[144,256]{1,0:T(8,128)(2,1)S(1)}, u32[]{:S(2)}, u32[]{:S(2)}) collective-permute-start(s16[144,256]{1,0:T(8,128)(2,1)S(1)} %add.1.refs_2_), channel_id=1, source_target_pairs={{0,4},{1,5},{2,6},{3,7},{4,0},{5,1},{6,2},{7,3},{8,12},{9,13},{10,... | collective-permute-start | bytes 221192 | tf_op jit(solution)/shard_map/ppermute | solution.py:90
  22.1 4.8 %collective-permute-start.10 = (bf16[384,128]{1,0:T(8,128)(2,1)S(1)}, bf16[384,128]{1,0:T(8,128)(2,1)S(1)}, u32[]{:S(2)}, u32[]{:S(2)}) collective-permute-start(bf16[384,128]{1,0:T(8,128)(2,1)S(1)} %get-tuple-element.35.refs_0_), channel_id=1, source_target_pairs={{0,1},{1,0},{2,3},{3,2},{4,5},{5,4},{6,7},{7,6},{8,9},{9,8},{10,11... | collective-permute-start | bytes 294920 | tf_op jit(solution)/shard_map/ppermute | solution.py:85
  22.8 5.5 %collective-permute-start.9 = (bf16[384,128]{1,0:T(8,128)(2,1)S(1)}, bf16[384,128]{1,0:T(8,128)(2,1)S(1)}, u32[]{:S(2)}, u32[]{:S(2)}) collective-permute-start(bf16[384,128]{1,0:T(8,128)(2,1)S(1)} %get-tuple-element.35.refs_0_), channel_id=1, source_target_pairs={{0,3},{1,2},{2,1},{3,0},{4,7},{5,6},{6,5},{7,4},{8,11},{9,10},{10,... | collective-permute-start | bytes 294920 | tf_op jit(solution)/shard_map/ppermute | solution.py:85
  24.1 5.1 %collective-permute-start.8 = (bf16[384,128]{1,0:T(8,128)(2,1)S(1)}, bf16[384,128]{1,0:T(8,128)(2,1)S(1)}, u32[]{:S(2)}, u32[]{:S(2)}) collective-permute-start(bf16[384,128]{1,0:T(8,128)(2,1)S(1)} %get-tuple-element.35.refs_0_), channel_id=1, source_target_pairs={{0,2},{1,3},{2,0},{3,1},{4,6},{5,7},{6,4},{7,5},{8,10},{9,11},{10,... | collective-permute-start | bytes 294920 | tf_op jit(solution)/shard_map/ppermute | solution.py:85
  29.7 4.5 %collective-permute-start.11 = (bf16[272,128]{1,0:T(8,128)(2,1)S(1)}, bf16[272,128]{1,0:T(8,128)(2,1)S(1)}, u32[]{:S(2)}, u32[]{:S(2)}) collective-permute-start(bf16[272,128]{1,0:T(8,128)(2,1)S(1)} %get-tuple-element.37), channel_id=1, source_target_pairs={{0,24},{8,16},{16,8},{24,0},{1,25},{9,17},{17,9},{25,1},{2,26},{10... | collective-permute-start | bytes 208904 | tf_op jit(solution)/shard_map/ppermute | solution.py:85
  29.8 5.1 %collective-permute-start.12 = (bf16[272,128]{1,0:T(8,128)(2,1)S(1)}, bf16[272,128]{1,0:T(8,128)(2,1)S(1)}, u32[]{:S(2)}, u32[]{:S(2)}) collective-permute-start(bf16[272,128]{1,0:T(8,128)(2,1)S(1)} %get-tuple-element.38), channel_id=1, source_target_pairs={{0,16},{8,24},{16,0},{24,8},{1,17},{9,25},{17,1},{25,9},{2,18},{10... | collective-permute-start | bytes 208904 | tf_op jit(solution)/shard_map/ppermute | solution.py:85
  30.8 4.0 %collective-permute-start.13 = (bf16[272,128]{1,0:T(8,128)(2,1)S(1)}, bf16[272,128]{1,0:T(8,128)(2,1)S(1)}, u32[]{:S(2)}, u32[]{:S(2)}) collective-permute-start(bf16[272,128]{1,0:T(8,128)(2,1)S(1)} %get-tuple-element.39), channel_id=1, source_target_pairs={{0,8},{8,0},{16,24},{24,16},{1,9},{9,1},{17,25},{25,17},{2,10},{10... | collective-permute-start | bytes 208904 | tf_op jit(solution)/shard_map/ppermute | solution.py:85
